TPU v7x, 32 devices: a whole 2x2x4 slice. The times are simulated.
32 devices in a mesh: dp: 8 (over z, y), expert: 4 (over x, core).
Axes of the slice: x: 2, y: 2, z: 4, core: 2. Of those that a mesh axis runs over, the one named last changes fastest.
Arguments:
- features: bfloat16 [16384, 80], P(('dp', 'expert')), may hold values from -6 to 6
- lengths: int32 [32, 4], P(('dp', 'expert')), may hold values from 0 to 512, as said below
- routes: int32 [2, 16384, 1], P(None, ('dp', 'expert')), may hold values from 0 to 3; in each aligned block of 512 rows (0 to 511, 512 to 1023, ..., all dimensions but the last counted through in order) at most 160 rows name the same one
- alignment: int32 [16384], P(('dp', 'expert')), may hold values from 0 to 8191
- attend_copy: bfloat16 [512, 1536], P('dp'), may hold values from -0.25 to 0.25
- output_copy: bfloat16 [512, 512], P('dp'), may hold values from -2 to 2
- conv_copy: bfloat16 [512, 1536], P('dp'), may hold values from -0.25 to 0.25
- head_copy: bfloat16 [512, 8192], P('dp'), may hold values from -0.5 to 0.5
- extra_copy: bfloat16 [512, 103], P('dp'), may hold values from -4 to 4
- gains_copy: bfloat16 [5, 512], P(None, 'dp'), may hold values from 0.3 to 2.5
- up_copy: bfloat16 [2, 4, 512, 2048], P(None, 'expert', 'dp'), may hold values from -0.25 to 0.25
- down_copy: bfloat16 [2, 4, 2048, 512], P(None, 'expert', None, 'dp'), may hold values from -1.5 to 1.5
- attend_master: float32 [512, 1536], P('dp'), may hold values from -0.25 to 0.25
- output_master: float32 [512, 512], P('dp'), may hold values from -2 to 2
- conv_master: float32 [512, 1536], P('dp'), may hold values from -0.25 to 0.25
- head_master: float32 [512, 8192], P('dp'), may hold values from -0.5 to 0.5
- extra_master: float32 [512, 103], P('dp'), may hold values from -0.625 to 0.625
- gains_master: float32 [5, 512], P(None, 'dp'), may hold values from 0.5 to 1.5
- up_master: float32 [2, 4, 512, 2048], P(None, 'expert', 'dp'), may hold values from -0.25 to 0.25
- down_master: float32 [2, 4, 2048, 512], P(None, 'expert', None, 'dp'), may hold values from -1.5 to 1.5
- attend_first: float32 [512, 1536], P('dp'), may hold values from -2.2888184e-05 to 2.2888184e-05
- output_first: float32 [512, 512], P('dp'), may hold values from -2.2888184e-05 to 2.2888184e-05
- conv_first: float32 [512, 1536], P('dp'), may hold values from -2.2888184e-05 to 2.2888184e-05
- head_first: float32 [512, 8192], P('dp'), may hold values from -2.2888184e-05 to 2.2888184e-05
- extra_first: float32 [512, 103], P('dp'), may hold values from -2.2888184e-05 to 2.2888184e-05
- gains_first: float32 [5, 512], P(None, 'dp'), may hold values from -9.1552734e-05 to 9.1552734e-05
- up_first: float32 [2, 4, 512, 2048], P(None, 'expert', 'dp'), may hold values from -2.2888184e-05 to 2.2888184e-05
- down_first: float32 [2, 4, 2048, 512], P(None, 'expert', None, 'dp'), may hold values from -5.722046e-06 to 5.722046e-06
- attend_second: float32 [512, 1536], P('dp'), may hold values from 6.8345377e-12 to 1.093526e-10
- output_second: float32 [512, 512], P('dp'), may hold values from 6.8345377e-12 to 1.093526e-10
- conv_second: float32 [512, 1536], P('dp'), may hold values from 6.8345377e-12 to 1.093526e-10
- head_second: float32 [512, 8192], P('dp'), may hold values from 6.8345377e-12 to 1.093526e-10
- extra_second: float32 [512, 103], P('dp'), may hold values from 6.8345377e-12 to 1.093526e-10
- gains_second: float32 [5, 512], P(None, 'dp'), may hold values from 1.093526e-10 to 1.7496417e-09
- up_second: float32 [2, 4, 512, 2048], P(None, 'expert', 'dp'), may hold values from 6.8345377e-12 to 1.093526e-10
- down_second: float32 [2, 4, 2048, 512], P(None, 'expert', None, 'dp'), may hold values from 4.271586e-13 to 6.8345377e-12
Outputs:
- loss_sum: float32 [], replicated
- frame_count: float32 [], replicated
- grad_norm: float32 [], replicated
- attend_moment: float32 [512, 1536], P('dp')
- output_moment: float32 [512, 512], P('dp')
- conv_moment: float32 [512, 1536], P('dp')
- head_moment: float32 [512, 8192], P('dp')
- extra_moment: float32 [512, 103], P('dp')
- gains_moment: float32 [5, 512], P(None, 'dp')
- up_moment: float32 [2, 4, 512, 2048], P(None, 'expert', 'dp')
- down_moment: float32 [2, 4, 2048, 512], P(None, 'expert', None, 'dp')
- attend_square: float32 [512, 1536], P('dp')
- output_square: float32 [512, 512], P('dp')
- conv_square: float32 [512, 1536], P('dp')
- head_square: float32 [512, 8192], P('dp')
- extra_square: float32 [512, 103], P('dp')
- gains_square: float32 [5, 512], P(None, 'dp')
- up_square: float32 [2, 4, 512, 2048], P(None, 'expert', 'dp')
- down_square: float32 [2, 4, 2048, 512], P(None, 'expert', None, 'dp')
- attend_new: float32 [512, 1536], P('dp')
- output_new: float32 [512, 512], P('dp')
- conv_new: float32 [512, 1536], P('dp')
- head_new: float32 [512, 8192], P('dp')
- extra_new: float32 [512, 103], P('dp')
- gains_new: float32 [5, 512], P(None, 'dp')
- up_new: float32 [2, 4, 512, 2048], P(None, 'expert', 'dp')
- down_new: float32 [2, 4, 2048, 512], P(None, 'expert', None, 'dp')
Inputs may be any that keep to these rules, and one draw needn't show every extreme that they name: `lengths`: each row has 3 utterances of one frame or more followed by padding of zero frames or more; a row sums to 512. `routes`: among the frames of one row, no expert of one feed-forward is named by more than 160 frames, and 160 is reached.
All inputs are finite; a program needn't handle non-finite values.
Results may differ from a plain program's by a relative error of at most 0.03.
Values may be sent and summed in bfloat16 or wider, within the bound.
No kernel may reach another device: no remote copies, remote signals or barrier semaphores. Data moves between devices by JAX's collectives and lax.ppermute only.
A program may use at most 256 MiB of HBM per device.

v0:
```python
import math

import jax
import jax.numpy as jnp
from jax import lax
from jax.sharding import PartitionSpec as P

HEADS = 8
STEP = 5


NORM_EPS = 1e-05
ADAM_EPS = 1e-08
BETA_ONE = 0.5
BETA_TWO = 0.5
MASKED = -1000000000.0
STEP_RATES = (0.02, 0.2, 0.02, 0.05, 0.05, 0.5, 0.02, 0.1)
DECAYS = (0.01, 0.01, 0.01, 0.01, 0.01, 0.0, 0.01, 0.01)


def matmul(left_side, right_side):
    return jnp.dot(left_side, right_side, preferred_element_type=jnp.float32)


def inner_last(left_side, right_side):
    return lax.dot_general(
        left_side, right_side, (((1,), (1,)), ((), ())), preferred_element_type=jnp.float32
    )


def outer_first(left_side, right_side):
    return lax.dot_general(
        left_side, right_side, (((0,), (0,)), ((), ())), preferred_element_type=jnp.float32
    )


def layer_norm(values, gain_row):
    centred = values - jnp.mean(values, axis=-1, keepdims=True)
    spread = jnp.mean(centred * centred, axis=-1, keepdims=True)
    return centred * lax.rsqrt(spread + NORM_EPS) * gain_row


def segment_ids(lengths, row_count):
    bounds = jnp.cumsum(lengths[:, :-1], axis=1)
    places = jnp.arange(row_count, dtype=jnp.int32)
    segment = jnp.sum((places[None, :, None] >= bounds[:, None, :]).astype(jnp.int32), axis=-1)
    counted = (places[None, :] < bounds[:, -1:]).astype(jnp.float32)
    return (segment[0], counted[0])


def to_experts(slots):
    return lax.all_to_all(slots, "expert", split_axis=0, concat_axis=1, tiled=True)


def from_experts(slots):
    return lax.all_to_all(slots, "expert", split_axis=1, concat_axis=0, tiled=True)


def mixture_forward(hidden, route_ids, router, up_block, down_block, gain_row, capacity):
    row_count, model_width = hidden.shape
    experts = router.shape[1]
    normed, norm_back = jax.vjp(layer_norm, hidden, gain_row)
    normed_low = normed.astype(jnp.bfloat16)
    router_prob = jax.nn.softmax(matmul(normed_low, router), axis=-1)
    chosen_mask = route_ids[:, None] == jnp.arange(experts, dtype=jnp.int32)[None, :]
    gate_prob = jnp.sum(jnp.where(chosen_mask, router_prob, 0.0), axis=-1)
    counts = chosen_mask.astype(jnp.int32)
    slot_rank = jnp.sum((jnp.cumsum(counts, axis=0) - counts) * counts, axis=-1)
    slot_index = route_ids * capacity + slot_rank
    source = (
        jnp.full((experts * capacity,), row_count, jnp.int32)
        .at[slot_index]
        .set(jnp.arange(row_count, dtype=jnp.int32))
    )
    padded = jnp.concatenate([normed_low, jnp.zeros((1, model_width), jnp.bfloat16)], axis=0)
    received = to_experts(padded[source].reshape(experts, capacity, model_width))
    hidden_units = jnp.einsum(
        "end,edf->enf", received, up_block, preferred_element_type=jnp.float32
    )
    activated, silu_back = jax.vjp(jax.nn.silu, hidden_units)
    activated_low = activated.astype(jnp.bfloat16)
    expert_out = jnp.einsum(
        "enf,efd->end", activated_low, down_block, preferred_element_type=jnp.float32
    ).astype(jnp.bfloat16)
    returned = from_experts(expert_out).reshape(experts * capacity, model_width)
    chosen_rows = returned[slot_index].astype(jnp.float32)
    stored = (
        norm_back,
        normed_low,
        router_prob,
        chosen_mask,
        gate_prob,
        slot_index,
        source,
        received,
        silu_back,
        activated_low,
        chosen_rows,
    )
    return (gate_prob[:, None] * chosen_rows, stored)


def mixture_backward(upstream, stored, router, up_block, down_block):
    (
        norm_back,
        normed_low,
        router_prob,
        chosen_mask,
        gate_prob,
        slot_index,
        source,
        received,
        silu_back,
        activated_low,
        chosen_rows,
    ) = stored
    row_count, model_width = upstream.shape
    experts = router.shape[1]
    capacity = source.shape[0] // experts
    chosen_grad = (gate_prob[:, None] * upstream).astype(jnp.bfloat16)
    gate_grad = jnp.sum(upstream * chosen_rows, axis=-1)
    logit_grad = (
        router_prob
        * (jnp.where(chosen_mask, gate_grad[:, None], 0.0) - (gate_prob * gate_grad)[:, None])
    ).astype(jnp.bfloat16)
    padded = jnp.concatenate([chosen_grad, jnp.zeros((1, model_width), jnp.bfloat16)], axis=0)
    out_grad = to_experts(padded[source].reshape(experts, capacity, model_width))
    activated_grad = jnp.einsum(
        "end,efd->enf", out_grad, down_block, preferred_element_type=jnp.float32
    )
    down_grad = jnp.einsum(
        "enf,end->efd", activated_low, out_grad, preferred_element_type=jnp.float32
    )
    hidden_grad = silu_back(activated_grad)[0].astype(jnp.bfloat16)
    up_grad = jnp.einsum("end,enf->edf", received, hidden_grad, preferred_element_type=jnp.float32)
    slot_grad = jnp.einsum(
        "enf,edf->end", hidden_grad, up_block, preferred_element_type=jnp.float32
    ).astype(jnp.bfloat16)
    returned = from_experts(slot_grad).reshape(experts * capacity, model_width)
    normed_grad = returned[slot_index].astype(jnp.float32) + inner_last(logit_grad, router)
    router_grad = outer_first(normed_low, logit_grad)
    input_grad, gain_grad = norm_back(normed_grad)
    return (input_grad, gain_grad, router_grad, up_grad, down_grad)


def attention_scores(hidden, segment, attend, gain_row):
    row_count, model_width = hidden.shape
    normed, norm_back = jax.vjp(layer_norm, hidden, gain_row)
    normed_low = normed.astype(jnp.bfloat16)
    packed = matmul(normed_low, attend).astype(jnp.bfloat16)
    head_shape = (row_count, HEADS, model_width // HEADS)
    queries = packed[:, :model_width].reshape(head_shape)
    key_rows = packed[:, model_width : 2 * model_width].reshape(head_shape)
    values = packed[:, 2 * model_width :].reshape(head_shape)
    score_scale = (model_width // HEADS) ** (-0.5)
    scores = (
        jnp.einsum("qhd,khd->hqk", queries, key_rows, preferred_element_type=jnp.float32)
        * score_scale
    )
    same_segment = segment[:, None] == segment[None, :]
    scores = jnp.where(same_segment[None], scores, MASKED)
    return (norm_back, normed_low, queries, key_rows, values, scores)


def attention_forward(hidden, segment, attend, output, gain_row):
    parts_kept = attention_scores(hidden, segment, attend, gain_row)
    scores = parts_kept[5]
    maximum = jnp.max(scores, axis=-1, keepdims=True)
    exponent = jnp.exp(scores - maximum)
    totals = jnp.sum(exponent, axis=-1, keepdims=True)
    weights = (exponent / totals).astype(jnp.bfloat16)
    blended = jnp.einsum(
        "hqk,khd->qhd", weights, parts_kept[4], preferred_element_type=jnp.float32
    ).astype(jnp.bfloat16)
    return (matmul(blended.reshape(hidden.shape), output), maximum + jnp.log(totals))


def attention_backward(upstream, hidden, segment, attend, output, gain_row, log_total):
    row_count, model_width = hidden.shape
    norm_back, normed_low, queries, key_rows, values, scores = attention_scores(
        hidden, segment, attend, gain_row
    )
    probs = jnp.exp(scores - log_total)
    weights = probs.astype(jnp.bfloat16)
    blended = jnp.einsum(
        "hqk,khd->qhd", weights, values, preferred_element_type=jnp.float32
    ).astype(jnp.bfloat16)
    upstream_low = upstream.astype(jnp.bfloat16)
    output_grad = outer_first(blended.reshape(row_count, model_width), upstream_low)
    blended_grad = inner_last(upstream_low, output).astype(jnp.bfloat16).reshape(blended.shape)
    value_grad = jnp.einsum(
        "hqk,qhd->khd", weights, blended_grad, preferred_element_type=jnp.float32
    ).astype(jnp.bfloat16)
    prob_grad = jnp.einsum("qhd,khd->hqk", blended_grad, values, preferred_element_type=jnp.float32)
    centre = jnp.sum(probs * prob_grad, axis=-1, keepdims=True)
    score_grad = (probs * (prob_grad - centre)).astype(jnp.bfloat16)
    score_scale = (model_width // HEADS) ** (-0.5)
    query_grad = (
        jnp.einsum("hqk,khd->qhd", score_grad, key_rows, preferred_element_type=jnp.float32)
        * score_scale
    ).astype(jnp.bfloat16)
    key_grad = (
        jnp.einsum("hqk,qhd->khd", score_grad, queries, preferred_element_type=jnp.float32)
        * score_scale
    ).astype(jnp.bfloat16)
    packed_grad = jnp.concatenate(
        [
            query_grad.reshape(row_count, model_width),
            key_grad.reshape(row_count, model_width),
            value_grad.reshape(row_count, model_width),
        ],
        axis=1,
    )
    attend_grad = outer_first(normed_low, packed_grad)
    input_grad, gain_grad = norm_back(inner_last(packed_grad, attend))
    return (input_grad, gain_grad, attend_grad, output_grad)


def depthwise(gated_half, depth_kernel, segment):
    row_count = gated_half.shape[0]
    half_span = depth_kernel.shape[1] // 2
    padded = jnp.pad(gated_half, ((half_span, half_span), (0, 0)))
    padded_ids = jnp.pad(segment, (half_span, half_span), constant_values=-1)
    totals = jnp.zeros_like(gated_half)
    for offset in range(depth_kernel.shape[1]):
        same_segment = (padded_ids[offset : offset + row_count] == segment)[:, None]
        totals = (
            totals
            + jnp.where(same_segment, padded[offset : offset + row_count], 0.0)
            * depth_kernel[:, offset]
        )
    return totals


def conv_inner(projected, depth_kernel, segment):
    model_width = projected.shape[1] // 2
    gated_half = projected[:, :model_width] * jax.nn.sigmoid(projected[:, model_width:])
    return jax.nn.silu(depthwise(gated_half, depth_kernel, segment))


def conv_parts(hidden, segment, conv_weight, depth_kernel, gain_row):
    model_width = hidden.shape[1]
    normed, norm_back = jax.vjp(layer_norm, hidden, gain_row)
    normed_low = normed.astype(jnp.bfloat16)
    projected = matmul(normed_low, conv_weight[:, : 2 * model_width])
    blended, inner_back = jax.vjp(
        lambda values, kernel: conv_inner(values, kernel, segment), projected, depth_kernel
    )
    return (norm_back, normed_low, blended.astype(jnp.bfloat16), inner_back)


def conv_forward(hidden, segment, conv_weight, depth_kernel, gain_row):
    model_width = hidden.shape[1]
    parts_kept = conv_parts(hidden, segment, conv_weight, depth_kernel, gain_row)
    return matmul(parts_kept[2], conv_weight[:, 2 * model_width :])


def conv_backward(upstream, hidden, segment, conv_weight, depth_kernel, gain_row):
    model_width = hidden.shape[1]
    norm_back, normed_low, blended_low, inner_back = conv_parts(
        hidden, segment, conv_weight, depth_kernel, gain_row
    )
    upstream_low = upstream.astype(jnp.bfloat16)
    second_grad = outer_first(blended_low, upstream_low)
    blended_grad = inner_last(upstream_low, conv_weight[:, 2 * model_width :])
    projected_grad, depth_grad = inner_back(blended_grad)
    projected_low = projected_grad.astype(jnp.bfloat16)
    first_grad = outer_first(normed_low, projected_low)
    input_grad, gain_grad = norm_back(inner_last(projected_low, conv_weight[:, : 2 * model_width]))
    return (input_grad, gain_grad, jnp.concatenate([first_grad, second_grad], axis=1), depth_grad)


def adamw(gradient, master, moment, square, rate, decay):
    moment = BETA_ONE * moment + (1.0 - BETA_ONE) * gradient
    square = BETA_TWO * square + (1.0 - BETA_TWO) * gradient * gradient
    update = (
        moment / (1.0 - BETA_ONE**STEP) / (jnp.sqrt(square / (1.0 - BETA_TWO**STEP)) + ADAM_EPS)
    )
    return (moment, square, master - rate * (update + decay * master))


def on_device(
    features,
    lengths,
    routes,
    alignment,
    attend_copy,
    output_copy,
    conv_copy,
    head_copy,
    extra_copy,
    gains_copy,
    up_copy,
    down_copy,
    attend_master,
    output_master,
    conv_master,
    head_master,
    extra_master,
    gains_master,
    up_master,
    down_master,
    attend_first,
    output_first,
    conv_first,
    head_first,
    extra_first,
    gains_first,
    up_first,
    down_first,
    attend_second,
    output_second,
    conv_second,
    head_second,
    extra_second,
    gains_second,
    up_second,
    down_second,
):
    attend, output, conv_weight, head_weight, extra, gains, up_weight, down_weight = (
        lax.all_gather(attend_copy, "dp", axis=0, tiled=True),
        lax.all_gather(output_copy, "dp", axis=0, tiled=True),
        lax.all_gather(conv_copy, "dp", axis=0, tiled=True),
        lax.all_gather(head_copy, "dp", axis=0, tiled=True),
        lax.all_gather(extra_copy, "dp", axis=0, tiled=True),
        lax.all_gather(gains_copy, "dp", axis=1, tiled=True),
        lax.all_gather(up_copy, "dp", axis=2, tiled=True),
        lax.all_gather(down_copy, "dp", axis=3, tiled=True),
    )
    row_count, feat_count = features.shape
    model_width = attend.shape[0]
    experts = up_weight.shape[1] * lax.axis_size("expert")
    capacity = row_count * 5 // (4 * experts)
    segment, counted = segment_ids(lengths, row_count)
    gain_rows = gains.astype(jnp.float32)
    router = extra[:, : 2 * experts]
    embedding = extra[:, 2 * experts : 2 * experts + feat_count]
    depth_kernel = extra[:, 2 * experts + feat_count :].astype(jnp.float32)
    embedded = inner_last(features, embedding)
    moe_one, stored_one = mixture_forward(
        embedded,
        routes[0, :, 0],
        router[:, :experts],
        up_weight[0],
        down_weight[0],
        gain_rows[0],
        capacity,
    )
    after_one = embedded + 0.5 * moe_one
    attended, log_total = attention_forward(after_one, segment, attend, output, gain_rows[1])
    after_attend = after_one + attended
    after_conv = after_attend + conv_forward(
        after_attend, segment, conv_weight, depth_kernel, gain_rows[2]
    )
    moe_two, stored_two = mixture_forward(
        after_conv,
        routes[1, :, 0],
        router[:, experts:],
        up_weight[1],
        down_weight[1],
        gain_rows[3],
        capacity,
    )
    after_two = after_conv + 0.5 * moe_two
    normed, norm_back = jax.vjp(layer_norm, after_two, gain_rows[4])
    normed_low = normed.astype(jnp.bfloat16)
    logits = matmul(normed_low, head_weight)
    maximum = jnp.max(logits, axis=-1, keepdims=True)
    log_head = maximum + jnp.log(jnp.sum(jnp.exp(logits - maximum), axis=-1, keepdims=True))
    picked = jnp.take_along_axis(logits, alignment[:, None], axis=1)[:, 0]
    loss_part = jnp.sum((log_head[:, 0] - picked) * counted)
    loss_sum, frame_count = lax.psum((loss_part, jnp.sum(counted)), ("dp", "expert"))
    probs = jnp.exp(logits - log_head)
    target = (alignment[:, None] == jnp.arange(logits.shape[1], dtype=jnp.int32)[None, :]).astype(
        jnp.float32
    )
    logit_grad = ((probs - target) * (counted / frame_count)[:, None]).astype(jnp.bfloat16)
    head_grad = outer_first(normed_low, logit_grad)
    two_grad, gain_five = norm_back(inner_last(logit_grad, head_weight))
    back_two = mixture_backward(
        0.5 * two_grad, stored_two, router[:, experts:], up_weight[1], down_weight[1]
    )
    conv_grad_in = two_grad + back_two[0]
    back_conv = conv_backward(
        conv_grad_in, after_attend, segment, conv_weight, depth_kernel, gain_rows[2]
    )
    attend_grad_in = conv_grad_in + back_conv[0]
    back_attend = attention_backward(
        attend_grad_in, after_one, segment, attend, output, gain_rows[1], log_total
    )
    one_grad = attend_grad_in + back_attend[0]
    back_one = mixture_backward(
        0.5 * one_grad, stored_one, router[:, :experts], up_weight[0], down_weight[0]
    )
    embedded_grad = (one_grad + back_one[0]).astype(jnp.bfloat16)
    embedding_grad = outer_first(embedded_grad, features)
    extra_grad = jnp.concatenate([back_one[2], back_two[2], embedding_grad, back_conv[3]], axis=1)
    gains_grad = jnp.stack([back_one[1], back_attend[1], back_conv[1], back_two[1], gain_five])
    attend_sum, output_sum, conv_sum, head_sum, extra_sum, gains_sum, up_sum, down_sum = (
        lax.psum_scatter(
            back_attend[2].astype(jnp.bfloat16), "dp", scatter_dimension=0, tiled=True
        ).astype(jnp.float32),
        lax.psum_scatter(
            back_attend[3].astype(jnp.bfloat16), "dp", scatter_dimension=0, tiled=True
        ).astype(jnp.float32),
        lax.psum_scatter(
            back_conv[2].astype(jnp.bfloat16), "dp", scatter_dimension=0, tiled=True
        ).astype(jnp.float32),
        lax.psum_scatter(
            head_grad.astype(jnp.bfloat16), "dp", scatter_dimension=0, tiled=True
        ).astype(jnp.float32),
        lax.psum_scatter(
            extra_grad.astype(jnp.bfloat16), "dp", scatter_dimension=0, tiled=True
        ).astype(jnp.float32),
        lax.psum_scatter(
            gains_grad.astype(jnp.bfloat16), "dp", scatter_dimension=1, tiled=True
        ).astype(jnp.float32),
        lax.psum_scatter(
            jnp.stack([back_one[3], back_two[3]]).astype(jnp.bfloat16),
            "dp",
            scatter_dimension=2,
            tiled=True,
        ).astype(jnp.float32),
        lax.psum_scatter(
            jnp.stack([back_one[4], back_two[4]]).astype(jnp.bfloat16),
            "dp",
            scatter_dimension=3,
            tiled=True,
        ).astype(jnp.float32),
    )
    attend_sum, output_sum, conv_sum, head_sum, extra_sum, gains_sum = (
        lax.psum(attend_sum.astype(jnp.bfloat16), "expert").astype(jnp.float32),
        lax.psum(output_sum.astype(jnp.bfloat16), "expert").astype(jnp.float32),
        lax.psum(conv_sum.astype(jnp.bfloat16), "expert").astype(jnp.float32),
        lax.psum(head_sum.astype(jnp.bfloat16), "expert").astype(jnp.float32),
        lax.psum(extra_sum.astype(jnp.bfloat16), "expert").astype(jnp.float32),
        lax.psum(gains_sum.astype(jnp.bfloat16), "expert").astype(jnp.float32),
    )
    shared_squares = jnp.float32(0.0)
    for member in (attend_sum, output_sum, conv_sum, head_sum, extra_sum, gains_sum):
        shared_squares = shared_squares + jnp.sum(member * member)
    expert_squares = jnp.sum(up_sum * up_sum) + jnp.sum(down_sum * down_sum)
    local_squares = jnp.where(lax.axis_index("expert") == 0, shared_squares, 0.0) + expert_squares
    global_norm = jnp.sqrt(lax.psum(local_squares, ("dp", "expert")))
    frames_all = row_count * lax.axis_size("dp") * lax.axis_size("expert")
    factor = jnp.minimum(1.0, 0.1 * math.sqrt(model_width / frames_all) / global_norm)
    gradients = (attend_sum, output_sum, conv_sum, head_sum, extra_sum, gains_sum, up_sum, down_sum)
    masters = (
        attend_master,
        output_master,
        conv_master,
        head_master,
        extra_master,
        gains_master,
        up_master,
        down_master,
    )
    moments = (
        attend_first,
        output_first,
        conv_first,
        head_first,
        extra_first,
        gains_first,
        up_first,
        down_first,
    )
    squares = (
        attend_second,
        output_second,
        conv_second,
        head_second,
        extra_second,
        gains_second,
        up_second,
        down_second,
    )
    results = [
        adamw(gradient * factor, master, moment, square, rate, decay)
        for gradient, master, moment, square, rate, decay in zip(
            gradients, masters, moments, squares, STEP_RATES, DECAYS
        )
    ]
    return (
        loss_sum,
        frame_count,
        global_norm,
        results[0][0],
        results[1][0],
        results[2][0],
        results[3][0],
        results[4][0],
        results[5][0],
        results[6][0],
        results[7][0],
        results[0][1],
        results[1][1],
        results[2][1],
        results[3][1],
        results[4][1],
        results[5][1],
        results[6][1],
        results[7][1],
        results[0][2],
        results[1][2],
        results[2][2],
        results[3][2],
        results[4][2],
        results[5][2],
        results[6][2],
        results[7][2],
    )


def solution(mesh):
    return jax.shard_map(
        on_device,
        mesh=mesh,
        in_specs=(
            P(("dp", "expert"), None),
            P(("dp", "expert"), None),
            P(None, ("dp", "expert"), None),
            P(("dp", "expert")),
            P("dp", None),
            P("dp", None),
            P("dp", None),
            P("dp", None),
            P("dp", None),
            P(None, "dp"),
            P(None, "expert", "dp", None),
            P(None, "expert", None, "dp"),
            P("dp", None),
            P("dp", None),
            P("dp", None),
            P("dp", None),
            P("dp", None),
            P(None, "dp"),
            P(None, "expert", "dp", None),
            P(None, "expert", None, "dp"),
            P("dp", None),
            P("dp", None),
            P("dp", None),
            P("dp", None),
            P("dp", None),
            P(None, "dp"),
            P(None, "expert", "dp", None),
            P(None, "expert", None, "dp"),
            P("dp", None),
            P("dp", None),
            P("dp", None),
            P("dp", None),
            P("dp", None),
            P(None, "dp"),
            P(None, "expert", "dp", None),
            P(None, "expert", None, "dp"),
        ),
        out_specs=(
            P(),
            P(),
            P(),
            P("dp", None),
            P("dp", None),
            P("dp", None),
            P("dp", None),
            P("dp", None),
            P(None, "dp"),
            P(None, "expert", "dp", None),
            P(None, "expert", None, "dp"),
            P("dp", None),
            P("dp", None),
            P("dp", None),
            P("dp", None),
            P("dp", None),
            P(None, "dp"),
            P(None, "expert", "dp", None),
            P(None, "expert", None, "dp"),
            P("dp", None),
            P("dp", None),
            P("dp", None),
            P("dp", None),
            P("dp", None),
            P(None, "dp"),
            P(None, "expert", "dp", None),
            P(None, "expert", None, "dp"),
        ),
        check_vma=False,
    )
```

profile of v0, /device:TPU:0, one launch (start us, length us, event | category | flops | bytes accessed | tf_op | source)
XLA Modules:
  0.0 1420.2 jit_solution(3920848715462637323)
XLA Ops:
  10.6 33.0 %all_gather.24 = bf16[512,103]{1,0:T(8,128)(2,1)S(1)} all-gather(bf16[64,103]{1,0:T(8,128)(2,1)} %param.44), channel_id=1, replica_groups=mesh['dp'=8,'expert'=4] {'dp'}, dimensions={0}, use_global_device_ids=true | all-gather | bytes 118656 | tf_op jit(solution)/shard_map/all_gather | solution.py:325
  44.4 26.6 %all-gather = bf16[8,64,5]{1,2,0:T(8,128)(2,1)S(1)} all-gather(bf16[1,64,5]{1,2,0:T(8,128)(2,1)S(1)} %bitcast.333), channel_id=1, replica_groups=mesh['dp'=8,'expert'=4] {'dp'}, dimensions={0}, use_global_device_ids=true | all-gather | bytes 5760 | tf_op jit(solution)/shard_map/all_gather | solution.py:326
  102.2 59.1 %all-gather.9.cloned.1.call-done = bf16[2,1,2048,512]{2,3,1,0:T(8,128)(2,1)} async-done(((bf16[2,1,2048,64]{2,3,1,0:T(8,128)(2,1)}), bf16[2,1,2048,512]{2,3,1,0:T(8,128)(2,1)}) %all-gather.9.cloned.1.call-update) | async-done | bytes 4194320 | tf_op jit(solution)/shard_map/all_gather | solution.py:328
  176.3 42.2 %psum.64 = f32[]{:T(128)} all-reduce(f32[]{:T(128)} %convert_reduce_fusion), channel_id=1, replica_groups=mesh['dp'=8,'expert'=4] {'dp','expert'}, use_global_device_ids=true, to_apply=%region_33.34 | all-reduce | flops 1 | bytes 8 | tf_op jit(solution)/shard_map/psum | solution.py:372
  219.2 34.7 %all_gather.29 = bf16[512,512]{1,0:T(8,128)(2,1)} all-gather(bf16[64,512]{1,0:T(8,128)(2,1)S(1)} %copy-done.75), channel_id=1, replica_groups=mesh['dp'=8,'expert'=4] {'dp'}, dimensions={0}, use_global_device_ids=true | all-gather | bytes 589824 | tf_op jit(solution)/shard_map/all_gather | solution.py:322
  290.4 9.5 all-to-all-done.2
  321.6 9.2 all-to-all-done.3
  336.8 45.9 %all-gather.15.cloned.1.call-done = bf16[512,8192]{1,0:T(8,128)(2,1)} async-done(((bf16[64,8192]{1,0:T(8,128)(2,1)}), bf16[512,8192]{1,0:T(8,128)(2,1)}) %all-gather.15.cloned.1.call-update) | async-done | bytes 8388624 | tf_op jit(solution)/shard_map/all_gather | solution.py:324
  382.7 11.6 fusion.159
  410.5 8.4 multiply_convert_fusion
  418.9 11.1 multiply_reduce_fusion.1
  435.0 13.7 all_to_all.32
  589.7 10.4 convolution_convert_fusion
  610.1 11.3 copy.222
  634.5 63.0 %reduce-scatter.22.cloned.1.call-done = bf16[64,103]{1,0:T(8,128)(2,1)} async-done(((bf16[512,103]{1,0:T(8,128)(2,1)}), bf16[64,103]{1,0:T(8,128)(2,1)}) %reduce-scatter.22.cloned.1.call-update) | async-done | bytes 13200 | tf_op jit(solution)/shard_map/reduce_scatter | solution.py:412
  697.5 10.3 all-reduce.40
  707.7 54.7 %reduce-scatter.14.cloned.1.call-done = bf16[64,512]{1,0:T(8,128)(2,1)} async-done(((bf16[512,512]{1,0:T(8,128)(2,1)}), bf16[64,512]{1,0:T(8,128)(2,1)}) %reduce-scatter.14.cloned.1.call-update) | async-done | bytes 65552 | tf_op jit(solution)/shard_map/reduce_scatter | solution.py:403
  762.4 68.4 %reduce-scatter.16.cloned.1.call-done = bf16[64,1536]{1,0:T(8,128)(2,1)} async-done(((bf16[512,1536]{1,0:T(8,128)(2,1)}), bf16[64,1536]{1,0:T(8,128)(2,1)}) %reduce-scatter.16.cloned.1.call-update) | async-done | bytes 196624 | tf_op jit(solution)/shard_map/reduce_scatter | solution.py:406
  830.8 67.7 %reduce-scatter.12.cloned.1.call-done = bf16[64,1536]{1,0:T(8,128)(2,1)} async-done(((bf16[512,1536]{1,0:T(8,128)(2,1)}), bf16[64,1536]{1,0:T(8,128)(2,1)}) %reduce-scatter.12.cloned.1.call-update) | async-done | bytes 196624 | tf_op jit(solution)/shard_map/reduce_scatter | solution.py:400
  898.5 152.1 %reduce-scatter.18.cloned.1.call-done = bf16[64,8192]{1,0:T(8,128)(2,1)} async-done(((bf16[512,8192]{1,0:T(8,128)(2,1)}), bf16[64,8192]{1,0:T(8,128)(2,1)}) %reduce-scatter.18.cloned.1.call-update) | async-done | bytes 1048592 | tf_op jit(solution)/shard_map/reduce_scatter | solution.py:409
  1051.8 157.6 %all-reduce.45.cloned.1.call-done = bf16[2,1,2048,512]{2,0,1,3:T(2,128)(2,1)} async-done(((bf16[2,1,2048,512]{2,0,1,3:T(2,128)(2,1)}), bf16[2,1,2048,512]{2,0,1,3:T(2,128)(2,1)}) %all-reduce.45.cloned.1.call-update) | async-done | bytes 4194320
  1211.7 88.3 %reduce-scatter.20.cloned.1.call-done = bf16[2,1,64,2048]{3,2,1,0:T(8,128)(2,1)} async-done(((bf16[2,1,512,2048]{3,2,1,0:T(8,128)(2,1)}), bf16[2,1,64,2048]{3,2,1,0:T(8,128)(2,1)}) %reduce-scatter.20.cloned.1.call-update) | async-done | bytes 524304 | tf_op jit(solution)/shard_map/reduce_scatter | solution.py:418
  1303.2 41.5 %all-reduce.47.cloned.1.call-done = (bf16[64,1536]{1,0:T(8,128)(2,1)}, bf16[64,512]{1,0:T(8,128)(2,1)}, bf16[64,1536]{1,0:T(8,128)(2,1)}, bf16[64,8192]{1,0:T(8,128)(2,1)}) async-done(((bf16[64,1536]{1,0:T(8,128)(2,1)}, bf16[64,512]{1,0:T(8,128)(2,1)}, bf16[64,1536]{1,0:T(8,128)(2,1)}, bf16[64,8192]{1,0:T(8,128)(2,1)}), (bf16[64,1536]{1,0:T(8,128)(2,1)}, bf16[64,512]{1,0:T(8,128)(2,1)}, ...) | async-done | bytes 1507344 | tf_op jit(solution)/shard_map/psum | solution.py:432
  1355.9 39.9 %all-reduce.39 = (f32[]{:T(128)}, f32[]{:T(128)}) all-reduce(f32[]{:T(128)} %get-tuple-element.248, f32[]{:T(128)S(6)} %add.529), channel_id=1, replica_groups=mesh['dp'=8,'expert'=4] {'dp','expert'}, use_global_device_ids=true, to_apply=%region_31.32 | all-reduce | flops 2 | bytes 16 | tf_op jit(solution)/shard_map/psum | solution.py:372
  (666 shorter events, 324.3 us)
Async XLA Ops:
  7.2 87.8 %all-gather.7.cloned.1.call-start = ((), (), s32[]{:S(2)}) async-start(), calls=%async_computation.15 | async-start | bytes 4718592 | tf_op jit(solution)/shard_map/all_gather | solution.py:327
  8.0 153.4 %all-gather.9.cloned.1.call-start = ((), (), s32[]{:S(2)}) async-start(), calls=%async_computation.16 | async-start | bytes 4718592 | tf_op jit(solution)/shard_map/all_gather | solution.py:328
  8.7 249.6 %all-gather.11.cloned.1.call-start = ((), (), s32[]{:S(2)}) async-start(), calls=%async_computation.17 | async-start | bytes 1769472 | tf_op jit(solution)/shard_map/all_gather | solution.py:321
  9.5 262.5 %all-gather.13.cloned.1.call-start = ((), (), s32[]{:S(2)}) async-start(), calls=%async_computation.18 | async-start | bytes 1769472 | tf_op jit(solution)/shard_map/all_gather | solution.py:323
  10.0 372.7 %all-gather.15.cloned.1.call-start = ((), (), s32[]{:S(2)}) async-start(), calls=%async_computation.19 | async-start | bytes 9437184 | tf_op jit(solution)/shard_map/all_gather | solution.py:324
  44.1 213.6 %copy-start.2 = (f32[512,512]{1,0:T(8,128)}, f32[512,512]{1,0:T(8,128)S(1)}, u32[]{:S(2)}) copy-start(f32[512,512]{1,0:T(8,128)S(1)} %get-tuple-element.302) | copy-start | bytes 3145732
  71.7 200.2 %copy-start.113 = (f32[1,512]{1,0:T(1,128)}, f32[1,512]{1,0:T(1,128)S(1)}, u32[]{:S(2)}) copy-start(f32[1,512]{1,0:T(1,128)S(1)} %get-tuple-element.280) | copy-start | bytes 6148
  81.3 13.7 all-to-all-start
  94.6 374.0 %copy-start.84 = (f32[512]{0:T(512)}, f32[512]{0:T(512)S(1)}, u32[]{:S(2)}) copy-start(f32[512]{0:T(512)S(1)} %get-tuple-element.256) | copy-start | bytes 6148
  172.8 82.1 %all-to-all-start.1 = ((bf16[4,2,40960]{2,1,0:T(2,128)(2,1)}), bf16[4,2,40960]{2,1,0:T(2,128)(2,1)S(1)}, u32[]{:S(2)}, u32[]{:S(2)}) async-start(bf16[4,2,40960]{2,1,0:T(2,128)(2,1)} %reshape.945), calls=%async_computation.1 | async-start | bytes 1310720 | tf_op jit(solution)/shard_map/all_to_all | solution.py:56
  286.0 13.9 all-to-all-start.2
  316.7 14.1 all-to-all-start.3
  464.7 14.1 all-to-all-start.5
  522.1 14.5 %all-to-all-start.6 = ((bf16[4,160,512]{2,1,0:T(8,128)(2,1)}), bf16[4,160,512]{2,1,0:T(8,128)(2,1)}, u32[]{:S(2)}, u32[]{:S(2)}) async-start(bf16[4,160,512]{2,1,0:T(8,128)(2,1)} %bitcast.273), calls=%async_computation.10 | async-start | bytes 1310720 | tf_op jit(solution)/shard_map/all_to_all | solution.py:52
  553.8 13.7 all-to-all-start.7
  557.3 76.3 %reduce-scatter.24.cloned.1.call-start = ((), (), s32[]{:S(2)}) async-start(), calls=%async_computation.26 | async-start | bytes 147456
  575.5 122.0 %reduce-scatter.22.cloned.1.call-start = ((), (), s32[]{:S(2)}) async-start(), calls=%async_computation.25 | async-start | bytes 147456 | tf_op jit(solution)/shard_map/reduce_scatter | solution.py:412
  578.6 183.9 %reduce-scatter.14.cloned.1.call-start = ((), (), s32[]{:S(2)}) async-start(), calls=%async_computation.21 | async-start | bytes 589824 | tf_op jit(solution)/shard_map/reduce_scatter | solution.py:403
  580.9 249.9 %reduce-scatter.16.cloned.1.call-start = ((), (), s32[]{:S(2)}) async-start(), calls=%async_computation.22 | async-start | bytes 1769472 | tf_op jit(solution)/shard_map/reduce_scatter | solution.py:406
  585.4 313.1 %reduce-scatter.12.cloned.1.call-start = ((), (), s32[]{:S(2)}) async-start(), calls=%async_computation.20 | async-start | bytes 1769472 | tf_op jit(solution)/shard_map/reduce_scatter | solution.py:400
  589.6 461.0 %reduce-scatter.18.cloned.1.call-start = ((), (), s32[]{:S(2)}) async-start(), calls=%async_computation.23 | async-start | bytes 9437184 | tf_op jit(solution)/shard_map/reduce_scatter | solution.py:409
  600.1 609.3 %all-reduce.45.cloned.1.call-start = ((), (), s32[]{:S(2)}) async-start(), calls=%async_computation.27 | async-start | bytes 8388608
  621.4 678.6 %reduce-scatter.20.cloned.1.call-start = ((), (), s32[]{:S(2)}) async-start(), calls=%async_computation.24 | async-start | bytes 4718592 | tf_op jit(solution)/shard_map/reduce_scatter | solution.py:418
  630.4 714.3 %all-reduce.47.cloned.1.call-start = ((), (), s32[]{:S(2)}) async-start(), calls=%async_computation.28 | async-start | bytes 3014656 | tf_op jit(solution)/shard_map/psum | solution.py:432
  (203 other events, 4891.2 us)
Sparse Core Ops, SparseCore 0:
  10.3 77.2 all-gather.6
  89.8 71.5 all-gather.8
  163.6 42.9 all-gather.10
  208.6 47.0 all-gather.12
  257.7 124.9 all-gather.14
  575.6 58.0 reduce-scatter.23
  637.6 59.8 reduce-scatter.21
  701.4 60.9 reduce-scatter.13
  766.8 63.9 reduce-scatter.15
  834.6 63.8 reduce-scatter.11
  902.6 147.9 reduce-scatter.17
  1054.1 155.2 all-reduce.44
  1213.1 86.9 reduce-scatter.19
  1302.6 42.0 all-reduce.46
where the time goes:
time: 1430 us; the launch traced here: 1420 us
  waiting for transfers between devices  840 us (59%)
  blocking collectives  200 us (14%)
  matrix products  124 us (9%)
  other arithmetic  107 us (7%)
  local copies, waits for them, and re-layouts  96.1 us (7%)
  starting transfers between devices  27.3 us (2%)
  between operations  25.7 us (2%)
    unnamed x16, waiting for transfers between devices  162 us
    reduce_scatter x1, waiting for transfers between devices, on_device(): lax.psum_scatter(head_grad.astype(jnp.bfloat16), 'dp', scatter_dimension=...  152 us
    reduce_scatter x1, waiting for transfers between devices, on_device(): lax.psum_scatter(jnp.stack([back_one[3], back_two[3]]).astype(jnp.bfloat1...  88.3 us
    psum x2, blocking collectives, on_device(): lax.psum((loss_part, jnp.sum(counted)), ('dp', 'expert'))  82.1 us
    reduce_scatter x1, waiting for transfers between devices, on_device(): lax.psum_scatter(back_conv[2].astype(jnp.bfloat16), 'dp', scatter_dimensi...  68.4 us
    reduce_scatter x1, waiting for transfers between devices, on_device(): lax.psum_scatter(back_attend[2].astype(jnp.bfloat16), 'dp', scatter_dimen...  67.7 us
    reduce_scatter x1, waiting for transfers between devices, on_device(): lax.psum_scatter(extra_grad.astype(jnp.bfloat16), 'dp', scatter_dimension...  63 us
    all_gather x1, waiting for transfers between devices, on_device(): lax.all_gather(down_copy, 'dp', axis=3, tiled=True)  59.1 us
  transfers between devices with their start and end apart: 21, of which 17 were waited for; matrix products, arithmetic and copies ran while one was open for 11% of the time, Pallas kernels for 0%

commit v1 on v0

v1 whole, which is shorter than its diff:
```python
import functools
import math

import jax
import jax.numpy as jnp
import numpy as np
from jax import lax
from jax.experimental import pallas as pl
from jax.experimental.pallas import tpu as pltpu
from jax.sharding import PartitionSpec as P

HEADS = 8
STEP = 5
NORM_EPS = 1e-05
ADAM_EPS = 1e-08
BETA_ONE = 0.5
BETA_TWO = 0.5
MASKED = -1000000000.0
STEP_RATES = (0.02, 0.2, 0.02, 0.05, 0.05, 0.5, 0.02, 0.1)
DECAYS = (0.01, 0.01, 0.01, 0.01, 0.01, 0.0, 0.01, 0.01)

BF = jnp.bfloat16
F32 = jnp.float32
ALL = ("dp", "expert")
VMEM_BYTES = 56 * 1024 * 1024
LANES = 128
TAP_PAD = 16


def nn(left, right):
    return jnp.dot(left, right, preferred_element_type=F32)


def nt(left, right):
    return lax.dot_general(left, right, (((1,), (1,)), ((), ())), preferred_element_type=F32)


def tn(left, right):
    return lax.dot_general(left, right, (((0,), (0,)), ((), ())), preferred_element_type=F32)


def norm_parts(values):
    centred = values - jnp.mean(values, axis=-1, keepdims=True)
    scale = lax.rsqrt(jnp.mean(centred * centred, axis=-1, keepdims=True) + NORM_EPS)
    return centred * scale, scale


def norm_back(grad, unit, scale, gain_row):
    weighted = grad * gain_row
    mean = jnp.mean(weighted, axis=-1, keepdims=True)
    along = jnp.mean(weighted * unit, axis=-1, keepdims=True)
    gain_grad = jnp.sum(grad * unit, axis=0, keepdims=True)
    return scale * (weighted - mean - unit * along), gain_grad


def lane_softmax(logits, first, count):
    lane = lax.broadcasted_iota(jnp.int32, logits.shape, 1)
    inside = (lane >= first) & (lane < first + count)
    logits = jnp.where(inside, logits, -jnp.inf)
    weight = jnp.exp(logits - jnp.max(logits, axis=-1, keepdims=True))
    return weight / jnp.sum(weight, axis=-1, keepdims=True)


def chosen_lanes(route_col, first, shape):
    lane = lax.broadcasted_iota(jnp.int32, shape, 1)
    return lane == (route_col.astype(jnp.int32) + first)


def bounds_of(lengths_ref):
    first = lengths_ref[0, 0]
    second = first + lengths_ref[0, 1]
    return first, second, second + lengths_ref[0, 2]


def segment_of(places, bounds):
    total = jnp.zeros(places.shape, jnp.int32)
    for bound in bounds:
        total = total + (places >= bound).astype(jnp.int32)
    return total


def tap_masks(rows, half_span, bounds):
    place = lax.broadcasted_iota(jnp.int32, (rows, LANES), 0)
    lane = lax.broadcasted_iota(jnp.int32, (rows, LANES), 1)
    same = segment_of(place, bounds) == segment_of(place + lane - half_span, bounds)
    return same.astype(F32)


def start_copies(pairs, sems):
    copies = [pltpu.make_async_copy(src, dst, sems.at[i]) for i, (src, dst) in enumerate(pairs)]
    for copy in copies:
        copy.start()
    return copies


def rows_at(rank, rows):
    return pl.ds(pl.multiple_of(rank * rows, rows), rows)


def shared_pairs(mine_ref, other_ref, full_ref, ranks_ref, core, steps, rows):
    width = mine_ref.shape[-1]
    own = pl.ds(pl.multiple_of(core * width, LANES), width)
    far = pl.ds(pl.multiple_of((1 - core) * width, LANES), width)
    pairs = []
    for k in range(steps):
        pairs.append((mine_ref.at[k], full_ref.at[rows_at(ranks_ref[0, k], rows), own]))
        pairs.append((other_ref.at[k], full_ref.at[rows_at(ranks_ref[1, k], rows), far]))
    return pairs


def shared_out_pairs(full_ref, mine_ref, other_ref, ranks_ref, core, steps, rows):
    width = mine_ref.shape[-1]
    own = pl.ds(pl.multiple_of(core * width, LANES), width)
    far = pl.ds(pl.multiple_of((1 - core) * width, LANES), width)
    pairs = []
    for k in range(steps):
        later = (k + 1) % steps
        pairs.append((full_ref.at[rows_at(ranks_ref[0, later], rows), own], mine_ref.at[k]))
        pairs.append((full_ref.at[rows_at(ranks_ref[1, later], rows), far], other_ref.at[k]))
    return pairs


def routing_kernel(capacity, routes_ref, align_ref, cols_ref, *place_refs):
    rows = routes_ref.shape[2]
    before = (
        lax.broadcasted_iota(jnp.int32, (rows, rows), 0)
        < lax.broadcasted_iota(jnp.int32, (rows, rows), 1)
    ).astype(BF)
    kept = []
    slots = []
    for f in range(2):
        route_row = routes_ref[f]
        named = lax.broadcasted_iota(jnp.int32, (16, rows), 0) == route_row
        counts = nn(named.astype(BF), before)
        rank = jnp.sum(jnp.where(named, counts, 0.0), axis=0, keepdims=True)
        slots.append(route_row.astype(F32) * capacity + rank)
        kept.append(route_row.astype(F32))
    lines = jnp.concatenate(
        kept + [align_ref[...].astype(F32)] + slots + [jnp.zeros((LANES - 5, rows), F32)], axis=0
    )
    cols = lines.T
    cols_ref[...] = cols
    for f in range(2):
        down_ref, across_ref = place_refs[2 * f], place_refs[2 * f + 1]
        slot_count = down_ref.shape[0]
        slot_row = slots[f].astype(jnp.int32)
        slot_col = cols[:, 3 + f : 4 + f].astype(jnp.int32)
        down_ref[...] = (
            lax.broadcasted_iota(jnp.int32, (slot_count, rows), 0) == slot_row
        ).astype(BF)
        across_ref[...] = (
            lax.broadcasted_iota(jnp.int32, (rows, slot_count), 1) == slot_col
        ).astype(BF)


def front_kernel(experts, feat_ref, extra_ref, place_ref, gain_at, x0_ref, slots_ref, prob_ref, lines_ref):
    extra = extra_ref[...]
    lines_ref[...] = extra.astype(F32).T
    feats = feat_ref.shape[0]
    table = lines_ref[2 * experts : 2 * experts + feats, :].astype(BF)
    embedded = tn(feat_ref[...], table)
    x0_ref[...] = embedded
    unit, _ = norm_parts(embedded)
    low = (unit * lines_ref[gain_at : gain_at + 1, :]).astype(BF)
    prob_ref[...] = lane_softmax(nn(low, extra), 0, experts)
    slots_ref[...] = nn(place_ref[...], low).astype(BF)


def load_experts(ranks_ref, chunk_refs, weight_ref, sems):
    rows = chunk_refs[0].shape[1]
    pairs = [
        (chunk, weight_ref.at[:, rows_at(ranks_ref[0, k], rows), :])
        for k, chunk in enumerate(chunk_refs)
    ]
    return start_copies(pairs, sems)


def expert_forward_kernel(steps, tile, ranks_ref, slots_ref, *refs):
    chunk_refs = refs[:steps]
    out_ref, weight_ref, sems = refs[steps:]
    for copy in load_experts(ranks_ref, chunk_refs, weight_ref, sems):
        copy.wait()
    slots = slots_ref[...]
    total = jnp.zeros(out_ref.shape, F32)
    for at in range(0, weight_ref.shape[2], tile):
        hidden = nn(slots, weight_ref[0, :, at : at + tile])
        active = (hidden * jax.nn.sigmoid(hidden)).astype(BF)
        total = total + nt(active, weight_ref[1, :, at : at + tile])
    out_ref[...] = total.astype(BF)


def expert_backward_kernel(steps, tile, ranks_ref, slots_ref, grad_ref, *refs):
    chunk_refs = refs[:steps]
    back_ref, active_ref, hidden_ref, weight_ref, sems = refs[steps:]
    for copy in load_experts(ranks_ref, chunk_refs, weight_ref, sems):
        copy.wait()
    slots = slots_ref[...]
    grad = grad_ref[...]
    total = jnp.zeros(back_ref.shape, F32)
    for at in range(0, weight_ref.shape[2], tile):
        here = slice(at, at + tile)
        hidden = nn(slots, weight_ref[0, :, here])
        gate = jax.nn.sigmoid(hidden)
        active_ref[:, here] = (hidden * gate).astype(BF)
        hidden_grad = (nn(grad, weight_ref[1, :, here]) * gate * (1.0 + hidden * (1.0 - gate))).astype(BF)
        hidden_ref[:, here] = hidden_grad
        total = total + nt(hidden_grad, weight_ref[0, :, here])
    back_ref[...] = total.astype(BF)


def expert_grads_kernel(steps, tile, ranks_ref, slots_ref, grad_ref, active_ref, hidden_ref, *refs):
    out_refs = refs[:steps]
    sum_ref, sems = refs[steps:]
    slots = slots_ref[...]
    grad = grad_ref[...]
    for at in range(0, active_ref.shape[1], tile):
        here = slice(at, at + tile)
        sum_ref[0, :, here] = tn(slots, hidden_ref[:, here]).astype(BF)
        sum_ref[1, :, here] = tn(grad, active_ref[:, here]).astype(BF)
    rows = out_refs[0].shape[1]
    pairs = [
        (sum_ref.at[:, rows_at(ranks_ref[0, (k + 1) % steps], rows), :], out)
        for k, out in enumerate(out_refs)
    ]
    for copy in start_copies(pairs, sems):
        copy.wait()


def head_lanes(pair_at, shape):
    lane = lax.broadcasted_iota(jnp.int32, shape, 1)
    return (lane < LANES // 2) if pair_at == 0 else (lane >= LANES // 2)


def conv_taps(padded_ref, masks, taps, flip):
    rows = masks.shape[0]
    count = len(taps)
    half = count // 2
    total = jnp.zeros((rows, padded_ref.shape[1]), F32)
    for j in range(count):
        shifted = padded_ref[TAP_PAD + j - half : TAP_PAD + j - half + rows, :]
        tap = taps[count - 1 - j] if flip else taps[j]
        total = total + shifted * masks[:, j : j + 1] * tap
    return total


def middle_forward_kernel(
    dims,
    ranks_ref,
    lengths_ref,
    x0_ref,
    prob_ref,
    cols_ref,
    across_ref,
    returned_ref,
    place_ref,
    extra_ref,
    lines_ref,
    mine_ref,
    other_ref,
    h1_ref,
    h2_ref,
    h3_ref,
    log_ref,
    prob_two_ref,
    slots_ref,
    weight_ref,
    packed_ref,
    blended_ref,
    padded_ref,
    sems,
):
    experts, steps, shard, tap_at, taps_count, gain_at = dims
    core = ranks_ref[2, 0]
    copies = start_copies(
        shared_pairs(mine_ref, other_ref, weight_ref, ranks_ref, core, steps, shard), sems
    )
    rows, width = x0_ref.shape
    bounds = bounds_of(lengths_ref)
    gain = lambda i: lines_ref[gain_at + i : gain_at + i + 1, :]
    prob = prob_ref[...]
    gate = jnp.sum(
        jnp.where(chosen_lanes(cols_ref[:, 0:1], 0, prob.shape), prob, 0.0), axis=-1, keepdims=True
    )
    h1 = x0_ref[...] + 0.5 * (gate * nn(across_ref[...], returned_ref[...]))
    h1_ref[...] = h1
    unit, _ = norm_parts(h1)
    low = (unit * gain(1)).astype(BF)
    for copy in copies:
        copy.wait()
    packed_ref[...] = nn(low, weight_ref[:, : 3 * width]).astype(BF)
    same = segment_of(lax.broadcasted_iota(jnp.int32, (rows, 1), 0), bounds) == segment_of(
        lax.broadcasted_iota(jnp.int32, (1, rows), 1), bounds
    )
    scale = (width // HEADS) ** (-0.5)
    log_lane = lax.broadcasted_iota(jnp.int32, (rows, LANES), 1)
    logs = jnp.zeros((rows, LANES), F32)
    for pair in range(HEADS // 2):
        at = pair * LANES
        query = packed_ref[:, at : at + LANES]
        keys = packed_ref[:, width + at : width + at + LANES]
        values = packed_ref[:, 2 * width + at : 2 * width + at + LANES]
        mixed = None
        for half in range(2):
            mine = head_lanes(half, query.shape)
            scores = nt(jnp.where(mine, query, jnp.zeros_like(query)), keys) * scale
            scores = jnp.where(same, scores, MASKED)
            top = jnp.max(scores, axis=-1, keepdims=True)
            exponent = jnp.exp(scores - top)
            sums = jnp.sum(exponent, axis=-1, keepdims=True)
            weights = (exponent * (1.0 / sums)).astype(BF)
            part = nn(weights, values)
            mixed = part if half == 0 else jnp.where(mine, part, mixed)
            logs = jnp.where(log_lane == 2 * pair + half, top + jnp.log(sums), logs)
        blended_ref[:, at : at + LANES] = mixed.astype(BF)
    log_ref[...] = logs
    h2 = h1 + nn(blended_ref[...], weight_ref[:, 3 * width : 4 * width])
    h2_ref[...] = h2
    unit, _ = norm_parts(h2)
    low = (unit * gain(2)).astype(BF)
    first = nn(low, weight_ref[:, 4 * width : 5 * width])
    second = nn(low, weight_ref[:, 5 * width : 6 * width])
    padded_ref[:TAP_PAD, :] = jnp.zeros((TAP_PAD, width), F32)
    padded_ref[TAP_PAD + rows :, :] = jnp.zeros((TAP_PAD, width), F32)
    padded_ref[TAP_PAD : TAP_PAD + rows, :] = first * jax.nn.sigmoid(second)
    taps = [lines_ref[tap_at + j : tap_at + j + 1, :] for j in range(taps_count)]
    mixed = conv_taps(padded_ref, tap_masks(rows, taps_count // 2, bounds), taps, False)
    active = (mixed * jax.nn.sigmoid(mixed)).astype(BF)
    h3 = h2 + nn(active, weight_ref[:, 6 * width :])
    h3_ref[...] = h3
    unit, _ = norm_parts(h3)
    low = (unit * gain(3)).astype(BF)
    prob_two_ref[...] = lane_softmax(nn(low, extra_ref[...]), experts, experts)
    slots_ref[...] = nn(place_ref[...], low).astype(BF)


def gate_backward(grad, prob, chosen, gate, rows_chosen):
    gate_grad = jnp.sum(grad * rows_chosen, axis=-1, keepdims=True)
    logit_grad = prob * (jnp.where(chosen, gate_grad, 0.0) - gate * gate_grad)
    return logit_grad.astype(BF)


def head_kernel(
    dims,
    ranks_ref,
    lengths_ref,
    frames_ref,
    h3_ref,
    prob_ref,
    cols_ref,
    across_ref,
    returned_ref,
    place_ref,
    lines_ref,
    mine_ref,
    other_ref,
    two_grad_ref,
    logit_grad_ref,
    slots_ref,
    gain_grad_ref,
    loss_ref,
    grad_mine_ref,
    grad_other_ref,
    weight_ref,
    logits_ref,
    grad_ref,
    sems,
):
    experts, steps, shard, gain_at, tile = dims
    core = ranks_ref[2, 0]
    copies = start_copies(
        shared_pairs(mine_ref, other_ref, weight_ref, ranks_ref, core, steps, shard), sems
    )
    rows, width = h3_ref.shape
    vocab = weight_ref.shape[1]
    gain = lines_ref[gain_at + 4 : gain_at + 5, :]
    prob = prob_ref[...]
    chosen = chosen_lanes(cols_ref[:, 1:2], experts, prob.shape)
    gate = jnp.sum(jnp.where(chosen, prob, 0.0), axis=-1, keepdims=True)
    rows_chosen = nn(across_ref[...], returned_ref[...])
    h4 = h3_ref[...] + 0.5 * (gate * rows_chosen)
    unit, scale = norm_parts(h4)
    low = (unit * gain).astype(BF)
    for copy in copies:
        copy.wait()

    def first_pass(i, carry):
        top, sums = carry
        at = pl.multiple_of(i * tile, tile)
        logits = nn(low, weight_ref[:, pl.ds(at, tile)])
        logits_ref[:, pl.ds(at, tile)] = logits
        higher = jnp.maximum(top, jnp.max(logits, axis=-1, keepdims=True))
        sums = sums * jnp.exp(top - higher) + jnp.sum(jnp.exp(logits - higher), axis=-1, keepdims=True)
        return higher, sums

    top, sums = lax.fori_loop(
        0,
        vocab // tile,
        first_pass,
        (jnp.full((rows, 1), -jnp.inf, F32), jnp.zeros((rows, 1), F32)),
    )
    log_total = top + jnp.log(sums)
    _, _, counted_end = bounds_of(lengths_ref)
    counted = (lax.broadcasted_iota(jnp.int32, (rows, 1), 0) < counted_end).astype(F32)
    portion = counted / frames_ref[0, 0]
    target = cols_ref[:, 2:3].astype(jnp.int32)

    def second_pass(i, carry):
        total, picked = carry
        at = pl.multiple_of(i * tile, tile)
        logits = logits_ref[:, pl.ds(at, tile)]
        hit = lax.broadcasted_iota(jnp.int32, (rows, tile), 1) == (target - at)
        picked = picked + jnp.sum(jnp.where(hit, logits, 0.0), axis=-1, keepdims=True)
        guess = jnp.exp(logits - log_total)
        low_grad = (jnp.where(hit, guess - 1.0, guess) * portion).astype(BF)
        grad_ref[:, pl.ds(at, tile)] = tn(low, low_grad).astype(BF)
        return total + nt(low_grad, weight_ref[:, pl.ds(at, tile)]), picked

    total, picked = lax.fori_loop(
        0,
        vocab // tile,
        second_pass,
        (jnp.zeros((rows, width), F32), jnp.zeros((rows, 1), F32)),
    )
    out_copies = start_copies(
        shared_out_pairs(grad_ref, grad_mine_ref, grad_other_ref, ranks_ref, core, steps, shard), sems
    )
    loss = jnp.sum((log_total - picked) * counted, axis=0, keepdims=True)
    loss_ref[...] = jnp.broadcast_to(loss, loss_ref.shape)
    two_grad, gain_grad = norm_back(total, unit, scale, gain)
    two_grad_ref[...] = two_grad
    gain_grad_ref[...] = jnp.broadcast_to(gain_grad, gain_grad_ref.shape)
    half_grad = 0.5 * two_grad
    logit_grad_ref[...] = gate_backward(half_grad, prob, chosen, gate, rows_chosen)
    slots_ref[...] = nn(place_ref[...], (gate * half_grad).astype(BF)).astype(BF)
    for copy in out_copies:
        copy.wait()


def middle_backward_kernel(
    dims,
    ranks_ref,
    lengths_ref,
    two_grad_ref,
    returned_two_ref,
    across_two_ref,
    logit_two_ref,
    h1_ref,
    h2_ref,
    h3_ref,
    log_ref,
    prob_ref,
    cols_ref,
    across_ref,
    returned_ref,
    place_ref,
    extra_ref,
    lines_ref,
    mine_ref,
    other_ref,
    one_grad_ref,
    logit_ref,
    slots_ref,
    small_ref,
    router_ref,
    grad_mine_ref,
    grad_other_ref,
    weight_ref,
    packed_ref,
    packed_grad_ref,
    blended_ref,
    padded_ref,
    padded_grad_ref,
    grad_ref,
    sems,
):
    experts, steps, shard, tap_at, taps_count, gain_at = dims
    core = ranks_ref[2, 0]
    copies = start_copies(
        shared_pairs(mine_ref, other_ref, weight_ref, ranks_ref, core, steps, shard), sems
    )
    rows, width = h1_ref.shape
    bounds = bounds_of(lengths_ref)
    gain = lambda i: lines_ref[gain_at + i : gain_at + i + 1, :]
    small_ref[...] = jnp.zeros(small_ref.shape, F32)
    unit, scale = norm_parts(h3_ref[...])
    low = (unit * gain(3)).astype(BF)
    logit_two = logit_two_ref[...]
    router_ref[...] = tn(logit_two, low)
    back = nn(across_two_ref[...], returned_two_ref[...]) + nt(logit_two, extra_ref[...])
    change, gain_grad = norm_back(back, unit, scale, gain(3))
    small_ref[taps_count : taps_count + 1, :] = gain_grad
    upstream = two_grad_ref[...] + change
    for copy in copies:
        copy.wait()
    upstream_low = upstream.astype(BF)
    unit, scale = norm_parts(h2_ref[...])
    low = (unit * gain(2)).astype(BF)
    first = nn(low, weight_ref[:, 4 * width : 5 * width])
    gate_half = jax.nn.sigmoid(nn(low, weight_ref[:, 5 * width : 6 * width]))
    padded_ref[:TAP_PAD, :] = jnp.zeros((TAP_PAD, width), F32)
    padded_ref[TAP_PAD + rows :, :] = jnp.zeros((TAP_PAD, width), F32)
    padded_ref[TAP_PAD : TAP_PAD + rows, :] = first * gate_half
    taps = [lines_ref[tap_at + j : tap_at + j + 1, :] for j in range(taps_count)]
    masks = tap_masks(rows, taps_count // 2, bounds)
    mixed = conv_taps(padded_ref, masks, taps, False)
    gate_mixed = jax.nn.sigmoid(mixed)
    active = (mixed * gate_mixed).astype(BF)
    grad_ref[:, 6 * width :] = tn(active, upstream_low).astype(BF)
    mixed_grad = (
        nt(upstream_low, weight_ref[:, 6 * width :]) * gate_mixed * (1.0 + mixed * (1.0 - gate_mixed))
    )
    padded_grad_ref[:TAP_PAD, :] = jnp.zeros((TAP_PAD, width), F32)
    padded_grad_ref[TAP_PAD + rows :, :] = jnp.zeros((TAP_PAD, width), F32)
    padded_grad_ref[TAP_PAD : TAP_PAD + rows, :] = mixed_grad
    half = taps_count // 2
    for j in range(taps_count):
        shifted = padded_ref[TAP_PAD + j - half : TAP_PAD + j - half + rows, :]
        small_ref[j : j + 1, :] = jnp.sum(
            shifted * masks[:, j : j + 1] * mixed_grad, axis=0, keepdims=True
        )
    gated_grad = conv_taps(padded_grad_ref, masks, taps, True)
    first_low = (gated_grad * gate_half).astype(BF)
    second_low = (gated_grad * first * gate_half * (1.0 - gate_half)).astype(BF)
    grad_ref[:, 4 * width : 5 * width] = tn(low, first_low).astype(BF)
    grad_ref[:, 5 * width : 6 * width] = tn(low, second_low).astype(BF)
    back = nt(first_low, weight_ref[:, 4 * width : 5 * width]) + nt(
        second_low, weight_ref[:, 5 * width : 6 * width]
    )
    change, gain_grad = norm_back(back, unit, scale, gain(2))
    small_ref[taps_count + 1 : taps_count + 2, :] = gain_grad
    upstream = upstream + change
    upstream_low = upstream.astype(BF)
    unit, scale_norm = norm_parts(h1_ref[...])
    low = (unit * gain(1)).astype(BF)
    packed_ref[...] = nn(low, weight_ref[:, : 3 * width]).astype(BF)
    mixed_low = nt(upstream_low, weight_ref[:, 3 * width : 4 * width]).astype(BF)
    same = segment_of(lax.broadcasted_iota(jnp.int32, (rows, 1), 0), bounds) == segment_of(
        lax.broadcasted_iota(jnp.int32, (1, rows), 1), bounds
    )
    scale = (width // HEADS) ** (-0.5)
    for pair in range(HEADS // 2):
        at = pair * LANES
        query = packed_ref[:, at : at + LANES]
        keys = packed_ref[:, width + at : width + at + LANES]
        values = packed_ref[:, 2 * width + at : 2 * width + at + LANES]
        spread = mixed_low[:, at : at + LANES]
        held = None
        for part in range(2):
            mine = head_lanes(part, query.shape)
            head = 2 * pair + part
            scores = nt(jnp.where(mine, query, jnp.zeros_like(query)), keys) * scale
            scores = jnp.where(same, scores, MASKED)
            probs = jnp.exp(scores - log_ref[:, head : head + 1])
            weights = probs.astype(BF)
            prob_grad = nt(jnp.where(mine, spread, jnp.zeros_like(spread)), values)
            centre = jnp.sum(probs * prob_grad, axis=-1, keepdims=True)
            score_grad = (probs * (prob_grad - centre)).astype(BF)
            found = (
                nn(weights, values),
                tn(weights, spread),
                nn(score_grad, keys) * scale,
                tn(score_grad, query) * scale,
            )
            held = found if part == 0 else tuple(jnp.where(mine, new, old) for new, old in zip(found, held))
        blended_ref[:, at : at + LANES] = held[0].astype(BF)
        packed_grad_ref[:, 2 * width + at : 2 * width + at + LANES] = held[1].astype(BF)
        packed_grad_ref[:, at : at + LANES] = held[2].astype(BF)
        packed_grad_ref[:, width + at : width + at + LANES] = held[3].astype(BF)
    grad_ref[:, 3 * width : 4 * width] = tn(blended_ref[...], upstream_low).astype(BF)
    packed_grad = packed_grad_ref[...]
    grad_ref[:, : 3 * width] = tn(low, packed_grad).astype(BF)
    out_copies = start_copies(
        shared_out_pairs(grad_ref, grad_mine_ref, grad_other_ref, ranks_ref, core, steps, shard), sems
    )
    change, gain_grad = norm_back(
        nt(packed_grad, weight_ref[:, : 3 * width]), unit, scale_norm, gain(1)
    )
    small_ref[taps_count + 2 : taps_count + 3, :] = gain_grad
    one_grad = upstream + change
    one_grad_ref[...] = one_grad
    prob = prob_ref[...]
    chosen = chosen_lanes(cols_ref[:, 0:1], 0, prob.shape)
    gate = jnp.sum(jnp.where(chosen, prob, 0.0), axis=-1, keepdims=True)
    half_grad = 0.5 * one_grad
    rows_chosen = nn(across_ref[...], returned_ref[...])
    logit_ref[...] = gate_backward(half_grad, prob, chosen, gate, rows_chosen)
    slots_ref[...] = nn(place_ref[...], (gate * half_grad).astype(BF)).astype(BF)
    for copy in out_copies:
        copy.wait()


def back_kernel(
    dims,
    one_grad_ref,
    returned_ref,
    across_ref,
    logit_ref,
    x0_ref,
    feat_ref,
    extra_ref,
    lines_ref,
    small_ref,
    router_ref,
    gain_four_ref,
    out_ref,
    lines_grad_ref,
):
    experts, tap_at, taps_count, gain_at = dims
    feats = feat_ref.shape[0]
    unit, scale = norm_parts(x0_ref[...])
    gain = lines_ref[gain_at : gain_at + 1, :]
    low = (unit * gain).astype(BF)
    logit = logit_ref[...]
    back = nn(across_ref[...], returned_ref[...]) + nt(logit, extra_ref[...])
    change, gain_grad = norm_back(back, unit, scale, gain)
    embedded_low = (one_grad_ref[...] + change).astype(BF)
    lines_grad_ref[...] = tn(logit, low) + router_ref[...]
    lines_grad_ref[2 * experts : 2 * experts + feats, :] = nn(feat_ref[...], embedded_low)
    lines_grad_ref[tap_at : tap_at + taps_count, :] = small_ref[:taps_count, :]
    lines_grad_ref[gain_at : gain_at + 1, :] = gain_grad
    lines_grad_ref[gain_at + 1 : gain_at + 2, :] = small_ref[taps_count + 2 : taps_count + 3, :]
    lines_grad_ref[gain_at + 2 : gain_at + 3, :] = small_ref[taps_count + 1 : taps_count + 2, :]
    lines_grad_ref[gain_at + 3 : gain_at + 4, :] = small_ref[taps_count : taps_count + 1, :]
    lines_grad_ref[gain_at + 4 : gain_at + 5, :] = gain_four_ref[0:1, :]
    out_ref[...] = lines_grad_ref[...].T.astype(BF)


def spec(kind):
    space = {"v": pltpu.VMEM, "s": pltpu.SMEM, "a": pl.ANY}[kind]
    return pl.BlockSpec(memory_space=space)


def shaped(shape, dtype):
    return jax.ShapeDtypeStruct(shape, dtype)


def call(kernel, name, kinds, args, outs, out_kinds, scratch=(), flops=0, moved=0):
    return pl.pallas_call(
        kernel,
        name=name,
        out_shape=tuple(outs),
        in_specs=[spec(kind) for kind in kinds],
        out_specs=tuple(spec(kind) for kind in out_kinds),
        scratch_shapes=list(scratch),
        compiler_params=pltpu.CompilerParams(vmem_limit_bytes=VMEM_BYTES),
        cost_estimate=pl.CostEstimate(flops=int(flops), bytes_accessed=int(moved), transcendentals=0),
    )(*args)


def ring_order(size):
    return list(range(0, size, 2)) + list(range(size - 1 - (size % 2), 0, -2))


def ring_pairs(size, experts):
    order = ring_order(size)
    pairs = []
    for place in range(size):
        for e in range(experts):
            step = 1 if e % 2 == 0 else -1
            pairs.append((order[place] * experts + e, order[(place + step) % size] * experts + e))
    return pairs


def rank_table(size):
    order = ring_order(size)
    where = {rank: place for place, rank in enumerate(order)}
    table = np.zeros((size, 2, size), np.int32)
    for rank in range(size):
        for core in range(2):
            step = 1 if core == 0 else -1
            for k in range(size):
                table[rank, core, k] = order[(where[rank] - step * k) % size]
    return table


def ring_step(array, pairs):
    return lax.ppermute(array, ALL, pairs)


def ring_gather(shard, pairs, size):
    chunks = [shard]
    for _ in range(size - 1):
        chunks.append(ring_step(chunks[-1], pairs))
    return chunks


def core_swap(array, experts):
    return lax.ppermute(array, "expert", [(e, e ^ 1) for e in range(experts)])


def over_chips(array, experts):
    total = array.astype(F32)
    chips = experts // 2
    for shift in range(1, chips):
        moved = lax.ppermute(
            array, "expert", [(e, (e // 2 + shift) % chips * 2 + e % 2) for e in range(experts)]
        )
        total = total + moved.astype(F32)
    return total


def swap_rows(slots, experts):
    parts = slots.reshape(experts, slots.shape[0] // experts, slots.shape[1])
    return lax.all_to_all(parts, "expert", split_axis=0, concat_axis=0, tiled=True).reshape(slots.shape)


def shared_scatter(mine, other, pairs, size, experts, core):
    arrived = core_swap(other, experts)
    partial = (mine[0] + arrived[0]).astype(BF)
    for k in range(1, size):
        partial = ring_step(partial, pairs) + (mine[k] + arrived[k])
    own = over_chips(partial, experts).astype(BF)
    far = core_swap(own, experts)
    return jnp.where(core == 0, jnp.concatenate([own, far], 1), jnp.concatenate([far, own], 1))


def expert_scatter(chunks, pairs):
    partial = chunks[0]
    for chunk in chunks[1:]:
        partial = ring_step(partial, pairs) + chunk
    return partial


def adamw(gradient, master, moment, square, rate, decay):
    moment = BETA_ONE * moment + (1.0 - BETA_ONE) * gradient
    square = BETA_TWO * square + (1.0 - BETA_TWO) * gradient * gradient
    update = (
        moment / (1.0 - BETA_ONE**STEP) / (jnp.sqrt(square / (1.0 - BETA_TWO**STEP)) + ADAM_EPS)
    )
    return (moment, square, master - rate * (update + decay * master))


def on_device(features, lengths, routes, alignment, *weights):
    copies, masters, firsts, seconds = (weights[8 * i : 8 * i + 8] for i in range(4))
    attend_copy, output_copy, conv_copy, head_copy, extra_copy, gains_copy, up_copy, down_copy = copies
    size = lax.axis_size("dp")
    experts = lax.axis_size("expert")
    dp_at = lax.axis_index("dp")
    expert_at = lax.axis_index("expert")
    core = expert_at % 2
    row_count, feat_count = features.shape
    shard = attend_copy.shape[0]
    width = shard * size
    vocab = head_copy.shape[1]
    units = up_copy.shape[3]
    aux = extra_copy.shape[1]
    taps_count = aux - 2 * experts - feat_count
    tap_at = 2 * experts + feat_count
    gain_at = aux
    capacity = row_count * 5 // (4 * experts)
    slot_count = experts * capacity
    pairs = ring_pairs(size, experts)
    table = jnp.asarray(rank_table(size))[dp_at]
    ranks = jnp.concatenate(
        [
            lax.dynamic_index_in_dim(table, core, 0, keepdims=True),
            lax.dynamic_index_in_dim(table, 1 - core, 0, keepdims=True),
            jnp.full((1, size), core, jnp.int32),
        ]
    )

    pack = jnp.concatenate(
        [extra_copy, gains_copy.T, jnp.zeros((shard, LANES - aux - gains_copy.shape[0]), BF)], axis=1
    )
    extra = lax.all_to_all(
        jnp.broadcast_to(pack[None], (size,) + pack.shape), "dp", split_axis=0, concat_axis=0, tiled=True
    ).reshape(width, LANES)
    everyone = size * experts
    frames_here = (row_count - lengths[0, 3]).astype(F32)
    frame_count = jnp.sum(
        lax.all_to_all(
            jnp.broadcast_to(frames_here, (everyone, 1, LANES)), ALL, split_axis=0, concat_axis=0, tiled=True
        )[:, 0, 0]
    )

    expert_shards = [
        jnp.stack([up_copy[f, 0], down_copy[f, 0].T]) for f in range(2)
    ]
    first_chunks = ring_gather(expert_shards[0], pairs, size)
    second_chunks = ring_gather(expert_shards[1], pairs, size)
    shared = jnp.concatenate([attend_copy, output_copy, conv_copy], axis=1)
    half_shared = shared.shape[1] // 2
    shared_mine = jnp.stack(
        ring_gather(lax.dynamic_slice_in_dim(shared, core * half_shared, half_shared, 1), pairs, size)
    )
    shared_other = core_swap(shared_mine, experts)
    half_vocab = vocab // 2
    head_mine = jnp.stack(
        ring_gather(lax.dynamic_slice_in_dim(head_copy, core * half_vocab, half_vocab, 1), pairs, size)
    )
    head_other = core_swap(head_mine, experts)

    square = (row_count, width)
    lanes = (row_count, LANES)
    cols, place_one, across_one, place_two, across_two = call(
        functools.partial(routing_kernel, capacity),
        "routing",
        "vv",
        (jnp.swapaxes(routes, 1, 2), alignment[None, :]),
        [shaped(lanes, F32)]
        + [shaped((slot_count, row_count), BF), shaped((row_count, slot_count), BF)] * 2,
        "vvvvv",
    )
    features_across = features.T

    def front(feat_ref, extra_ref, place_ref, *outs):
        front_kernel(experts, feat_ref, extra_ref, place_ref, gain_at, *outs)

    x0, slots_one, prob_one, lines = call(
        front,
        "front",
        "vvv",
        (features_across, extra, place_one),
        [shaped(square, F32), shaped((slot_count, width), BF), shaped(lanes, F32), shaped((LANES, width), F32)],
        "vvvv",
        flops=1e9,
        moved=4e6,
    )
    expert_scratch = [pltpu.VMEM((2, width, units), BF), pltpu.SemaphoreType.DMA((size,))]
    tile = 512

    def expert_forward(slots, chunks):
        return call(
            functools.partial(expert_forward_kernel, size, tile),
            "expert_forward",
            "sv" + "a" * size,
            (ranks, slots, *chunks),
            [shaped(slots.shape, BF)],
            "v",
            expert_scratch,
            flops=4.0 * slot_count * width * units,
            moved=6e6,
        )[0]

    received_one = swap_rows(slots_one, experts)
    returned_one = swap_rows(expert_forward(received_one, first_chunks), experts)
    copy_sems = pltpu.SemaphoreType.DMA((2 * size,))
    middle_dims = (experts, size, shard, tap_at, taps_count, gain_at)
    h1, h2, h3, logs, prob_two, slots_two = call(
        functools.partial(middle_forward_kernel, middle_dims),
        "middle_forward",
        "ssvvvvvvvvaa",
        (
            ranks,
            lengths,
            x0,
            prob_one,
            cols,
            across_one,
            returned_one,
            place_two,
            extra,
            lines,
            shared_mine,
            shared_other,
        ),
        [shaped(square, F32)] * 3
        + [shaped(lanes, F32), shaped(lanes, F32), shaped((slot_count, width), BF)],
        "vvvvvv",
        [
            pltpu.VMEM((width, 7 * width), BF),
            pltpu.VMEM((row_count, 3 * width), BF),
            pltpu.VMEM(square, BF),
            pltpu.VMEM((row_count + 2 * TAP_PAD, width), F32),
            copy_sems,
        ],
        flops=12e9,
        moved=10e6,
    )
    received_two = swap_rows(slots_two, experts)
    returned_two = swap_rows(expert_forward(received_two, second_chunks), experts)
    two_grad, logit_two, grad_slots_two, gain_four, loss_part, head_grad_mine, head_grad_other = call(
        functools.partial(head_kernel, (experts, size, shard, gain_at, 1024)),
        "head",
        "sssvvvvvvvaa",
        (
            ranks,
            lengths,
            frame_count.reshape(1, 1),
            h3,
            prob_two,
            cols,
            across_two,
            returned_two,
            place_two,
            lines,
            head_mine,
            head_other,
        ),
        [
            shaped(square, F32),
            shaped(lanes, BF),
            shaped((slot_count, width), BF),
            shaped((8, width), F32),
            shaped((8, LANES), F32),
            shaped((size, shard, half_vocab), BF),
            shaped((size, shard, half_vocab), BF),
        ],
        "vvvvvaa",
        [
            pltpu.VMEM((width, vocab), BF),
            pltpu.VMEM((row_count, vocab), F32),
            pltpu.VMEM((width, vocab), BF),
            copy_sems,
        ],
        flops=20e9,
        moved=20e6,
    )

    def expert_backward(slots, grads, chunks):
        back, active, hidden = call(
            functools.partial(expert_backward_kernel, size, tile),
            "expert_backward",
            "svv" + "a" * size,
            (ranks, slots, grads, *chunks),
            [shaped(slots.shape, BF), shaped((slot_count, units), BF), shaped((slot_count, units), BF)],
            "vvv",
            expert_scratch,
            flops=6.0 * slot_count * width * units,
            moved=12e6,
        )
        sums = call(
            functools.partial(expert_grads_kernel, size, tile),
            "expert_grads",
            "svvvv",
            (ranks, slots, grads, active, hidden),
            [shaped((2, shard, units), BF)] * size,
            "a" * size,
            expert_scratch,
            flops=4.0 * slot_count * width * units,
            moved=10e6,
        )
        return back, sums

    out_grad_two = swap_rows(grad_slots_two, experts)
    back_two, sums_two = expert_backward(received_two, out_grad_two, second_chunks)
    slot_grad_two = swap_rows(back_two, experts)
    one_grad, logit_one, grad_slots_one, small, router_two, mid_grad_mine, mid_grad_other = call(
        functools.partial(middle_backward_kernel, middle_dims),
        "middle_backward",
        "ss" + "v" * 15 + "aa",
        (
            ranks,
            lengths,
            two_grad,
            slot_grad_two,
            across_two,
            logit_two,
            h1,
            h2,
            h3,
            logs,
            prob_one,
            cols,
            across_one,
            returned_one,
            place_one,
            extra,
            lines,
            shared_mine,
            shared_other,
        ),
        [
            shaped(square, F32),
            shaped(lanes, BF),
            shaped((slot_count, width), BF),
            shaped((24, width), F32),
            shaped((LANES, width), F32),
            shaped((size, shard, half_shared), BF),
            shaped((size, shard, half_shared), BF),
        ],
        "vvvvvaa",
        [
            pltpu.VMEM((width, 7 * width), BF),
            pltpu.VMEM((row_count, 3 * width), BF),
            pltpu.VMEM((row_count, 3 * width), BF),
            pltpu.VMEM(square, BF),
            pltpu.VMEM((row_count + 2 * TAP_PAD, width), F32),
            pltpu.VMEM((row_count + 2 * TAP_PAD, width), F32),
            pltpu.VMEM((width, 7 * width), BF),
            copy_sems,
        ],
        flops=25e9,
        moved=20e6,
    )
    out_grad_one = swap_rows(grad_slots_one, experts)
    back_one, sums_one = expert_backward(received_one, out_grad_one, first_chunks)
    slot_grad_one = swap_rows(back_one, experts)
    (extra_grad,) = call(
        functools.partial(back_kernel, (experts, tap_at, taps_count, gain_at)),
        "back",
        "v" * 11,
        (
            one_grad,
            slot_grad_one,
            across_one,
            logit_one,
            x0,
            features_across,
            extra,
            lines,
            small,
            router_two,
            gain_four,
        ),
        [shaped((width, LANES), BF)],
        "v",
        [pltpu.VMEM((LANES, width), F32)],
        flops=2e9,
        moved=5e6,
    )

    head_sum = shared_scatter(head_grad_mine, head_grad_other, pairs, size, experts, core).astype(F32)
    sums_two = expert_scatter(sums_two, pairs)
    mid_sum = shared_scatter(mid_grad_mine, mid_grad_other, pairs, size, experts, core).astype(F32)
    sums_one = expert_scatter(sums_one, pairs)
    spread = jnp.broadcast_to(
        extra_grad.reshape(size, 1, shard, LANES), (size, experts, shard, LANES)
    ).reshape(everyone, shard, LANES)
    small_sum = jnp.sum(
        lax.all_to_all(spread, ALL, split_axis=0, concat_axis=0, tiled=True).astype(F32), axis=0
    )
    extra_sum = small_sum[:, :aux]
    gains_sum = small_sum[:, aux : aux + gains_copy.shape[0]].T
    attend_sum = mid_sum[:, : 3 * width]
    output_sum = mid_sum[:, 3 * width : 4 * width]
    conv_sum = mid_sum[:, 4 * width :]
    up_sum = jnp.stack([sums_one[0], sums_two[0]])[:, None].astype(F32)
    down_sum = jnp.stack([sums_one[1], sums_two[1]])[:, None].astype(F32)
    shared_squares = jnp.float32(0.0)
    for member in (mid_sum, head_sum, extra_sum, gains_sum):
        shared_squares = shared_squares + jnp.sum(member * member)
    expert_squares = jnp.sum(up_sum * up_sum) + jnp.sum(down_sum * down_sum)
    local_squares = jnp.where(expert_at == 0, shared_squares, 0.0) + expert_squares
    totals = jnp.stack([local_squares, loss_part[0, 0]])
    totals = jnp.sum(
        lax.all_to_all(
            jnp.broadcast_to(totals[None, :, None], (everyone, 2, LANES)),
            ALL,
            split_axis=0,
            concat_axis=0,
            tiled=True,
        )[:, :, 0],
        axis=0,
    )
    global_norm = jnp.sqrt(totals[0])
    loss_sum = totals[1]
    factor = jnp.minimum(1.0, 0.1 * math.sqrt(width / (row_count * everyone)) / global_norm)
    gradients = (attend_sum, output_sum, conv_sum, head_sum, extra_sum, gains_sum, up_sum, down_sum)
    turned = lambda arrays: arrays[:7] + (jnp.swapaxes(arrays[7], 2, 3),)
    results = [
        adamw(gradient * factor, master, moment, second, rate, decay)
        for gradient, master, moment, second, rate, decay in zip(
            gradients, turned(masters), turned(firsts), turned(seconds), STEP_RATES, DECAYS
        )
    ]
    results[7] = tuple(jnp.swapaxes(member, 2, 3) for member in results[7])
    return (
        loss_sum,
        frame_count,
        global_norm,
        *(result[0] for result in results),
        *(result[1] for result in results),
        *(result[2] for result in results),
    )


def solution(mesh):
    weight_specs = (
        P("dp", None),
        P("dp", None),
        P("dp", None),
        P("dp", None),
        P("dp", None),
        P(None, "dp"),
        P(None, "expert", "dp", None),
        P(None, "expert", None, "dp"),
    )
    return jax.shard_map(
        on_device,
        mesh=mesh,
        in_specs=(
            P(("dp", "expert"), None),
            P(("dp", "expert"), None),
            P(None, ("dp", "expert"), None),
            P(("dp", "expert")),
        )
        + weight_specs * 4,
        out_specs=(P(), P(), P()) + weight_specs * 3,
        check_vma=False,
    )
```

time: 1430 us -> 588 us (0.41)
  waiting for transfers between devices: 840 us -> 177 us
  blocking collectives: 200 us -> 14.5 us
  Pallas kernels: 0 us -> 146 us
  matrix products: 124 us -> 0 us
  starting transfers between devices: 27.3 us -> 139 us
  local copies, waits for them, and re-layouts: 96.1 us -> 29.9 us
  other arithmetic: 107 us -> 63.9 us
  between operations: 25.7 us -> 8.19 us
    reduce_scatter x6 -> x0, waiting for transfers between devices: 494 us -> none  [the longest x1 152 us: on_device(): lax.psum_scatter(head_grad.astype(jnp.bfloat16), 'dp', scatter_dimension=...]
    unnamed x16 -> x0, waiting for transfers between devices: 162 us -> none
    pallas_call x0 -> x12, Pallas kernels: none -> 146 us  [call(): pl.pallas_call(kernel, name=name, out_shape=tuple(outs), in_specs=[spec(k...]
    dot_general x42 -> x0, matrix products: 124 us -> none  [the longest x8 22.8 us: inner_last(): lax.dot_general(left_side, right_side, (((1,), (1,)), ((), ())), preferre...]
    ppermute x0 -> x64, waiting for transfers between devices: none -> 119 us  [the longest x56 110 us: ring_step(): return lax.ppermute(array, ALL, pairs)]
    all_gather x5 -> x0, waiting for transfers between devices: 105 us -> none  [the longest x1 59.1 us: on_device(): lax.all_gather(down_copy, 'dp', axis=3, tiled=True)]
    ppermute x0 -> x64, starting transfers between devices: none -> 96.3 us  [the longest x56 94.2 us: ring_step(): return lax.ppermute(array, ALL, pairs)]
    all_gather x3 -> x0, blocking collectives: 94.3 us -> none  [the longest x1 34.7 us: on_device(): lax.all_gather(output_copy, 'dp', axis=0, tiled=True)]
  transfers between devices with their start and end apart: 21 -> 75, of which waited for: 17 -> 34; matrix products, arithmetic and copies ran while one was open for 11% -> 11% of each run, Pallas kernels for 0% -> 18%
where the time goes in v1:
time: 588 us; the launch traced here: 579 us
  waiting for transfers between devices  177 us (30%)
  Pallas kernels  146 us (25%)
  starting transfers between devices  139 us (24%)
  other arithmetic  63.9 us (11%)
  local copies, waits for them, and re-layouts  29.9 us (5%)
  blocking collectives  14.5 us (2%)
  between operations  8.19 us (1%)
    pallas_call x12, Pallas kernels, call(): pl.pallas_call(kernel, name=name, out_shape=tuple(outs), in_specs=[spec(k...  146 us
    ppermute x56, waiting for transfers between devices, ring_step(): return lax.ppermute(array, ALL, pairs)  110 us
    ppermute x56, starting transfers between devices, ring_step(): return lax.ppermute(array, ALL, pairs)  94.2 us
    all_to_all x7, waiting for transfers between devices, swap_rows(): lax.all_to_all(parts, 'expert', split_axis=0, concat_axis=0, tiled=True)  49.1 us
    all_to_all x7, starting transfers between devices, swap_rows(): lax.all_to_all(parts, 'expert', split_axis=0, concat_axis=0, tiled=True)  24.6 us
    add x14, other arithmetic, shared_scatter(): partial = ring_step(partial, pairs) + (mine[k] + arrived[k])  22.7 us
    unnamed x134, local copies, waits for them, and re-layouts  18.6 us
    add x14, other arithmetic, expert_scatter(): partial = ring_step(partial, pairs) + chunk  16.5 us
  transfers between devices with their start and end apart: 75, of which 34 were waited for; matrix products, arithmetic and copies ran while one was open for 11% of the time, Pallas kernels for 18%

profile of v1, /device:TPU:0, one launch (start us, length us, event | category | flops | bytes accessed | tf_op | source)
XLA Modules:
  0.0 579.1 jit_solution(10564422407533617967)
XLA Ops:
  12.7 8.6 %collective-permute-done.7 = bf16[64,1792]{1,0:T(8,128)(2,1)S(1)} collective-permute-done((bf16[64,1792]{1,0:T(8,128)(2,1)S(1)}, bf16[64,1792]{1,0:T(8,128)(2,1)S(1)}, u32[]{:S(2)}, u32[]{:S(2)}) %collective-permute-start.7) | collective-permute-done | bytes 229408 | tf_op jit(solution)/shard_map/ppermute | solution.py:677
  38.9 16.2 %collective-permute-done.10 = bf16[64,1792]{1,0:T(8,128)(2,1)S(1)} collective-permute-done((bf16[64,1792]{1,0:T(8,128)(2,1)S(1)}, bf16[64,1792]{1,0:T(8,128)(2,1)S(1)}, u32[]{:S(2)}, u32[]{:S(2)}) %collective-permute-start.10) | collective-permute-done | bytes 229408 | tf_op jit(solution)/shard_map/ppermute | solution.py:677
  64.2 16.2 %collective-permute-done.12 = bf16[64,1792]{1,0:T(8,128)(2,1)S(1)} collective-permute-done((bf16[64,1792]{1,0:T(8,128)(2,1)S(1)}, bf16[64,1792]{1,0:T(8,128)(2,1)S(1)}, u32[]{:S(2)}, u32[]{:S(2)}) %collective-permute-start.12) | collective-permute-done | bytes 229408 | tf_op jit(solution)/shard_map/ppermute | solution.py:677
  93.8 9.5 %collective-permute-done.25 = bf16[64,4096]{1,0:T(8,128)(2,1)S(1)} collective-permute-done((bf16[64,4096]{1,0:T(8,128)(2,1)S(1)}, bf16[64,4096]{1,0:T(8,128)(2,1)S(1)}, u32[]{:S(2)}, u32[]{:S(2)}) %collective-permute-start.25) | collective-permute-done | bytes 524320 | tf_op jit(solution)/shard_map/ppermute | solution.py:677
  117.1 8.7 %collective-permute-done.27 = bf16[64,4096]{1,0:T(8,128)(2,1)S(1)} collective-permute-done((bf16[64,4096]{1,0:T(8,128)(2,1)S(1)}, bf16[64,4096]{1,0:T(8,128)(2,1)S(1)}, u32[]{:S(2)}, u32[]{:S(2)}) %collective-permute-start.27) | collective-permute-done | bytes 524320 | tf_op jit(solution)/shard_map/ppermute | solution.py:677
  128.3 6.6 %collective-permute-done.28 = bf16[64,4096]{1,0:T(8,128)(2,1)S(1)} collective-permute-done((bf16[64,4096]{1,0:T(8,128)(2,1)S(1)}, bf16[64,4096]{1,0:T(8,128)(2,1)S(1)}, u32[]{:S(2)}, u32[]{:S(2)}) %collective-permute-start.28) | collective-permute-done | bytes 524320 | tf_op jit(solution)/shard_map/ppermute | solution.py:677
  159.6 8.5 %all-to-all-done.2 = bf16[4,160,512]{2,1,0:T(8,128)(2,1)S(1)} async-done(((bf16[4,160,512]{2,1,0:T(8,128)(2,1)}), bf16[4,160,512]{2,1,0:T(8,128)(2,1)S(1)}, u32[]{:S(2)}, u32[]{:S(2)}) %all-to-all-start.2) | async-done | bytes 655392 | tf_op jit(solution)/shard_map/all_to_all | solution.py:704
  169.2 7.0 %expert_forward.2 = bf16[640,512]{1,0:T(8,128)(2,1)} custom-call(s32[3,8]{1,0:T(4,128)} %add_add_fusion.ranks_ref, bf16[640,512]{1,0:T(8,128)(2,1)} %bitcast.184, bf16[2,64,2048]{2,1,0:T(8,128)(2,1)} %copy-done.27, bf16[2,64,2048]{2,1,0:T(8,128)(2,1)} %copy-done.48, bf16[2,64,2048]{2,1,0:T(8,128)(2,1)} %copy-done.49, bf16[2,64,2048]{2,1,0:T(8,128)(2,1)} %copy-done.50, ...), custom_call_target="tpu_custom_call" | custom-call | flops 2684354560 | bytes 6000000 | tf_op jit(solution)/shard_map/expert_forward/pallas_call | solution.py:638
  180.5 9.5 %all-to-all-done.3 = bf16[4,160,512]{2,1,0:T(8,128)(2,1)S(1)} async-done(((bf16[4,160,512]{2,1,0:T(8,128)(2,1)}), bf16[4,160,512]{2,1,0:T(8,128)(2,1)S(1)}, u32[]{:S(2)}, u32[]{:S(2)}) %all-to-all-start.3) | async-done | bytes 655392 | tf_op jit(solution)/shard_map/all_to_all | solution.py:704
  190.8 15.5 %middle_forward.1 = (f32[512,512]{1,0:T(8,128)}, f32[512,512]{1,0:T(8,128)}, f32[512,512]{1,0:T(8,128)}, f32[512,128]{1,0:T(8,128)}, f32[512,128]{1,0:T(8,128)}, /*index=5*/bf16[640,512]{1,0:T(8,128)(2,1)}) custom-call(s32[3,8]{1,0:T(4,128)} %add_add_fusion.ranks_ref, s32[1,4]{1,0:T(1,128)} %lengths_ref.5, f32[512,512]{1,0:T(8,128)} %get-tuple-element.79.x0_ref, ...), custom_call_target="tpu_custom_call" | custom-call | flops 12000000000 | bytes 10000000 | tf_op jit(solution)/shard_map/middle_forward/pallas_call | solution.py:638
  211.1 9.0 %all-to-all-done.4 = bf16[4,160,512]{2,1,0:T(8,128)(2,1)S(1)} async-done(((bf16[4,160,512]{2,1,0:T(8,128)(2,1)}), bf16[4,160,512]{2,1,0:T(8,128)(2,1)S(1)}, u32[]{:S(2)}, u32[]{:S(2)}) %all-to-all-start.4) | async-done | bytes 655392 | tf_op jit(solution)/shard_map/all_to_all | solution.py:704
  224.3 7.0 %expert_forward.3 = bf16[640,512]{1,0:T(8,128)(2,1)} custom-call(s32[3,8]{1,0:T(4,128)} %add_add_fusion.ranks_ref, bf16[640,512]{1,0:T(8,128)(2,1)} %bitcast.189, bf16[2,64,2048]{2,1,0:T(8,128)(2,1)} %copy-done.28, bf16[2,64,2048]{2,1,0:T(8,128)(2,1)} %collective-permute-done.15.refs_1_, bf16[2,64,2048]{2,1,0:T(8,128)(2,1)} %copy-done.52, ...), custom_call_target="tpu_custom_call" | custom-call | flops 2684354560 | bytes 6000000 | tf_op jit(solution)/shard_map/expert_forward/pallas_call | solution.py:638
  235.5 9.6 %all-to-all-done.5 = bf16[4,160,512]{2,1,0:T(8,128)(2,1)S(1)} async-done(((bf16[4,160,512]{2,1,0:T(8,128)(2,1)}), bf16[4,160,512]{2,1,0:T(8,128)(2,1)S(1)}, u32[]{:S(2)}, u32[]{:S(2)}) %all-to-all-start.5) | async-done | bytes 655392 | tf_op jit(solution)/shard_map/all_to_all | solution.py:704
  245.9 34.4 %head.1 = (f32[512,512]{1,0:T(8,128)}, bf16[512,128]{1,0:T(8,128)(2,1)}, bf16[640,512]{1,0:T(8,128)(2,1)}, f32[8,512]{1,0:T(8,128)}, f32[8,128]{1,0:T(8,128)}, /...) custom-call(s32[3,8]{1,0:T(4,128)} %add_add_fusion.ranks_ref, s32[1,4]{1,0:T(1,128)} %lengths_ref.5, ...), custom_call_target="tpu_custom_call" | custom-call | flops 20000000000 | bytes 20000000 | tf_op jit(solution)/shard_map/head/pallas_call | solution.py:638
  280.4 14.5 %all_to_all.60 = bf16[4,160,512]{2,1,0:T(8,128)(2,1)} all-to-all(bf16[4,160,512]{2,1,0:T(8,128)(2,1)} %bitcast.203), channel_id=1, replica_groups=mesh['dp'=8,'expert'=4] {'expert'}, dimensions={0} | all-to-all | bytes 1310720 | tf_op jit(solution)/shard_map/all_to_all | solution.py:704
  294.9 10.5 %expert_backward.2 = (bf16[640,512]{1,0:T(8,128)(2,1)}, bf16[640,2048]{1,0:T(8,128)(2,1)}, bf16[640,2048]{1,0:T(8,128)(2,1)}) custom-call(s32[3,8]{1,0:T(4,128)} %add_add_fusion.ranks_ref, bf16[640,512]{1,0:T(8,128)(2,1)} %bitcast.190, bf16[640,512]{1,0:T(8,128)(2,1)} %bitcast.193, bf16[2,64,2048]{2,1,0:T(8,128)(2,1)} %copy-done.28, ...), custom_call_target="tpu_custom_call" | custom-call | flops 4026531840 | bytes 12000000 | tf_op jit(solution)/shard_map/expert_backward/pallas_call | solution.py:638
  309.6 9.5 %all-to-all-done.7 = bf16[4,160,512]{2,1,0:T(8,128)(2,1)S(1)} async-done(((bf16[4,160,512]{2,1,0:T(8,128)(2,1)}), bf16[4,160,512]{2,1,0:T(8,128)(2,1)S(1)}, u32[]{:S(2)}, u32[]{:S(2)}) %all-to-all-start.7) | async-done | bytes 655392 | tf_op jit(solution)/shard_map/all_to_all | solution.py:704
  320.0 33.8 %middle_backward.1 = (f32[512,512]{1,0:T(8,128)}, bf16[512,128]{1,0:T(8,128)(2,1)}, bf16[640,512]{1,0:T(8,128)(2,1)}, f32[24,512]{1,0:T(8,128)}, f32[128,512]{1,...) custom-call(s32[3,8]{1,0:T(4,128)} %add_add_fusion.ranks_ref, s32[1,4]{1,0:T(1,128)} %lengths_ref.5, ...), custom_call_target="tpu_custom_call" | custom-call | flops 24999999488 | bytes 20000000 | tf_op jit(solution)/shard_map/middle_backward/pallas_call | solution.py:638
  353.9 8.5 %expert_grads.3 = (bf16[2,64,2048]{2,1,0:T(8,128)(2,1)}, bf16[2,64,2048]{2,1,0:T(8,128)(2,1)}, bf16[2,64,2048]{2,1,0:T(8,128)(2,1)}, bf16[2,64,2048]{2,1,0:T(8,1...) custom-call(s32[3,8]{1,0:T(4,128)} %add_add_fusion.ranks_ref, ...), custom_call_target="tpu_custom_call" | custom-call | flops 2684354560 | bytes 10000000 | tf_op jit(solution)/shard_map/expert_grads/pallas_call | solution.py:638
  378.8 10.7 %expert_backward.3 = (bf16[640,512]{1,0:T(8,128)(2,1)}, bf16[640,2048]{1,0:T(8,128)(2,1)}, bf16[640,2048]{1,0:T(8,128)(2,1)}) custom-call(s32[3,8]{1,0:T(4,128)} %add_add_fusion.ranks_ref, bf16[640,512]{1,0:T(8,128)(2,1)} %bitcast.185, bf16[640,512]{1,0:T(8,128)(2,1)} %bitcast.196, bf16[2,64,2048]{2,1,0:T(8,128)(2,1)} %copy-done.27, ...), custom_call_target="tpu_custom_call" | custom-call | flops 4026531840 | bytes 12000000 | tf_op jit(solution)/shard_map/expert_backward/pallas_call | solution.py:638
  395.1 8.5 %expert_grads.2 = (bf16[2,64,2048]{2,1,0:T(8,128)(2,1)}, bf16[2,64,2048]{2,1,0:T(8,128)(2,1)}, bf16[2,64,2048]{2,1,0:T(8,128)(2,1)}, bf16[2,64,2048]{2,1,0:T(8,1...) custom-call(s32[3,8]{1,0:T(4,128)} %add_add_fusion.ranks_ref, ...), custom_call_target="tpu_custom_call" | custom-call | flops 2684354560 | bytes 10000000 | tf_op jit(solution)/shard_map/expert_grads/pallas_call | solution.py:638
  511.5 7.9 %collective-permute-done.37 = bf16[64,1792]{1,0:T(8,128)(2,1)S(1)} collective-permute-done((bf16[64,1792]{1,0:T(8,128)(2,1)S(1)}, bf16[64,1792]{1,0:T(8,128)(2,1)S(1)}, u32[]{:S(2)}, u32[]{:S(2)}) %collective-permute-start.37) | collective-permute-done | bytes 229408 | tf_op jit(solution)/shard_map/ppermute | solution.py:677
  531.2 7.2 %collective-permute-done.48 = bf16[64,4096]{1,0:T(8,128)(2,1)S(1)} collective-permute-done((bf16[64,4096]{1,0:T(8,128)(2,1)S(1)}, bf16[64,4096]{1,0:T(8,128)(2,1)S(1)}, u32[]{:S(2)}, u32[]{:S(2)}) %collective-permute-start.48) | collective-permute-done | bytes 524320 | tf_op jit(solution)/shard_map/ppermute | solution.py:695
  552.7 7.1 %all-to-all-done.11 = f32[32,2,128]{2,1,0:T(2,128)S(1)} async-done(((f32[32,2,128]{2,1,0:T(2,128)}), f32[32,2,128]{2,1,0:T(2,128)S(1)}, u32[]{:S(2)}, u32[]{:S(2)}) %all-to-all-start.11) | async-done | bytes 32800 | tf_op jit(solution)/shard_map/all_to_all | solution.py:1037
  (346 shorter events, 286.2 us)
Async XLA Ops:
  3.1 29.1 %collective-permute-start = (bf16[2,64,2048]{2,1,0:T(8,128)(2,1)S(1)}, bf16[2,64,2048]{2,1,0:T(8,128)(2,1)S(1)}, u32[]{:S(2)}, u32[]{:S(2)}) collective-permute-start(bf16[2,64,2048]{2,1,0:T(8,128)(2,1)S(1)} %pad_maximum_fusion.refs_0_), channel_id=1, source_target_pairs={{0,8},{1,5},{2,10},{3,7},{8,16},{9,1},{10,18},{11,3},{16,24},{17,9... | collective-permute-start | bytes 1572872 | tf_op jit(solution)/shard_map/ppermute | solution.py:677
  6.2 27.6 %collective-permute-start.15 = (bf16[2,64,2048]{2,1,0:T(8,128)(2,1)S(1)}, bf16[2,64,2048]{2,1,0:T(8,128)(2,1)}, u32[]{:S(2)}, u32[]{:S(2)}) collective-permute-start(bf16[2,64,2048]{2,1,0:T(8,128)(2,1)S(1)} %pad_maximum_fusion.1.refs_0_), channel_id=1, source_target_pairs={{0,8},{1,5},{2,10},{3,7},{8,16},{9,1},{10,18},{11,3},{16,24},{17,9... | collective-permute-start | bytes 1572872 | tf_op jit(solution)/shard_map/ppermute | solution.py:677
  11.2 24.2 %collective-permute-start.22 = (bf16[64,4096]{1,0:T(8,128)(2,1)S(1)}, bf16[64,4096]{1,0:T(8,128)(2,1)S(1)}, u32[]{:S(2)}, u32[]{:S(2)}) collective-permute-start(bf16[64,4096]{1,0:T(8,128)(2,1)S(1)} %get-tuple-element.232), channel_id=1, source_target_pairs={{0,8},{1,5},{2,10},{3,7},{8,16},{9,1},{10,18},{11,3},{16,24},{17,9... | collective-permute-start | bytes 1572872 | tf_op jit(solution)/shard_map/ppermute | solution.py:677
  32.2 25.3 %collective-permute-start.1 = (bf16[2,64,2048]{2,1,0:T(8,128)(2,1)S(1)}, bf16[2,64,2048]{2,1,0:T(8,128)(2,1)S(1)}, u32[]{:S(2)}, u32[]{:S(2)}) collective-permute-start(bf16[2,64,2048]{2,1,0:T(8,128)(2,1)S(1)} %collective-permute-done.refs_1_), channel_id=1, source_target_pairs={{0,8},{1,5},{2,10},{3,7},{8,16},{9,1},{10,18},{11,3},{16,24},{17,9... | collective-permute-start | bytes 1572872 | tf_op jit(solution)/shard_map/ppermute | solution.py:677
  33.8 25.3 %collective-permute-start.16 = (bf16[2,64,2048]{2,1,0:T(8,128)(2,1)}, bf16[2,64,2048]{2,1,0:T(8,128)(2,1)S(1)}, u32[]{:S(2)}, u32[]{:S(2)}) collective-permute-start(bf16[2,64,2048]{2,1,0:T(8,128)(2,1)} %collective-permute-done.15.refs_1_), channel_id=1, source_target_pairs={{0,8},{1,5},{2,10},{3,7},{8,16},{9,1},{10,18},{11,3},{16,24},{17,9... | collective-permute-start | bytes 1572872 | tf_op jit(solution)/shard_map/ppermute | solution.py:677
  35.4 25.3 %collective-permute-start.23 = (bf16[64,4096]{1,0:T(8,128)(2,1)S(1)}, bf16[64,4096]{1,0:T(8,128)(2,1)S(1)}, u32[]{:S(2)}, u32[]{:S(2)}) collective-permute-start(bf16[64,4096]{1,0:T(8,128)(2,1)S(1)} %collective-permute-done.22), channel_id=1, source_target_pairs={{0,8},{1,5},{2,10},{3,7},{8,16},{9,1},{10,18},{11,3},{16,24},{17,9... | collective-permute-start | bytes 1572872 | tf_op jit(solution)/shard_map/ppermute | solution.py:677
  57.5 25.3 %collective-permute-start.2 = (bf16[2,64,2048]{2,1,0:T(8,128)(2,1)S(1)}, bf16[2,64,2048]{2,1,0:T(8,128)(2,1)S(1)}, u32[]{:S(2)}, u32[]{:S(2)}) collective-permute-start(bf16[2,64,2048]{2,1,0:T(8,128)(2,1)S(1)} %collective-permute-done.1.refs_2_), channel_id=1, source_target_pairs={{0,8},{1,5},{2,10},{3,7},{8,16},{9,1},{10,18},{11,3},{16,24},{17,9... | collective-permute-start | bytes 1572872 | tf_op jit(solution)/shard_map/ppermute | solution.py:677
  59.1 25.3 %collective-permute-start.17 = (bf16[2,64,2048]{2,1,0:T(8,128)(2,1)S(1)}, bf16[2,64,2048]{2,1,0:T(8,128)(2,1)}, u32[]{:S(2)}, u32[]{:S(2)}) collective-permute-start(bf16[2,64,2048]{2,1,0:T(8,128)(2,1)S(1)} %collective-permute-done.16.refs_2_), channel_id=1, source_target_pairs={{0,8},{1,5},{2,10},{3,7},{8,16},{9,1},{10,18},{11,3},{16,24},{17,9... | collective-permute-start | bytes 1572872 | tf_op jit(solution)/shard_map/ppermute | solution.py:677
  60.7 25.3 %collective-permute-start.24 = (bf16[64,4096]{1,0:T(8,128)(2,1)S(1)}, bf16[64,4096]{1,0:T(8,128)(2,1)S(1)}, u32[]{:S(2)}, u32[]{:S(2)}) collective-permute-start(bf16[64,4096]{1,0:T(8,128)(2,1)S(1)} %collective-permute-done.23), channel_id=1, source_target_pairs={{0,8},{1,5},{2,10},{3,7},{8,16},{9,1},{10,18},{11,3},{16,24},{17,9... | collective-permute-start | bytes 1572872 | tf_op jit(solution)/shard_map/ppermute | solution.py:677
  84.4 61.3 %collective-permute-start.18 = (bf16[2,64,2048]{2,1,0:T(8,128)(2,1)}, bf16[2,64,2048]{2,1,0:T(8,128)(2,1)}, u32[]{:S(2)}, u32[]{:S(2)}) collective-permute-start(bf16[2,64,2048]{2,1,0:T(8,128)(2,1)} %collective-permute-done.17.refs_3_), channel_id=1, source_target_pairs={{0,8},{1,5},{2,10},{3,7},{8,16},{9,1},{10,18},{11,3},{16,24},{17,9... | collective-permute-start | bytes 1572872 | tf_op jit(solution)/shard_map/ppermute | solution.py:677
  89.1 91.4 %collective-permute-start.14 = (bf16[8,64,1792]{2,1,0:T(8,128)(2,1)}, bf16[8,64,1792]{2,1,0:T(8,128)(2,1)}, u32[]{:S(2)}, u32[]{:S(2)}) collective-permute-start(bf16[8,64,1792]{2,1,0:T(8,128)(2,1)} %bitcast_dynamic-update-slice_fusion.8.mine_ref), channel_id=1, source_target_pairs={{0,1},{1,0},{2,3},{3,2},{4,5},{5,4},{6,7},{7,6},{8,9},{9,8},{10,11... | collective-permute-start | bytes 5505032 | tf_op jit(solution)/shard_map/ppermute | solution.py:688
  108.9 38.8 %collective-permute-start.5 = (bf16[2,64,2048]{2,1,0:T(8,128)(2,1)S(1)}, bf16[2,64,2048]{2,1,0:T(8,128)(2,1)S(1)}, u32[]{:S(2)}, u32[]{:S(2)}) collective-permute-start(bf16[2,64,2048]{2,1,0:T(8,128)(2,1)S(1)} %collective-permute-done.4.refs_5_), channel_id=1, source_target_pairs={{0,8},{1,5},{2,10},{3,7},{8,16},{9,1},{10,18},{11,3},{16,24},{17,9... | collective-permute-start | bytes 1572872 | tf_op jit(solution)/shard_map/ppermute | solution.py:677
  135.8 109.3 %collective-permute-start.29 = (bf16[8,64,4096]{2,1,0:T(8,128)(2,1)}, bf16[8,64,4096]{2,1,0:T(8,128)(2,1)}, u32[]{:S(2)}, u32[]{:S(2)}) collective-permute-start(bf16[8,64,4096]{2,1,0:T(8,128)(2,1)} %bitcast_dynamic-update-slice_fusion.mine_ref), channel_id=1, source_target_pairs={{0,1},{1,0},{2,3},{3,2},{4,5},{5,4},{6,7},{7,6},{8,9},{9,8},{10,11... | collective-permute-start | bytes 12582920 | tf_op jit(solution)/shard_map/ppermute | solution.py:688
  179.7 43.8 %collective-permute-start.21 = (bf16[2,64,2048]{2,1,0:T(8,128)(2,1)S(1)}, bf16[2,64,2048]{2,1,0:T(8,128)(2,1)S(1)}, u32[]{:S(2)}, u32[]{:S(2)}) collective-permute-start(bf16[2,64,2048]{2,1,0:T(8,128)(2,1)S(1)} %collective-permute-done.20.refs_6_), channel_id=1, source_target_pairs={{0,8},{1,5},{2,10},{3,7},{8,16},{9,1},{10,18},{11,3},{16,24},{17,9... | collective-permute-start | bytes 1572872 | tf_op jit(solution)/shard_map/ppermute | solution.py:677
  309.1 82.9 %collective-permute-start.40 = (bf16[8,64,4096]{2,1,0:T(8,128)(2,1)}, bf16[8,64,4096]{2,1,0:T(8,128)(2,1)}, u32[]{:S(2)}, u32[]{:S(2)}) collective-permute-start(bf16[8,64,4096]{2,1,0:T(8,128)(2,1)} %get-tuple-element.100), channel_id=1, source_target_pairs={{0,1},{1,0},{2,3},{3,2},{4,5},{5,4},{6,7},{7,6},{8,9},{9,8},{10,11... | collective-permute-start | bytes 12582920 | tf_op jit(solution)/shard_map/ppermute | solution.py:688
  353.8 35.7 %collective-permute-start.30 = (bf16[8,64,1792]{2,1,0:T(8,128)(2,1)}, bf16[8,64,1792]{2,1,0:T(8,128)(2,1)}, u32[]{:S(2)}, u32[]{:S(2)}) collective-permute-start(bf16[8,64,1792]{2,1,0:T(8,128)(2,1)} %get-tuple-element.98), channel_id=1, source_target_pairs={{0,1},{1,0},{2,3},{3,2},{4,5},{5,4},{6,7},{7,6},{8,9},{9,8},{10,11... | collective-permute-start | bytes 5505032 | tf_op jit(solution)/shard_map/ppermute | solution.py:688
  373.0 35.5 %collective-permute-start.58 = (bf16[2,64,2048]{2,1,0:T(8,128)(2,1)S(1)}, bf16[2,64,2048]{2,1,0:T(8,128)(2,1)S(1)}, u32[]{:S(2)}, u32[]{:S(2)}) collective-permute-start(bf16[2,64,2048]{2,1,0:T(8,128)(2,1)S(1)} %add.400), channel_id=1, source_target_pairs={{0,8},{1,5},{2,10},{3,7},{8,16},{9,1},{10,18},{11,3},{16,24},{17,9... | collective-permute-start | bytes 1572872 | tf_op jit(solution)/shard_map/ppermute | solution.py:677
  431.3 22.4 %collective-permute-start.60 = (bf16[2,64,2048]{2,1,0:T(8,128)(2,1)}, bf16[2,64,2048]{2,1,0:T(8,128)(2,1)}, u32[]{:S(2)}, u32[]{:S(2)}) collective-permute-start(bf16[2,64,2048]{2,1,0:T(8,128)(2,1)} %add.402), channel_id=1, source_target_pairs={{0,8},{1,5},{2,10},{3,7},{8,16},{9,1},{10,18},{11,3},{16,24},{17,9... | collective-permute-start | bytes 1572872 | tf_op jit(solution)/shard_map/ppermute | solution.py:677
  434.4 23.0 %collective-permute-start.52 = (bf16[2,64,2048]{2,1,0:T(8,128)(2,1)}, bf16[2,64,2048]{2,1,0:T(8,128)(2,1)}, u32[]{:S(2)}, u32[]{:S(2)}) collective-permute-start(bf16[2,64,2048]{2,1,0:T(8,128)(2,1)} %add.394), channel_id=1, source_target_pairs={{0,8},{1,5},{2,10},{3,7},{8,16},{9,1},{10,18},{11,3},{16,24},{17,9... | collective-permute-start | bytes 1572872 | tf_op jit(solution)/shard_map/ppermute | solution.py:677
  437.7 23.3 %collective-permute-start.34 = (bf16[64,1792]{1,0:T(8,128)(2,1)}, bf16[64,1792]{1,0:T(8,128)(2,1)}, u32[]{:S(2)}, u32[]{:S(2)}) collective-permute-start(bf16[64,1792]{1,0:T(8,128)(2,1)} %fusion.40), channel_id=1, source_target_pairs={{0,8},{1,5},{2,10},{3,7},{8,16},{9,1},{10,18},{11,3},{16,24},{17,9... | collective-permute-start | bytes 688136 | tf_op jit(solution)/shard_map/ppermute | solution.py:677
  442.7 21.5 %collective-permute-start.44 = (bf16[64,4096]{1,0:T(8,128)(2,1)}, bf16[64,4096]{1,0:T(8,128)(2,1)}, u32[]{:S(2)}, u32[]{:S(2)}) collective-permute-start(bf16[64,4096]{1,0:T(8,128)(2,1)} %fusion.19), channel_id=1, source_target_pairs={{0,8},{1,5},{2,10},{3,7},{8,16},{9,1},{10,18},{11,3},{16,24},{17,9... | collective-permute-start | bytes 1572872 | tf_op jit(solution)/shard_map/ppermute | solution.py:677
  462.7 21.1 %collective-permute-start.35 = (bf16[64,1792]{1,0:T(8,128)(2,1)}, bf16[64,1792]{1,0:T(8,128)(2,1)}, u32[]{:S(2)}, u32[]{:S(2)}) collective-permute-start(bf16[64,1792]{1,0:T(8,128)(2,1)} %fusion.38), channel_id=1, source_target_pairs={{0,8},{1,5},{2,10},{3,7},{8,16},{9,1},{10,18},{11,3},{16,24},{17,9... | collective-permute-start | bytes 688136 | tf_op jit(solution)/shard_map/ppermute | solution.py:677
  466.5 21.6 %collective-permute-start.45 = (bf16[64,4096]{1,0:T(8,128)(2,1)}, bf16[64,4096]{1,0:T(8,128)(2,1)}, u32[]{:S(2)}, u32[]{:S(2)}) collective-permute-start(bf16[64,4096]{1,0:T(8,128)(2,1)} %fusion.17), channel_id=1, source_target_pairs={{0,8},{1,5},{2,10},{3,7},{8,16},{9,1},{10,18},{11,3},{16,24},{17,9... | collective-permute-start | bytes 1572872 | tf_op jit(solution)/shard_map/ppermute | solution.py:677
  497.9 22.9 %collective-permute-start.55 = (bf16[2,64,2048]{2,1,0:T(8,128)(2,1)S(1)}, bf16[2,64,2048]{2,1,0:T(8,128)(2,1)S(1)}, u32[]{:S(2)}, u32[]{:S(2)}) collective-permute-start(bf16[2,64,2048]{2,1,0:T(8,128)(2,1)S(1)} %add.397), channel_id=1, source_target_pairs={{0,8},{1,5},{2,10},{3,7},{8,16},{9,1},{10,18},{11,3},{16,24},{17,9... | collective-permute-start | bytes 1572872 | tf_op jit(solution)/shard_map/ppermute | solution.py:677
  (111 other events, 1579.1 us)

commit v2 on v1

--- a/solution.py
+++ b/solution.py
@@ -25,6 +25,7 @@
 VMEM_BYTES = 56 * 1024 * 1024
 LANES = 128
 TAP_PAD = 16
+TAP_ROWS = 256
 
 
 def nn(left, right):
@@ -118,6 +119,13 @@
         pairs.append((full_ref.at[rows_at(ranks_ref[0, later], rows), own], mine_ref.at[k]))
         pairs.append((full_ref.at[rows_at(ranks_ref[1, later], rows), far], other_ref.at[k]))
     return pairs
+
+
+def half_pairs(mine_ref, other_ref, full_ref, core):
+    width = mine_ref.shape[-1]
+    own = pl.ds(pl.multiple_of(core * width, LANES), width)
+    partner = pl.ds(pl.multiple_of((1 - core) * width, LANES), width)
+    return [(mine_ref, full_ref.at[:, own]), (other_ref, full_ref.at[:, partner])]
 
 
 def routing_kernel(capacity, routes_ref, align_ref, cols_ref, *place_refs):
@@ -166,23 +174,28 @@
     slots_ref[...] = nn(place_ref[...], low).astype(BF)
 
 
-def load_experts(ranks_ref, chunk_refs, weight_ref, sems):
+def load_experts(tile, ranks_ref, chunk_refs, weight_ref, sems):
     rows = chunk_refs[0].shape[1]
-    pairs = [
-        (chunk, weight_ref.at[:, rows_at(ranks_ref[0, k], rows), :])
-        for k, chunk in enumerate(chunk_refs)
-    ]
-    return start_copies(pairs, sems)
+    groups = []
+    for i in range(weight_ref.shape[2] // tile):
+        columns = pl.ds(i * tile, tile)
+        pairs = [
+            (chunk.at[:, :, columns], weight_ref.at[:, rows_at(ranks_ref[0, k], rows), columns])
+            for k, chunk in enumerate(chunk_refs)
+        ]
+        groups.append(start_copies(pairs, sems.at[i]))
+    return groups
 
 
 def expert_forward_kernel(steps, tile, ranks_ref, slots_ref, *refs):
     chunk_refs = refs[:steps]
     out_ref, weight_ref, sems = refs[steps:]
-    for copy in load_experts(ranks_ref, chunk_refs, weight_ref, sems):
-        copy.wait()
+    groups = load_experts(tile, ranks_ref, chunk_refs, weight_ref, sems)
     slots = slots_ref[...]
     total = jnp.zeros(out_ref.shape, F32)
     for at in range(0, weight_ref.shape[2], tile):
+        for copy in groups[at // tile]:
+            copy.wait()
         hidden = nn(slots, weight_ref[0, :, at : at + tile])
         active = (hidden * jax.nn.sigmoid(hidden)).astype(BF)
         total = total + nt(active, weight_ref[1, :, at : at + tile])
@@ -192,13 +205,14 @@
 def expert_backward_kernel(steps, tile, ranks_ref, slots_ref, grad_ref, *refs):
     chunk_refs = refs[:steps]
     back_ref, active_ref, hidden_ref, weight_ref, sems = refs[steps:]
-    for copy in load_experts(ranks_ref, chunk_refs, weight_ref, sems):
-        copy.wait()
+    groups = load_experts(tile, ranks_ref, chunk_refs, weight_ref, sems)
     slots = slots_ref[...]
     grad = grad_ref[...]
     total = jnp.zeros(back_ref.shape, F32)
     for at in range(0, weight_ref.shape[2], tile):
         here = slice(at, at + tile)
+        for copy in groups[at // tile]:
+            copy.wait()
         hidden = nn(slots, weight_ref[0, :, here])
         gate = jax.nn.sigmoid(hidden)
         active_ref[:, here] = (hidden * gate).astype(BF)
@@ -211,12 +225,12 @@
 def expert_grads_kernel(steps, tile, ranks_ref, slots_ref, grad_ref, active_ref, hidden_ref, *refs):
     out_refs = refs[:steps]
     sum_ref, sems = refs[steps:]
-    slots = slots_ref[...]
-    grad = grad_ref[...]
+    slots = slots_ref[...].T
+    grad = grad_ref[...].T
     for at in range(0, active_ref.shape[1], tile):
         here = slice(at, at + tile)
-        sum_ref[0, :, here] = tn(slots, hidden_ref[:, here]).astype(BF)
-        sum_ref[1, :, here] = tn(grad, active_ref[:, here]).astype(BF)
+        sum_ref[0, :, here] = nn(slots, hidden_ref[:, here]).astype(BF)
+        sum_ref[1, :, here] = nn(grad, active_ref[:, here]).astype(BF)
     rows = out_refs[0].shape[1]
     pairs = [
         (sum_ref.at[:, rows_at(ranks_ref[0, (k + 1) % steps], rows), :], out)
@@ -231,16 +245,46 @@
     return (lane < LANES // 2) if pair_at == 0 else (lane >= LANES // 2)
 
 
-def conv_taps(padded_ref, masks, taps, flip):
-    rows = masks.shape[0]
+def tap_window(padded_ref, base, half_span):
+    start = base + TAP_PAD - half_span
+    return lambda j: padded_ref[start + j : start + j + TAP_ROWS, :]
+
+
+def clear_edges(padded_ref):
+    edge = jnp.zeros((TAP_PAD, padded_ref.shape[1]), F32)
+    padded_ref[:TAP_PAD, :] = edge
+    padded_ref[padded_ref.shape[0] - TAP_PAD :, :] = edge
+
+
+def conv_rows(padded_ref, masks_ref, taps, out_ref):
     count = len(taps)
-    half = count // 2
-    total = jnp.zeros((rows, padded_ref.shape[1]), F32)
-    for j in range(count):
-        shifted = padded_ref[TAP_PAD + j - half : TAP_PAD + j - half + rows, :]
-        tap = taps[count - 1 - j] if flip else taps[j]
-        total = total + shifted * masks[:, j : j + 1] * tap
-    return total
+
+    for base in range(0, masks_ref.shape[0], TAP_ROWS):
+        shifted = tap_window(padded_ref, base, count // 2)
+        masks = masks_ref[pl.ds(base, TAP_ROWS), :]
+        total = jnp.zeros((TAP_ROWS, padded_ref.shape[1]), F32)
+        for j in range(count):
+            total = total + shifted(j) * masks[:, j : j + 1] * taps[j]
+        out_ref[pl.ds(base, TAP_ROWS), :] = total
+
+
+def conv_rows_back(padded_ref, padded_grad_ref, masks_ref, taps, out_ref, sums_ref):
+    count = len(taps)
+    width = padded_ref.shape[1]
+    sums_ref[...] = jnp.zeros(sums_ref.shape, F32)
+
+    for base in range(0, masks_ref.shape[0], TAP_ROWS):
+        values = tap_window(padded_ref, base, count // 2)
+        grads = tap_window(padded_grad_ref, base, count // 2)
+        masks = masks_ref[pl.ds(base, TAP_ROWS), :]
+        here = grads(count // 2)
+        total = jnp.zeros((TAP_ROWS, width), F32)
+        for j in range(count):
+            mask = masks[:, j : j + 1]
+            total = total + grads(j) * mask * taps[count - 1 - j]
+            part = values(j) * mask * here
+            sums_ref[j] += jnp.sum(part.reshape(TAP_ROWS // 8, 8, width), axis=0)
+        out_ref[pl.ds(base, TAP_ROWS), :] = total
 
 
 def middle_forward_kernel(
@@ -263,10 +307,12 @@
     log_ref,
     prob_two_ref,
     slots_ref,
-    weight_ref,
+    mixed_ref,
     packed_ref,
     blended_ref,
+    weight_ref,
     padded_ref,
+    masks_ref,
     sems,
 ):
     experts, steps, shard, tap_at, taps_count, gain_at = dims
@@ -319,11 +365,12 @@
     low = (unit * gain(2)).astype(BF)
     first = nn(low, weight_ref[:, 4 * width : 5 * width])
     second = nn(low, weight_ref[:, 5 * width : 6 * width])
-    padded_ref[:TAP_PAD, :] = jnp.zeros((TAP_PAD, width), F32)
-    padded_ref[TAP_PAD + rows :, :] = jnp.zeros((TAP_PAD, width), F32)
+    clear_edges(padded_ref)
     padded_ref[TAP_PAD : TAP_PAD + rows, :] = first * jax.nn.sigmoid(second)
+    masks_ref[...] = tap_masks(rows, taps_count // 2, bounds)
     taps = [lines_ref[tap_at + j : tap_at + j + 1, :] for j in range(taps_count)]
-    mixed = conv_taps(padded_ref, tap_masks(rows, taps_count // 2, bounds), taps, False)
+    conv_rows(padded_ref, masks_ref, taps, mixed_ref)
+    mixed = mixed_ref[...]
     active = (mixed * jax.nn.sigmoid(mixed)).astype(BF)
     h3 = h2 + nn(active, weight_ref[:, 6 * width :])
     h3_ref[...] = h3
@@ -367,8 +414,18 @@
 ):
     experts, steps, shard, gain_at, tile = dims
     core = ranks_ref[2, 0]
+    half = weight_ref.shape[1] // 2
+    own, partner = pl.multiple_of(core * half, LANES), pl.multiple_of((1 - core) * half, LANES)
+    tiles = []
+    for ref, out_ref, at in ((mine_ref, grad_mine_ref, own), (other_ref, grad_other_ref, partner)):
+        for k in range(half // tile):
+            tiles.append((ref, out_ref, k * tile, pl.multiple_of(at + k * tile, LANES)))
     copies = start_copies(
-        shared_pairs(mine_ref, other_ref, weight_ref, ranks_ref, core, steps, shard), sems
+        [
+            (ref.at[:, pl.ds(near, tile)], weight_ref.at[:, pl.ds(at, tile)])
+            for ref, _, near, at in tiles
+        ],
+        sems,
     )
     rows, width = h3_ref.shape
     vocab = weight_ref.shape[1]
@@ -380,50 +437,36 @@
     h4 = h3_ref[...] + 0.5 * (gate * rows_chosen)
     unit, scale = norm_parts(h4)
     low = (unit * gain).astype(BF)
-    for copy in copies:
+    turned = low.T
+    top, sums = jnp.full((rows, 1), -jnp.inf, F32), jnp.zeros((rows, 1), F32)
+    for copy, (_, _, _, at) in zip(copies, tiles):
         copy.wait()
-
-    def first_pass(i, carry):
-        top, sums = carry
-        at = pl.multiple_of(i * tile, tile)
         logits = nn(low, weight_ref[:, pl.ds(at, tile)])
         logits_ref[:, pl.ds(at, tile)] = logits
         higher = jnp.maximum(top, jnp.max(logits, axis=-1, keepdims=True))
         sums = sums * jnp.exp(top - higher) + jnp.sum(jnp.exp(logits - higher), axis=-1, keepdims=True)
-        return higher, sums
-
-    top, sums = lax.fori_loop(
-        0,
-        vocab // tile,
-        first_pass,
-        (jnp.full((rows, 1), -jnp.inf, F32), jnp.zeros((rows, 1), F32)),
-    )
+        top = higher
     log_total = top + jnp.log(sums)
     _, _, counted_end = bounds_of(lengths_ref)
     counted = (lax.broadcasted_iota(jnp.int32, (rows, 1), 0) < counted_end).astype(F32)
     portion = counted / frames_ref[0, 0]
     target = cols_ref[:, 2:3].astype(jnp.int32)
 
-    def second_pass(i, carry):
-        total, picked = carry
-        at = pl.multiple_of(i * tile, tile)
+    total, picked = jnp.zeros((rows, width), F32), jnp.zeros((rows, 1), F32)
+    out_copies = []
+    for i, (_, out_ref, near, at) in enumerate(tiles):
         logits = logits_ref[:, pl.ds(at, tile)]
         hit = lax.broadcasted_iota(jnp.int32, (rows, tile), 1) == (target - at)
         picked = picked + jnp.sum(jnp.where(hit, logits, 0.0), axis=-1, keepdims=True)
         guess = jnp.exp(logits - log_total)
         low_grad = (jnp.where(hit, guess - 1.0, guess) * portion).astype(BF)
-        grad_ref[:, pl.ds(at, tile)] = tn(low, low_grad).astype(BF)
-        return total + nt(low_grad, weight_ref[:, pl.ds(at, tile)]), picked
-
-    total, picked = lax.fori_loop(
-        0,
-        vocab // tile,
-        second_pass,
-        (jnp.zeros((rows, width), F32), jnp.zeros((rows, 1), F32)),
-    )
-    out_copies = start_copies(
-        shared_out_pairs(grad_ref, grad_mine_ref, grad_other_ref, ranks_ref, core, steps, shard), sems
-    )
+        grad_ref[:, pl.ds(at, tile)] = nn(turned, low_grad).astype(BF)
+        copy = pltpu.make_async_copy(
+            grad_ref.at[:, pl.ds(at, tile)], out_ref.at[:, pl.ds(near, tile)], sems.at[i]
+        )
+        copy.start()
+        out_copies.append(copy)
+        total = total + nt(low_grad, weight_ref[:, pl.ds(at, tile)])
     loss = jnp.sum((log_total - picked) * counted, axis=0, keepdims=True)
     loss_ref[...] = jnp.broadcast_to(loss, loss_ref.shape)
     two_grad, gain_grad = norm_back(total, unit, scale, gain)
@@ -455,6 +498,9 @@
     place_ref,
     extra_ref,
     lines_ref,
+    mixed_ref,
+    packed_ref,
+    blended_ref,
     mine_ref,
     other_ref,
     one_grad_ref,
@@ -465,11 +511,12 @@
     grad_mine_ref,
     grad_other_ref,
     weight_ref,
-    packed_ref,
     packed_grad_ref,
-    blended_ref,
     padded_ref,
     padded_grad_ref,
+    masks_ref,
+    gated_ref,
+    sums_ref,
     grad_ref,
     sems,
 ):
@@ -497,28 +544,23 @@
     low = (unit * gain(2)).astype(BF)
     first = nn(low, weight_ref[:, 4 * width : 5 * width])
     gate_half = jax.nn.sigmoid(nn(low, weight_ref[:, 5 * width : 6 * width]))
-    padded_ref[:TAP_PAD, :] = jnp.zeros((TAP_PAD, width), F32)
-    padded_ref[TAP_PAD + rows :, :] = jnp.zeros((TAP_PAD, width), F32)
+    clear_edges(padded_ref)
     padded_ref[TAP_PAD : TAP_PAD + rows, :] = first * gate_half
     taps = [lines_ref[tap_at + j : tap_at + j + 1, :] for j in range(taps_count)]
-    masks = tap_masks(rows, taps_count // 2, bounds)
-    mixed = conv_taps(padded_ref, masks, taps, False)
+    masks_ref[...] = tap_masks(rows, taps_count // 2, bounds)
+    mixed = mixed_ref[...]
     gate_mixed = jax.nn.sigmoid(mixed)
     active = (mixed * gate_mixed).astype(BF)
     grad_ref[:, 6 * width :] = tn(active, upstream_low).astype(BF)
     mixed_grad = (
         nt(upstream_low, weight_ref[:, 6 * width :]) * gate_mixed * (1.0 + mixed * (1.0 - gate_mixed))
     )
-    padded_grad_ref[:TAP_PAD, :] = jnp.zeros((TAP_PAD, width), F32)
-    padded_grad_ref[TAP_PAD + rows :, :] = jnp.zeros((TAP_PAD, width), F32)
+    clear_edges(padded_grad_ref)
     padded_grad_ref[TAP_PAD : TAP_PAD + rows, :] = mixed_grad
-    half = taps_count // 2
+    conv_rows_back(padded_ref, padded_grad_ref, masks_ref, taps, gated_ref, sums_ref)
     for j in range(taps_count):
-        shifted = padded_ref[TAP_PAD + j - half : TAP_PAD + j - half + rows, :]
-        small_ref[j : j + 1, :] = jnp.sum(
-            shifted * masks[:, j : j + 1] * mixed_grad, axis=0, keepdims=True
-        )
-    gated_grad = conv_taps(padded_grad_ref, masks, taps, True)
+        small_ref[j : j + 1, :] = jnp.sum(sums_ref[j], axis=0, keepdims=True)
+    gated_grad = gated_ref[...]
     first_low = (gated_grad * gate_half).astype(BF)
     second_low = (gated_grad * first * gate_half * (1.0 - gate_half)).astype(BF)
     grad_ref[:, 4 * width : 5 * width] = tn(low, first_low).astype(BF)
@@ -532,7 +574,6 @@
     upstream_low = upstream.astype(BF)
     unit, scale_norm = norm_parts(h1_ref[...])
     low = (unit * gain(1)).astype(BF)
-    packed_ref[...] = nn(low, weight_ref[:, : 3 * width]).astype(BF)
     mixed_low = nt(upstream_low, weight_ref[:, 3 * width : 4 * width]).astype(BF)
     same = segment_of(lax.broadcasted_iota(jnp.int32, (rows, 1), 0), bounds) == segment_of(
         lax.broadcasted_iota(jnp.int32, (1, rows), 1), bounds
@@ -556,16 +597,14 @@
             centre = jnp.sum(probs * prob_grad, axis=-1, keepdims=True)
             score_grad = (probs * (prob_grad - centre)).astype(BF)
             found = (
-                nn(weights, values),
                 tn(weights, spread),
                 nn(score_grad, keys) * scale,
                 tn(score_grad, query) * scale,
             )
             held = found if part == 0 else tuple(jnp.where(mine, new, old) for new, old in zip(found, held))
-        blended_ref[:, at : at + LANES] = held[0].astype(BF)
-        packed_grad_ref[:, 2 * width + at : 2 * width + at + LANES] = held[1].astype(BF)
-        packed_grad_ref[:, at : at + LANES] = held[2].astype(BF)
-        packed_grad_ref[:, width + at : width + at + LANES] = held[3].astype(BF)
+        packed_grad_ref[:, 2 * width + at : 2 * width + at + LANES] = held[0].astype(BF)
+        packed_grad_ref[:, at : at + LANES] = held[1].astype(BF)
+        packed_grad_ref[:, width + at : width + at + LANES] = held[2].astype(BF)
     grad_ref[:, 3 * width : 4 * width] = tn(blended_ref[...], upstream_low).astype(BF)
     packed_grad = packed_grad_ref[...]
     grad_ref[:, : 3 * width] = tn(low, packed_grad).astype(BF)
@@ -673,6 +712,10 @@
     return table
 
 
+def tie(value, *others):
+    return lax.optimization_barrier((value, *others))[0]
+
+
 def ring_step(array, pairs):
     return lax.ppermute(array, ALL, pairs)
 
@@ -704,14 +747,18 @@
     return lax.all_to_all(parts, "expert", split_axis=0, concat_axis=0, tiled=True).reshape(slots.shape)
 
 
+def shared_finish(partial, experts, core):
+    own = over_chips(partial, experts).astype(BF)
+    far = core_swap(own, experts)
+    return jnp.where(core == 0, jnp.concatenate([own, far], 1), jnp.concatenate([far, own], 1))
+
+
 def shared_scatter(mine, other, pairs, size, experts, core):
     arrived = core_swap(other, experts)
     partial = (mine[0] + arrived[0]).astype(BF)
     for k in range(1, size):
         partial = ring_step(partial, pairs) + (mine[k] + arrived[k])
-    own = over_chips(partial, experts).astype(BF)
-    far = core_swap(own, experts)
-    return jnp.where(core == 0, jnp.concatenate([own, far], 1), jnp.concatenate([far, own], 1))
+    return shared_finish(partial, experts, core)
 
 
 def expert_scatter(chunks, pairs):
@@ -759,36 +806,41 @@
         ]
     )
 
+    everyone = size * experts
+    gain_count = gains_copy.shape[0]
+    frames_here = row_count - lengths[0, 3]
+    digits = jnp.stack([frames_here // 16, frames_here % 16]).astype(BF)
     pack = jnp.concatenate(
-        [extra_copy, gains_copy.T, jnp.zeros((shard, LANES - aux - gains_copy.shape[0]), BF)], axis=1
-    )
-    extra = lax.all_to_all(
+        [
+            extra_copy,
+            gains_copy.T,
+            jnp.broadcast_to(digits[None], (shard, 2)),
+            jnp.zeros((shard, LANES - aux - gain_count - 2), BF),
+        ],
+        axis=1,
+    )
+    packs = lax.all_to_all(
         jnp.broadcast_to(pack[None], (size,) + pack.shape), "dp", split_axis=0, concat_axis=0, tiled=True
-    ).reshape(width, LANES)
-    everyone = size * experts
-    frames_here = (row_count - lengths[0, 3]).astype(F32)
-    frame_count = jnp.sum(
-        lax.all_to_all(
-            jnp.broadcast_to(frames_here, (everyone, 1, LANES)), ALL, split_axis=0, concat_axis=0, tiled=True
-        )[:, 0, 0]
-    )
+    )
+    extra = packs.reshape(width, LANES)
+    tops = jnp.sum(packs[:, 0].astype(F32), axis=0)
+    frames = jnp.full((8, LANES), 16.0 * tops[gain_at + gain_count] + tops[gain_at + gain_count + 1])
+    frames = frames + core_swap(frames, experts)
+    frame_count = over_chips(frames, experts)[0, 0]
 
     expert_shards = [
         jnp.stack([up_copy[f, 0], down_copy[f, 0].T]) for f in range(2)
     ]
-    first_chunks = ring_gather(expert_shards[0], pairs, size)
     second_chunks = ring_gather(expert_shards[1], pairs, size)
     shared = jnp.concatenate([attend_copy, output_copy, conv_copy], axis=1)
     half_shared = shared.shape[1] // 2
-    shared_mine = jnp.stack(
-        ring_gather(lax.dynamic_slice_in_dim(shared, core * half_shared, half_shared, 1), pairs, size)
-    )
+    shared_chunks = ring_gather(
+        lax.dynamic_slice_in_dim(shared, core * half_shared, half_shared, 1), pairs, size
+    )
+    shared_mine = jnp.stack(shared_chunks)
     shared_other = core_swap(shared_mine, experts)
     half_vocab = vocab // 2
-    head_mine = jnp.stack(
-        ring_gather(lax.dynamic_slice_in_dim(head_copy, core * half_vocab, half_vocab, 1), pairs, size)
-    )
-    head_other = core_swap(head_mine, experts)
+    head_half = lax.dynamic_slice_in_dim(head_copy, core * half_vocab, half_vocab, 1)
 
     square = (row_count, width)
     lanes = (row_count, LANES)
@@ -816,7 +868,12 @@
         flops=1e9,
         moved=4e6,
     )
-    expert_scratch = [pltpu.VMEM((2, width, units), BF), pltpu.SemaphoreType.DMA((size,))]
+    tile = 512
+    expert_scratch = [
+        pltpu.VMEM((2, width, units), BF),
+        pltpu.SemaphoreType.DMA((units // tile, size)),
+    ]
+    grads_scratch = [pltpu.VMEM((2, width, units), BF), pltpu.SemaphoreType.DMA((size,))]
     tile = 512
 
     def expert_forward(slots, chunks):
@@ -833,10 +890,17 @@
         )[0]
 
     received_one = swap_rows(slots_one, experts)
+    waits = {1: [extra], 4: [slots_one], 6: [received_one]}
+    first_chunks = [expert_shards[0]]
+    for k in range(1, size):
+        first_chunks.append(ring_step(tie(first_chunks[-1], *waits.get(k, [])), pairs))
+    head_mine = lax.all_gather(
+        tie(head_half, first_chunks[-1], second_chunks[-1], shared_chunks[-1]), "dp", axis=0, tiled=True
+    )
     returned_one = swap_rows(expert_forward(received_one, first_chunks), experts)
     copy_sems = pltpu.SemaphoreType.DMA((2 * size,))
     middle_dims = (experts, size, shard, tap_at, taps_count, gain_at)
-    h1, h2, h3, logs, prob_two, slots_two = call(
+    h1, h2, h3, logs, prob_two, slots_two, mixed, packed, blended = call(
         functools.partial(middle_forward_kernel, middle_dims),
         "middle_forward",
         "ssvvvvvvvvaa",
@@ -855,22 +919,31 @@
             shared_other,
         ),
         [shaped(square, F32)] * 3
-        + [shaped(lanes, F32), shaped(lanes, F32), shaped((slot_count, width), BF)],
-        "vvvvvv",
+        + [
+            shaped(lanes, F32),
+            shaped(lanes, F32),
+            shaped((slot_count, width), BF),
+            shaped(square, F32),
+            shaped((row_count, 3 * width), BF),
+            shaped(square, BF),
+        ],
+        "vvvvvvvvv",
         [
             pltpu.VMEM((width, 7 * width), BF),
-            pltpu.VMEM((row_count, 3 * width), BF),
-            pltpu.VMEM(square, BF),
             pltpu.VMEM((row_count + 2 * TAP_PAD, width), F32),
+            pltpu.VMEM(lanes, F32),
             copy_sems,
         ],
         flops=12e9,
         moved=10e6,
     )
     received_two = swap_rows(slots_two, experts)
-    returned_two = swap_rows(expert_forward(received_two, second_chunks), experts)
+    expert_two = expert_forward(received_two, second_chunks)
+    returned_two = swap_rows(expert_two, experts)
+    head_mine = tie(head_mine, expert_two)
+    head_other = core_swap(head_mine, experts)
     two_grad, logit_two, grad_slots_two, gain_four, loss_part, head_grad_mine, head_grad_other = call(
-        functools.partial(head_kernel, (experts, size, shard, gain_at, 1024)),
+        functools.partial(head_kernel, (experts, size, shard, gain_at, 2048)),
         "head",
         "sssvvvvvvvaa",
         (
@@ -893,8 +966,8 @@
             shaped((slot_count, width), BF),
             shaped((8, width), F32),
             shaped((8, LANES), F32),
-            shaped((size, shard, half_vocab), BF),
-            shaped((size, shard, half_vocab), BF),
+            shaped((width, half_vocab), BF),
+            shaped((width, half_vocab), BF),
         ],
         "vvvvvaa",
         [
@@ -926,19 +999,21 @@
             (ranks, slots, grads, active, hidden),
             [shaped((2, shard, units), BF)] * size,
             "a" * size,
-            expert_scratch,
+            grads_scratch,
             flops=4.0 * slot_count * width * units,
             moved=10e6,
         )
         return back, sums
 
-    out_grad_two = swap_rows(grad_slots_two, experts)
+    head_total = head_grad_mine + core_swap(head_grad_other, experts)
+    out_grad_two = tie(swap_rows(grad_slots_two, experts), head_total)
+    head_part = lax.psum_scatter(head_total, "dp", scatter_dimension=0, tiled=True)
     back_two, sums_two = expert_backward(received_two, out_grad_two, second_chunks)
-    slot_grad_two = swap_rows(back_two, experts)
+    slot_grad_two = tie(swap_rows(back_two, experts), sums_two[0])
     one_grad, logit_one, grad_slots_one, small, router_two, mid_grad_mine, mid_grad_other = call(
         functools.partial(middle_backward_kernel, middle_dims),
         "middle_backward",
-        "ss" + "v" * 15 + "aa",
+        "ss" + "v" * 18 + "aa",
         (
             ranks,
             lengths,
@@ -957,6 +1032,9 @@
             place_one,
             extra,
             lines,
+            mixed,
+            packed,
+            blended,
             shared_mine,
             shared_other,
         ),
@@ -973,10 +1051,11 @@
         [
             pltpu.VMEM((width, 7 * width), BF),
             pltpu.VMEM((row_count, 3 * width), BF),
-            pltpu.VMEM((row_count, 3 * width), BF),
-            pltpu.VMEM(square, BF),
             pltpu.VMEM((row_count + 2 * TAP_PAD, width), F32),
             pltpu.VMEM((row_count + 2 * TAP_PAD, width), F32),
+            pltpu.VMEM(lanes, F32),
+            pltpu.VMEM(square, F32),
+            pltpu.VMEM((16, 8, width), F32),
             pltpu.VMEM((width, 7 * width), BF),
             copy_sems,
         ],
@@ -985,7 +1064,7 @@
     )
     out_grad_one = swap_rows(grad_slots_one, experts)
     back_one, sums_one = expert_backward(received_one, out_grad_one, first_chunks)
-    slot_grad_one = swap_rows(back_one, experts)
+    slot_grad_one = tie(swap_rows(back_one, experts), sums_one[0])
     (extra_grad,) = call(
         functools.partial(back_kernel, (experts, tap_at, taps_count, gain_at)),
         "back",
@@ -1010,7 +1089,7 @@
         moved=5e6,
     )
 
-    head_sum = shared_scatter(head_grad_mine, head_grad_other, pairs, size, experts, core).astype(F32)
+    head_sum = shared_finish(head_part, experts, core).astype(F32)
     sums_two = expert_scatter(sums_two, pairs)
     mid_sum = shared_scatter(mid_grad_mine, mid_grad_other, pairs, size, experts, core).astype(F32)
     sums_one = expert_scatter(sums_one, pairs)

time: 588 us -> 533 us (0.906)
  waiting for transfers between devices: 177 us -> 143 us
  starting transfers between devices: 139 us -> 122 us
  between operations: 8.19 us -> 23 us
  Pallas kernels: 146 us -> 134 us
    all_to_all x7, waiting for transfers between devices: 49.1 us -> 11.1 us  [swap_rows(): lax.all_to_all(parts, 'expert', split_axis=0, concat_axis=0, tiled=True)]
    ppermute x56 -> x42, starting transfers between devices: 94.2 us -> 73.1 us  [ring_step(): return lax.ppermute(array, ALL, pairs)]
    add x14 -> x7, other arithmetic: 22.7 us -> 8.52 us  [shared_scatter(): partial = ring_step(partial, pairs) + (mine[k] + arrived[k])]
    pallas_call x12, Pallas kernels: 146 us -> 134 us  [call(): pl.pallas_call(kernel, name=name, out_shape=tuple(outs), in_specs=[spec(k...]
    ppermute x56 -> x42, waiting for transfers between devices: 110 us -> 98.7 us  [ring_step(): return lax.ppermute(array, ALL, pairs)]
    all_gather x0 -> x1, waiting for transfers between devices: none -> 8.09 us  [on_device(): lax.all_gather(tie(head_half, first_chunks[-1], second_chunks[-1], shared...]
    add x0 -> x3, other arithmetic: none -> 7.26 us  [the longest x1 7.25 us: on_device(): head_total = head_grad_mine + core_swap(head_grad_other, experts)]
    unnamed x134 -> x107, local copies, waits for them, and re-layouts: 18.6 us -> 12.6 us
  transfers between devices with their start and end apart: 75 -> 64, of which waited for: 34 -> 29; matrix products, arithmetic and copies ran while one was open for 11% -> 11% of each run, Pallas kernels for 18% -> 19%
where the time goes in v2:
time: 533 us; the launch traced here: 525 us
  waiting for transfers between devices  143 us (27%)
  Pallas kernels  134 us (25%)
  starting transfers between devices  122 us (23%)
  other arithmetic  62.1 us (12%)
  local copies, waits for them, and re-layouts  25.5 us (5%)
  between operations  23 us (4%)
  blocking collectives  14.5 us (3%)
    pallas_call x12, Pallas kernels, call(): pl.pallas_call(kernel, name=name, out_shape=tuple(outs), in_specs=[spec(k...  134 us
    ppermute x42, waiting for transfers between devices, ring_step(): return lax.ppermute(array, ALL, pairs)  98.7 us
    ppermute x42, starting transfers between devices, ring_step(): return lax.ppermute(array, ALL, pairs)  73.1 us
    all_to_all x7, starting transfers between devices, swap_rows(): lax.all_to_all(parts, 'expert', split_axis=0, concat_axis=0, tiled=True)  25.1 us
    add x14, other arithmetic, expert_scatter(): partial = ring_step(partial, pairs) + chunk  21.3 us
    all_to_all x1, blocking collectives, swap_rows(): lax.all_to_all(parts, 'expert', split_axis=0, concat_axis=0, tiled=True)  14.5 us
    unnamed x107, local copies, waits for them, and re-layouts  12.6 us
    all_to_all x7, waiting for transfers between devices, swap_rows(): lax.all_to_all(parts, 'expert', split_axis=0, concat_axis=0, tiled=True)  11.1 us
  transfers between devices with their start and end apart: 64, of which 29 were waited for; matrix products, arithmetic and copies ran while one was open for 11% of the time, Pallas kernels for 19%

profile of v2, /device:TPU:0, one launch (start us, length us, event | category | flops | bytes accessed | tf_op | source)
XLA Modules:
  0.0 524.7 jit_solution(14571311160233983281)
XLA Ops:
  11.7 7.3 %all-to-all-start = ((bf16[8,64,128]{2,1,0:T(8,128)(2,1)}), bf16[8,64,128]{2,1,0:T(8,128)(2,1)S(1)}, u32[]{:S(2)}, u32[]{:S(2)}) async-start(bf16[8,64,128]{2,1,0:T(8,128)(2,1)} %broadcast_in_dim.42), calls=%async_computation | async-start | bytes 262144 | tf_op jit(solution)/shard_map/all_to_all | solution.py:822
  26.4 4.4 collective-permute-done.17.refs_1_
  62.9 10.1 %collective-permute-done.9 = bf16[64,1792]{1,0:T(8,128)(2,1)S(1)} collective-permute-done((bf16[64,1792]{1,0:T(8,128)(2,1)S(1)}, bf16[64,1792]{1,0:T(8,128)(2,1)S(1)}, u32[]{:S(2)}, u32[]{:S(2)}) %collective-permute-start.9) | collective-permute-done | bytes 229408 | tf_op jit(solution)/shard_map/ppermute | solution.py:720
  82.2 10.6 %collective-permute-done.11 = bf16[64,1792]{1,0:T(8,128)(2,1)S(1)} collective-permute-done((bf16[64,1792]{1,0:T(8,128)(2,1)S(1)}, bf16[64,1792]{1,0:T(8,128)(2,1)S(1)}, u32[]{:S(2)}, u32[]{:S(2)}) %collective-permute-start.11) | collective-permute-done | bytes 229408 | tf_op jit(solution)/shard_map/ppermute | solution.py:720
  100.3 12.2 %collective-permute-done.13 = bf16[64,1792]{1,0:T(8,128)(2,1)S(1)} collective-permute-done((bf16[64,1792]{1,0:T(8,128)(2,1)S(1)}, bf16[64,1792]{1,0:T(8,128)(2,1)S(1)}, u32[]{:S(2)}, u32[]{:S(2)}) %collective-permute-start.13) | collective-permute-done | bytes 229408 | tf_op jit(solution)/shard_map/ppermute | solution.py:720
  120.8 11.4 %collective-permute-done.15 = bf16[64,1792]{1,0:T(8,128)(2,1)S(1)} collective-permute-done((bf16[64,1792]{1,0:T(8,128)(2,1)S(1)}, bf16[64,1792]{1,0:T(8,128)(2,1)S(1)}, u32[]{:S(2)}, u32[]{:S(2)}) %collective-permute-start.15) | collective-permute-done | bytes 229408 | tf_op jit(solution)/shard_map/ppermute | solution.py:720
  138.7 7.1 %expert_forward.2 = bf16[640,512]{1,0:T(8,128)(2,1)} custom-call(s32[3,8]{1,0:T(4,128)} %add_add_fusion.ranks_ref, bf16[640,512]{1,0:T(8,128)(2,1)} %bitcast.141, bf16[2,64,2048]{2,1,0:T(8,128)(2,1)} %copy-done.28, bf16[2,64,2048]{2,1,0:T(8,128)(2,1)} %copy-done.47, bf16[2,64,2048]{2,1,0:T(8,128)(2,1)} %copy-done.48, ...), custom_call_target="tpu_custom_call" | custom-call | flops 2684354560 | bytes 6000000 | tf_op jit(solution)/shard_map/expert_forward/pallas_call | solution.py:677
  149.5 10.2 %all-to-all-done.2 = bf16[4,160,512]{2,1,0:T(8,128)(2,1)S(1)} async-done(((bf16[4,160,512]{2,1,0:T(8,128)(2,1)}), bf16[4,160,512]{2,1,0:T(8,128)(2,1)S(1)}, u32[]{:S(2)}, u32[]{:S(2)}) %all-to-all-start.2) | async-done | bytes 655392 | tf_op jit(solution)/shard_map/all_to_all | solution.py:747
  160.5 16.1 %middle_forward.1 = (f32[512,512]{1,0:T(8,128)}, f32[512,512]{1,0:T(8,128)}, f32[512,512]{1,0:T(8,128)}, f32[512,128]{1,0:T(8,128)}, f32[512,128]{1,0:T(8,128)},...) custom-call(s32[3,8]{1,0:T(4,128)} %add_add_fusion.ranks_ref, ...), custom_call_target="tpu_custom_call" | custom-call | flops 12000000000 | bytes 10000000 | tf_op jit(solution)/shard_map/middle_forward/pallas_call | solution.py:677
  176.7 14.5 %all_to_all.55 = bf16[4,160,512]{2,1,0:T(8,128)(2,1)} all-to-all(bf16[4,160,512]{2,1,0:T(8,128)(2,1)} %bitcast.161), channel_id=1, replica_groups=mesh['dp'=8,'expert'=4] {'expert'}, dimensions={0} | all-to-all | bytes 1310720 | tf_op jit(solution)/shard_map/all_to_all | solution.py:747
  191.2 7.0 %expert_forward.3 = bf16[640,512]{1,0:T(8,128)(2,1)} custom-call(s32[3,8]{1,0:T(4,128)} %add_add_fusion.ranks_ref, bf16[640,512]{1,0:T(8,128)(2,1)} %bitcast.146, bf16[2,64,2048]{2,1,0:T(8,128)(2,1)} %copy-done.29, bf16[2,64,2048]{2,1,0:T(8,128)(2,1)} %collective-permute-done.17.refs_1_, bf16[2,64,2048]{2,1,0:T(8,128)(2,1)} %copy-done.49, ...), custom_call_target="tpu_custom_call" | custom-call | flops 2684354560 | bytes 6000000 | tf_op jit(solution)/shard_map/expert_forward/pallas_call | solution.py:677
  198.2 8.1 %all-gather.2.cloned.1.call-done.mine_ref = bf16[512,4096]{1,0:T(8,128)(2,1)} async-done(((bf16[64,4096]{1,0:T(8,128)(2,1)}), bf16[512,4096]{1,0:T(8,128)(2,1)}) %all-gather.2.cloned.1.call-update) | async-done | bytes 4194320 | tf_op jit(solution)/shard_map/all_gather | solution.py:897
  216.1 4.7 collective-permute-done.1
  222.3 26.5 %head.1 = (f32[512,512]{1,0:T(8,128)}, bf16[512,128]{1,0:T(8,128)(2,1)}, bf16[640,512]{1,0:T(8,128)(2,1)}, f32[8,512]{1,0:T(8,128)}, f32[8,128]{1,0:T(8,128)}, /...) custom-call(s32[3,8]{1,0:T(4,128)} %add_add_fusion.ranks_ref, s32[1,4]{1,0:T(1,128)} %lengths_ref.5, ...), custom_call_target="tpu_custom_call" | custom-call | flops 20000000000 | bytes 20000000 | tf_op jit(solution)/shard_map/head/pallas_call | solution.py:677
  256.3 7.3 %add.299 = bf16[512,4096]{1,0:T(8,128)(2,1)} add(bf16[512,4096]{1,0:T(8,128)(2,1)} %get-tuple-element.108, bf16[512,4096]{1,0:T(8,128)(2,1)} %collective-permute-done.25) | non-fusion elementwise | flops 2097152 | bytes 12582912 | tf_op jit(solution)/shard_map/add | solution.py:1008
  264.4 10.2 %expert_backward.2 = (bf16[640,512]{1,0:T(8,128)(2,1)}, bf16[640,2048]{1,0:T(8,128)(2,1)}, bf16[640,2048]{1,0:T(8,128)(2,1)}) custom-call(s32[3,8]{1,0:T(4,128)} %add_add_fusion.ranks_ref, bf16[640,512]{1,0:T(8,128)(2,1)} %bitcast.147, bf16[640,512]{1,0:T(8,128)(2,1)} %bitcast.155, bf16[2,64,2048]{2,1,0:T(8,128)(2,1)} %copy-done.29, ...), custom_call_target="tpu_custom_call" | custom-call | flops 4026531840 | bytes 12000000 | tf_op jit(solution)/shard_map/expert_backward/pallas_call | solution.py:677
  278.9 8.5 %expert_grads.2 = (bf16[2,64,2048]{2,1,0:T(8,128)(2,1)}, bf16[2,64,2048]{2,1,0:T(8,128)(2,1)}, bf16[2,64,2048]{2,1,0:T(8,128)(2,1)}, bf16[2,64,2048]{2,1,0:T(8,1...) custom-call(s32[3,8]{1,0:T(4,128)} %add_add_fusion.ranks_ref, ...), custom_call_target="tpu_custom_call" | custom-call | flops 2684354560 | bytes 10000000 | tf_op jit(solution)/shard_map/expert_grads/pallas_call | solution.py:677
  289.2 29.8 %middle_backward.1 = (f32[512,512]{1,0:T(8,128)}, bf16[512,128]{1,0:T(8,128)(2,1)}, bf16[640,512]{1,0:T(8,128)(2,1)}, f32[24,512]{1,0:T(8,128)}, f32[128,512]{1,...) custom-call(s32[3,8]{1,0:T(4,128)} %add_add_fusion.ranks_ref, s32[1,4]{1,0:T(1,128)} %lengths_ref.5, ...), custom_call_target="tpu_custom_call" | custom-call | flops 24999999488 | bytes 20000000 | tf_op jit(solution)/shard_map/middle_backward/pallas_call | solution.py:677
  323.5 10.7 %collective-permute-done.45 = bf16[2,64,2048]{2,1,0:T(8,128)(2,1)S(1)} collective-permute-done((bf16[2,64,2048]{2,1,0:T(8,128)(2,1)}, bf16[2,64,2048]{2,1,0:T(8,128)(2,1)S(1)}, u32[]{:S(2)}, u32[]{:S(2)}) %collective-permute-start.45) | collective-permute-done | bytes 524320 | tf_op jit(solution)/shard_map/ppermute | solution.py:720
  338.9 10.2 %expert_backward.3 = (bf16[640,512]{1,0:T(8,128)(2,1)}, bf16[640,2048]{1,0:T(8,128)(2,1)}, bf16[640,2048]{1,0:T(8,128)(2,1)}) custom-call(s32[3,8]{1,0:T(4,128)} %add_add_fusion.ranks_ref, bf16[640,512]{1,0:T(8,128)(2,1)} %bitcast.142, bf16[640,512]{1,0:T(8,128)(2,1)} %bitcast.150, bf16[2,64,2048]{2,1,0:T(8,128)(2,1)} %copy-done.28, ...), custom_call_target="tpu_custom_call" | custom-call | flops 4026531840 | bytes 12000000 | tf_op jit(solution)/shard_map/expert_backward/pallas_call | solution.py:677
  351.4 8.5 %expert_grads.3 = (bf16[2,64,2048]{2,1,0:T(8,128)(2,1)}, bf16[2,64,2048]{2,1,0:T(8,128)(2,1)}, bf16[2,64,2048]{2,1,0:T(8,128)(2,1)}, bf16[2,64,2048]{2,1,0:T(8,1...) custom-call(s32[3,8]{1,0:T(4,128)} %add_add_fusion.ranks_ref, ...), custom_call_target="tpu_custom_call" | custom-call | flops 2684354560 | bytes 10000000 | tf_op jit(solution)/shard_map/expert_grads/pallas_call | solution.py:677
  367.6 9.8 %collective-permute-done.38 = bf16[2,64,2048]{2,1,0:T(8,128)(2,1)S(1)} collective-permute-done((bf16[2,64,2048]{2,1,0:T(8,128)(2,1)}, bf16[2,64,2048]{2,1,0:T(8,128)(2,1)S(1)}, u32[]{:S(2)}, u32[]{:S(2)}) %collective-permute-start.38) | collective-permute-done | bytes 524320 | tf_op jit(solution)/shard_map/ppermute | solution.py:720
  484.6 6.5 %all-to-all-start.10 = ((f32[32,2,128]{2,1,0:T(2,128)}), f32[32,2,128]{2,1,0:T(2,128)S(1)}, u32[]{:S(2)}, u32[]{:S(2)}) async-start(f32[32,2,128]{2,1,0:T(2,128)} %broadcast_in_dim.47), calls=%async_computation.11 | async-start | bytes 65536 | tf_op jit(solution)/shard_map/all_to_all | solution.py:1116
  491.2 7.1 %all-to-all-done.10 = f32[32,2,128]{2,1,0:T(2,128)S(1)} async-done(((f32[32,2,128]{2,1,0:T(2,128)}), f32[32,2,128]{2,1,0:T(2,128)S(1)}, u32[]{:S(2)}, u32[]{:S(2)}) %all-to-all-start.10) | async-done | bytes 32800 | tf_op jit(solution)/shard_map/all_to_all | solution.py:1116
  (297 shorter events, 242.7 us)
Async XLA Ops:
  55.6 19.0 %collective-permute-start.20 = (bf16[2,64,2048]{2,1,0:T(8,128)(2,1)}, bf16[2,64,2048]{2,1,0:T(8,128)(2,1)}, u32[]{:S(2)}, u32[]{:S(2)}) collective-permute-start(bf16[2,64,2048]{2,1,0:T(8,128)(2,1)} %collective-permute-done.19.refs_3_), channel_id=1, source_target_pairs={{0,8},{1,5},{2,10},{3,7},{8,16},{9,1},{10,18},{11,3},{16,24},{17,9... | collective-permute-start | bytes 1572872 | tf_op jit(solution)/shard_map/ppermute | solution.py:720
  58.9 17.1 %collective-permute-start.5 = (bf16[2,64,2048]{2,1,0:T(8,128)(2,1)}, bf16[2,64,2048]{2,1,0:T(8,128)(2,1)}, u32[]{:S(2)}, u32[]{:S(2)}) collective-permute-start(bf16[2,64,2048]{2,1,0:T(8,128)(2,1)} %collective-permute-done.4.refs_3_), channel_id=1, source_target_pairs={{0,8},{1,5},{2,10},{3,7},{8,16},{9,1},{10,18},{11,3},{16,24},{17,9... | collective-permute-start | bytes 1572872 | tf_op jit(solution)/shard_map/ppermute | solution.py:720
  74.5 19.7 %collective-permute-start.21 = (bf16[2,64,2048]{2,1,0:T(8,128)(2,1)}, bf16[2,64,2048]{2,1,0:T(8,128)(2,1)}, u32[]{:S(2)}, u32[]{:S(2)}) collective-permute-start(bf16[2,64,2048]{2,1,0:T(8,128)(2,1)} %collective-permute-done.20.refs_4_), channel_id=1, source_target_pairs={{0,8},{1,5},{2,10},{3,7},{8,16},{9,1},{10,18},{11,3},{16,24},{17,9... | collective-permute-start | bytes 1572872 | tf_op jit(solution)/shard_map/ppermute | solution.py:720
  76.0 19.7 %collective-permute-start.6 = (bf16[2,64,2048]{2,1,0:T(8,128)(2,1)}, bf16[2,64,2048]{2,1,0:T(8,128)(2,1)}, u32[]{:S(2)}, u32[]{:S(2)}) collective-permute-start(bf16[2,64,2048]{2,1,0:T(8,128)(2,1)} %collective-permute-done.5.refs_4_), channel_id=1, source_target_pairs={{0,8},{1,5},{2,10},{3,7},{8,16},{9,1},{10,18},{11,3},{16,24},{17,9... | collective-permute-start | bytes 1572872 | tf_op jit(solution)/shard_map/ppermute | solution.py:720
  77.5 18.3 %all-to-all-start.1 = ((bf16[4,160,512]{2,1,0:T(8,128)(2,1)}), bf16[4,160,512]{2,1,0:T(8,128)(2,1)S(1)}, u32[]{:S(2)}, u32[]{:S(2)}) async-start(bf16[4,160,512]{2,1,0:T(8,128)(2,1)} %bitcast.149), calls=%async_computation.1 | async-start | bytes 1310720 | tf_op jit(solution)/shard_map/all_to_all | solution.py:747
  81.0 125.4 %all-gather.2.cloned.1.call-start = ((), (), s32[]{:S(2)}) async-start(), calls=%async_computation.12 | async-start | bytes 4718592 | tf_op jit(solution)/shard_map/all_gather | solution.py:897
  94.3 19.7 %collective-permute-start.22 = (bf16[2,64,2048]{2,1,0:T(8,128)(2,1)}, bf16[2,64,2048]{2,1,0:T(8,128)(2,1)}, u32[]{:S(2)}, u32[]{:S(2)}) collective-permute-start(bf16[2,64,2048]{2,1,0:T(8,128)(2,1)} %collective-permute-done.21.refs_5_), channel_id=1, source_target_pairs={{0,8},{1,5},{2,10},{3,7},{8,16},{9,1},{10,18},{11,3},{16,24},{17,9... | collective-permute-start | bytes 1572872 | tf_op jit(solution)/shard_map/ppermute | solution.py:720
  95.7 19.7 %collective-permute-start.7 = (bf16[2,64,2048]{2,1,0:T(8,128)(2,1)}, bf16[2,64,2048]{2,1,0:T(8,128)(2,1)}, u32[]{:S(2)}, u32[]{:S(2)}) collective-permute-start(bf16[2,64,2048]{2,1,0:T(8,128)(2,1)} %collective-permute-done.6.refs_5_), channel_id=1, source_target_pairs={{0,8},{1,5},{2,10},{3,7},{8,16},{9,1},{10,18},{11,3},{16,24},{17,9... | collective-permute-start | bytes 1572872 | tf_op jit(solution)/shard_map/ppermute | solution.py:720
  114.0 18.3 %collective-permute-start.23 = (bf16[2,64,2048]{2,1,0:T(8,128)(2,1)}, bf16[2,64,2048]{2,1,0:T(8,128)(2,1)}, u32[]{:S(2)}, u32[]{:S(2)}) collective-permute-start(bf16[2,64,2048]{2,1,0:T(8,128)(2,1)} %collective-permute-done.22.refs_6_), channel_id=1, source_target_pairs={{0,8},{1,5},{2,10},{3,7},{8,16},{9,1},{10,18},{11,3},{16,24},{17,9... | collective-permute-start | bytes 1572872 | tf_op jit(solution)/shard_map/ppermute | solution.py:720
  115.4 16.8 %collective-permute-start.8 = (bf16[2,64,2048]{2,1,0:T(8,128)(2,1)}, bf16[2,64,2048]{2,1,0:T(8,128)(2,1)}, u32[]{:S(2)}, u32[]{:S(2)}) collective-permute-start(bf16[2,64,2048]{2,1,0:T(8,128)(2,1)} %collective-permute-done.7.refs_6_), channel_id=1, source_target_pairs={{0,8},{1,5},{2,10},{3,7},{8,16},{9,1},{10,18},{11,3},{16,24},{17,9... | collective-permute-start | bytes 1572872 | tf_op jit(solution)/shard_map/ppermute | solution.py:720
  278.1 186.8 %reduce-scatter.2.cloned.1.call-start = ((), (), s32[]{:S(2)}) async-start(), calls=%async_computation.13 | async-start | bytes 4718592 | tf_op jit(solution)/shard_map/reduce_scatter | solution.py:1010
  319.1 17.3 %collective-permute-start.26 = (bf16[8,64,1792]{2,1,0:T(8,128)(2,1)}, bf16[8,64,1792]{2,1,0:T(8,128)(2,1)}, u32[]{:S(2)}, u32[]{:S(2)}) collective-permute-start(bf16[8,64,1792]{2,1,0:T(8,128)(2,1)} %get-tuple-element.124), channel_id=1, source_target_pairs={{0,1},{1,0},{2,3},{3,2},{4,5},{5,4},{6,7},{7,6},{8,9},{9,8},{10,11... | collective-permute-start | bytes 5505032 | tf_op jit(solution)/shard_map/ppermute | solution.py:731
  320.0 18.0 %all-to-all-start.7 = ((bf16[4,160,512]{2,1,0:T(8,128)(2,1)}), bf16[4,160,512]{2,1,0:T(8,128)(2,1)S(1)}, u32[]{:S(2)}, u32[]{:S(2)}) async-start(bf16[4,160,512]{2,1,0:T(8,128)(2,1)} %bitcast.154), calls=%async_computation.8 | async-start | bytes 1310720 | tf_op jit(solution)/shard_map/all_to_all | solution.py:747
  336.3 27.2 %collective-permute-start.46 = (bf16[2,64,2048]{2,1,0:T(8,128)(2,1)S(1)}, bf16[2,64,2048]{2,1,0:T(8,128)(2,1)}, u32[]{:S(2)}, u32[]{:S(2)}) collective-permute-start(bf16[2,64,2048]{2,1,0:T(8,128)(2,1)S(1)} %add.335), channel_id=1, source_target_pairs={{0,8},{1,5},{2,10},{3,7},{8,16},{9,1},{10,18},{11,3},{16,24},{17,9... | collective-permute-start | bytes 1572872 | tf_op jit(solution)/shard_map/ppermute | solution.py:720
  359.9 17.6 %collective-permute-start.38 = (bf16[2,64,2048]{2,1,0:T(8,128)(2,1)}, bf16[2,64,2048]{2,1,0:T(8,128)(2,1)S(1)}, u32[]{:S(2)}, u32[]{:S(2)}) collective-permute-start(bf16[2,64,2048]{2,1,0:T(8,128)(2,1)} %get-tuple-element.130), channel_id=1, source_target_pairs={{0,8},{1,5},{2,10},{3,7},{8,16},{9,1},{10,18},{11,3},{16,24},{17,9... | collective-permute-start | bytes 1572872 | tf_op jit(solution)/shard_map/ppermute | solution.py:720
  363.4 16.7 %collective-permute-start.29 = (bf16[64,1792]{1,0:T(8,128)(2,1)S(1)}, bf16[64,1792]{1,0:T(8,128)(2,1)S(1)}, u32[]{:S(2)}, u32[]{:S(2)}) collective-permute-start(bf16[64,1792]{1,0:T(8,128)(2,1)S(1)} %fusion.27), channel_id=1, source_target_pairs={{0,8},{1,5},{2,10},{3,7},{8,16},{9,1},{10,18},{11,3},{16,24},{17,9... | collective-permute-start | bytes 688136 | tf_op jit(solution)/shard_map/ppermute | solution.py:720
  364.8 20.7 %collective-permute-start.47 = (bf16[2,64,2048]{2,1,0:T(8,128)(2,1)S(1)}, bf16[2,64,2048]{2,1,0:T(8,128)(2,1)S(1)}, u32[]{:S(2)}, u32[]{:S(2)}) collective-permute-start(bf16[2,64,2048]{2,1,0:T(8,128)(2,1)S(1)} %add.336), channel_id=1, source_target_pairs={{0,8},{1,5},{2,10},{3,7},{8,16},{9,1},{10,18},{11,3},{16,24},{17,9... | collective-permute-start | bytes 1572872 | tf_op jit(solution)/shard_map/ppermute | solution.py:720
  397.9 15.7 %all-to-all-start.8 = ((bf16[4,160,512]{2,1,0:T(8,128)(2,1)}), bf16[4,160,512]{2,1,0:T(8,128)(2,1)S(1)}, u32[]{:S(2)}, u32[]{:S(2)}) async-start(bf16[4,160,512]{2,1,0:T(8,128)(2,1)} %bitcast.49), calls=%async_computation.9 | async-start | bytes 1310720 | tf_op jit(solution)/shard_map/all_to_all | solution.py:747
  403.4 20.9 %collective-permute-start.49 = (bf16[2,64,2048]{2,1,0:T(8,128)(2,1)}, bf16[2,64,2048]{2,1,0:T(8,128)(2,1)}, u32[]{:S(2)}, u32[]{:S(2)}) collective-permute-start(bf16[2,64,2048]{2,1,0:T(8,128)(2,1)} %add.338), channel_id=1, source_target_pairs={{0,8},{1,5},{2,10},{3,7},{8,16},{9,1},{10,18},{11,3},{16,24},{17,9... | collective-permute-start | bytes 1572872 | tf_op jit(solution)/shard_map/ppermute | solution.py:720
  407.0 21.3 %collective-permute-start.41 = (bf16[2,64,2048]{2,1,0:T(8,128)(2,1)}, bf16[2,64,2048]{2,1,0:T(8,128)(2,1)}, u32[]{:S(2)}, u32[]{:S(2)}) collective-permute-start(bf16[2,64,2048]{2,1,0:T(8,128)(2,1)} %add.330), channel_id=1, source_target_pairs={{0,8},{1,5},{2,10},{3,7},{8,16},{9,1},{10,18},{11,3},{16,24},{17,9... | collective-permute-start | bytes 1572872 | tf_op jit(solution)/shard_map/ppermute | solution.py:720
  411.2 20.7 %collective-permute-start.32 = (bf16[64,1792]{1,0:T(8,128)(2,1)}, bf16[64,1792]{1,0:T(8,128)(2,1)}, u32[]{:S(2)}, u32[]{:S(2)}) collective-permute-start(bf16[64,1792]{1,0:T(8,128)(2,1)} %fusion.21), channel_id=1, source_target_pairs={{0,8},{1,5},{2,10},{3,7},{8,16},{9,1},{10,18},{11,3},{16,24},{17,9... | collective-permute-start | bytes 688136 | tf_op jit(solution)/shard_map/ppermute | solution.py:720
  420.5 33.5 %all-to-all-start.9 = ((bf16[32,64,128]{2,1,0:T(8,128)(2,1)}), bf16[32,64,128]{2,1,0:T(8,128)(2,1)S(1)}, u32[]{:S(2)}, u32[]{:S(2)}) async-start(bf16[32,64,128]{2,1,0:T(8,128)(2,1)} %bitcast.52), calls=%async_computation.10 | async-start | bytes 1048576 | tf_op jit(solution)/shard_map/all_to_all | solution.py:1100
  430.5 15.8 %collective-permute-start.42 = (bf16[2,64,2048]{2,1,0:T(8,128)(2,1)}, bf16[2,64,2048]{2,1,0:T(8,128)(2,1)}, u32[]{:S(2)}, u32[]{:S(2)}) collective-permute-start(bf16[2,64,2048]{2,1,0:T(8,128)(2,1)} %add.331), channel_id=1, source_target_pairs={{0,8},{1,5},{2,10},{3,7},{8,16},{9,1},{10,18},{11,3},{16,24},{17,9... | collective-permute-start | bytes 1572872 | tf_op jit(solution)/shard_map/ppermute | solution.py:720
  433.7 17.5 %collective-permute-start.33 = (bf16[64,1792]{1,0:T(8,128)(2,1)}, bf16[64,1792]{1,0:T(8,128)(2,1)}, u32[]{:S(2)}, u32[]{:S(2)}) collective-permute-start(bf16[64,1792]{1,0:T(8,128)(2,1)} %fusion.19), channel_id=1, source_target_pairs={{0,8},{1,5},{2,10},{3,7},{8,16},{9,1},{10,18},{11,3},{16,24},{17,9... | collective-permute-start | bytes 688136 | tf_op jit(solution)/shard_map/ppermute | solution.py:720
  (90 other events, 1181.4 us)
Sparse Core Ops, SparseCore 0:
  132.4 73.8 all-gather.1
  282.6 94.9 reduce-scatter.1

commit v3 on v2

--- a/solution.py
+++ b/solution.py
@@ -868,13 +868,12 @@
         flops=1e9,
         moved=4e6,
     )
-    tile = 512
+    tile = 1024
     expert_scratch = [
         pltpu.VMEM((2, width, units), BF),
         pltpu.SemaphoreType.DMA((units // tile, size)),
     ]
     grads_scratch = [pltpu.VMEM((2, width, units), BF), pltpu.SemaphoreType.DMA((size,))]
-    tile = 512
 
     def expert_forward(slots, chunks):
         return call(
@@ -890,7 +889,7 @@
         )[0]
 
     received_one = swap_rows(slots_one, experts)
-    waits = {1: [extra], 4: [slots_one], 6: [received_one]}
+    waits = {2: [extra], 4: [slots_one], 6: [received_one]}
     first_chunks = [expert_shards[0]]
     for k in range(1, size):
         first_chunks.append(ring_step(tie(first_chunks[-1], *waits.get(k, [])), pairs))
@@ -1092,7 +1091,10 @@
     head_sum = shared_finish(head_part, experts, core).astype(F32)
     sums_two = expert_scatter(sums_two, pairs)
     mid_sum = shared_scatter(mid_grad_mine, mid_grad_other, pairs, size, experts, core).astype(F32)
-    sums_one = expert_scatter(sums_one, pairs)
+    one_sum = sums_one[0]
+    for k in range(1, size):
+        one_sum = ring_step(tie(one_sum, *([head_sum] if k == 4 else [])), pairs) + sums_one[k]
+    sums_one = one_sum
     spread = jnp.broadcast_to(
         extra_grad.reshape(size, 1, shard, LANES), (size, experts, shard, LANES)
     ).reshape(everyone, shard, LANES)

time: 533 us -> 527 us (0.989)
  starting transfers between devices: 122 us -> 99.7 us
  blocking collectives: 14.5 us -> 29.4 us
  waiting for transfers between devices: 143 us -> 151 us
    ppermute x42, starting transfers between devices: 73.1 us -> 56.8 us  [ring_step(): return lax.ppermute(array, ALL, pairs)]
    all_to_all x0 -> x1, blocking collectives: none -> 14.9 us  [on_device(): lax.all_to_all(jnp.broadcast_to(pack[None], (size,) + pack.shape), 'dp',...]
    ppermute x42, waiting for transfers between devices: 98.7 us -> 111 us  [ring_step(): return lax.ppermute(array, ALL, pairs)]
    add x0 -> x7, other arithmetic: none -> 10.7 us  [on_device(): ring_step(tie(one_sum, *([head_sum] if k == 4 else [])), pairs)]
    add x14 -> x7, other arithmetic: 21.3 us -> 10.6 us  [expert_scatter(): partial = ring_step(partial, pairs) + chunk]
    all_to_all x1 -> x0, starting transfers between devices: 7.28 us -> none  [on_device(): lax.all_to_all(jnp.broadcast_to(pack[None], (size,) + pack.shape), 'dp',...]
    unnamed x107 -> x111, local copies, waits for them, and re-layouts: 12.6 us -> 12.6 us
  transfers between devices with their start and end apart: 64 -> 63, of which waited for: 29 -> 27; matrix products, arithmetic and copies ran while one was open for 11% -> 11% of each run, Pallas kernels for 19% -> 18%
where the time goes in v3:
time: 527 us; the launch traced here: 519 us
  waiting for transfers between devices  151 us (29%)
  Pallas kernels  131 us (25%)
  starting transfers between devices  99.7 us (19%)
  other arithmetic  61.4 us (12%)
  blocking collectives  29.4 us (6%)
  local copies, waits for them, and re-layouts  23.5 us (4%)
  between operations  23.1 us (4%)
    pallas_call x12, Pallas kernels, call(): pl.pallas_call(kernel, name=name, out_shape=tuple(outs), in_specs=[spec(k...  131 us
    ppermute x42, waiting for transfers between devices, ring_step(): return lax.ppermute(array, ALL, pairs)  111 us
    ppermute x42, starting transfers between devices, ring_step(): return lax.ppermute(array, ALL, pairs)  56.8 us
    all_to_all x7, starting transfers between devices, swap_rows(): lax.all_to_all(parts, 'expert', split_axis=0, concat_axis=0, tiled=True)  25.1 us
    all_to_all x1, blocking collectives, on_device(): lax.all_to_all(jnp.broadcast_to(pack[None], (size,) + pack.shape), 'dp',...  14.9 us
    all_to_all x1, blocking collectives, swap_rows(): lax.all_to_all(parts, 'expert', split_axis=0, concat_axis=0, tiled=True)  14.5 us
    unnamed x111, local copies, waits for them, and re-layouts  12.6 us
    all_to_all x7, waiting for transfers between devices, swap_rows(): lax.all_to_all(parts, 'expert', split_axis=0, concat_axis=0, tiled=True)  11.1 us
  transfers between devices with their start and end apart: 63, of which 27 were waited for; matrix products, arithmetic and copies ran while one was open for 11% of the time, Pallas kernels for 18%

profile of v3, /device:TPU:0, one launch (start us, length us, event | category | flops | bytes accessed | tf_op | source)
XLA Modules:
  0.0 518.9 jit_solution(6595609389585147407)
XLA Ops:
  16.0 14.9 %all_to_all.55 = bf16[8,64,128]{2,1,0:T(8,128)(2,1)} all-to-all(bf16[8,64,128]{2,1,0:T(8,128)(2,1)S(1)} %broadcast_in_dim.42), channel_id=1, replica_groups=mesh['dp'=8,'expert'=4] {'dp'}, dimensions={0} | all-to-all | bytes 262144 | tf_op jit(solution)/shard_map/all_to_all | solution.py:822
  31.8 8.2 %collective-permute-done.3.refs_2_ = bf16[2,64,2048]{2,1,0:T(8,128)(2,1)S(1)} collective-permute-done((bf16[2,64,2048]{2,1,0:T(8,128)(2,1)S(1)}, bf16[2,64,2048]{2,1,0:T(8,128)(2,1)S(1)}, u32[]{:S(2)}, u32[]{:S(2)}) %collective-permute-start.3) | collective-permute-done | bytes 524320 | tf_op jit(solution)/shard_map/ppermute | solution.py:720
  40.1 5.6 %collective-permute-done.18.refs_2_ = bf16[2,64,2048]{2,1,0:T(8,128)(2,1)S(1)} collective-permute-done((bf16[2,64,2048]{2,1,0:T(8,128)(2,1)}, bf16[2,64,2048]{2,1,0:T(8,128)(2,1)S(1)}, u32[]{:S(2)}, u32[]{:S(2)}) %collective-permute-start.18) | collective-permute-done | bytes 524320 | tf_op jit(solution)/shard_map/ppermute | solution.py:720
  58.8 11.8 %collective-permute-done.9 = bf16[64,1792]{1,0:T(8,128)(2,1)S(1)} collective-permute-done((bf16[64,1792]{1,0:T(8,128)(2,1)S(1)}, bf16[64,1792]{1,0:T(8,128)(2,1)S(1)}, u32[]{:S(2)}, u32[]{:S(2)}) %collective-permute-start.9) | collective-permute-done | bytes 229408 | tf_op jit(solution)/shard_map/ppermute | solution.py:720
  78.0 12.3 %collective-permute-done.11 = bf16[64,1792]{1,0:T(8,128)(2,1)S(1)} collective-permute-done((bf16[64,1792]{1,0:T(8,128)(2,1)S(1)}, bf16[64,1792]{1,0:T(8,128)(2,1)S(1)}, u32[]{:S(2)}, u32[]{:S(2)}) %collective-permute-start.11) | collective-permute-done | bytes 229408 | tf_op jit(solution)/shard_map/ppermute | solution.py:720
  96.3 13.7 %collective-permute-done.13 = bf16[64,1792]{1,0:T(8,128)(2,1)S(1)} collective-permute-done((bf16[64,1792]{1,0:T(8,128)(2,1)S(1)}, bf16[64,1792]{1,0:T(8,128)(2,1)S(1)}, u32[]{:S(2)}, u32[]{:S(2)}) %collective-permute-start.13) | collective-permute-done | bytes 229408 | tf_op jit(solution)/shard_map/ppermute | solution.py:720
  116.9 12.9 %collective-permute-done.15 = bf16[64,1792]{1,0:T(8,128)(2,1)S(1)} collective-permute-done((bf16[64,1792]{1,0:T(8,128)(2,1)S(1)}, bf16[64,1792]{1,0:T(8,128)(2,1)S(1)}, u32[]{:S(2)}, u32[]{:S(2)}) %collective-permute-start.15) | collective-permute-done | bytes 229408 | tf_op jit(solution)/shard_map/ppermute | solution.py:720
  136.2 6.9 %expert_forward.2 = bf16[640,512]{1,0:T(8,128)(2,1)} custom-call(s32[3,8]{1,0:T(4,128)} %add_add_fusion.ranks_ref, bf16[640,512]{1,0:T(8,128)(2,1)} %bitcast.141, bf16[2,64,2048]{2,1,0:T(8,128)(2,1)} %copy-done.28, bf16[2,64,2048]{2,1,0:T(8,128)(2,1)} %copy-done.48, bf16[2,64,2048]{2,1,0:T(8,128)(2,1)} %copy-done.49, ...), custom_call_target="tpu_custom_call" | custom-call | flops 2684354560 | bytes 6000000 | tf_op jit(solution)/shard_map/expert_forward/pallas_call | solution.py:677
  146.8 10.2 %all-to-all-done.2 = bf16[4,160,512]{2,1,0:T(8,128)(2,1)S(1)} async-done(((bf16[4,160,512]{2,1,0:T(8,128)(2,1)}), bf16[4,160,512]{2,1,0:T(8,128)(2,1)S(1)}, u32[]{:S(2)}, u32[]{:S(2)}) %all-to-all-start.2) | async-done | bytes 655392 | tf_op jit(solution)/shard_map/all_to_all | solution.py:747
  157.8 16.1 %middle_forward.1 = (f32[512,512]{1,0:T(8,128)}, f32[512,512]{1,0:T(8,128)}, f32[512,512]{1,0:T(8,128)}, f32[512,128]{1,0:T(8,128)}, f32[512,128]{1,0:T(8,128)},...) custom-call(s32[3,8]{1,0:T(4,128)} %add_add_fusion.ranks_ref, ...), custom_call_target="tpu_custom_call" | custom-call | flops 12000000000 | bytes 10000000 | tf_op jit(solution)/shard_map/middle_forward/pallas_call | solution.py:677
  174.0 14.5 %all_to_all.56 = bf16[4,160,512]{2,1,0:T(8,128)(2,1)} all-to-all(bf16[4,160,512]{2,1,0:T(8,128)(2,1)} %bitcast.161), channel_id=1, replica_groups=mesh['dp'=8,'expert'=4] {'expert'}, dimensions={0} | all-to-all | bytes 1310720 | tf_op jit(solution)/shard_map/all_to_all | solution.py:747
  188.5 6.7 %expert_forward.3 = bf16[640,512]{1,0:T(8,128)(2,1)} custom-call(s32[3,8]{1,0:T(4,128)} %add_add_fusion.ranks_ref, bf16[640,512]{1,0:T(8,128)(2,1)} %bitcast.146, bf16[2,64,2048]{2,1,0:T(8,128)(2,1)} %copy-done.29, bf16[2,64,2048]{2,1,0:T(8,128)(2,1)} %collective-permute-done.17.refs_1_, bf16[2,64,2048]{2,1,0:T(8,128)(2,1)} %copy-done.50, ...), custom_call_target="tpu_custom_call" | custom-call | flops 2684354560 | bytes 6000000 | tf_op jit(solution)/shard_map/expert_forward/pallas_call | solution.py:677
  195.2 6.9 %all-gather.2.cloned.1.call-done.mine_ref = bf16[512,4096]{1,0:T(8,128)(2,1)} async-done(((bf16[64,4096]{1,0:T(8,128)(2,1)}), bf16[512,4096]{1,0:T(8,128)(2,1)}) %all-gather.2.cloned.1.call-update) | async-done | bytes 4194320 | tf_op jit(solution)/shard_map/all_gather | solution.py:896
  218.1 26.5 %head.1 = (f32[512,512]{1,0:T(8,128)}, bf16[512,128]{1,0:T(8,128)(2,1)}, bf16[640,512]{1,0:T(8,128)(2,1)}, f32[8,512]{1,0:T(8,128)}, f32[8,128]{1,0:T(8,128)}, /...) custom-call(s32[3,8]{1,0:T(4,128)} %add_add_fusion.ranks_ref, s32[1,4]{1,0:T(1,128)} %lengths_ref.5, ...), custom_call_target="tpu_custom_call" | custom-call | flops 20000000000 | bytes 20000000 | tf_op jit(solution)/shard_map/head/pallas_call | solution.py:677
  252.2 7.3 %add.299 = bf16[512,4096]{1,0:T(8,128)(2,1)} add(bf16[512,4096]{1,0:T(8,128)(2,1)} %get-tuple-element.109, bf16[512,4096]{1,0:T(8,128)(2,1)} %collective-permute-done.25) | non-fusion elementwise | flops 2097152 | bytes 12582912 | tf_op jit(solution)/shard_map/add | solution.py:1007
  260.3 8.8 %expert_backward.2 = (bf16[640,512]{1,0:T(8,128)(2,1)}, bf16[640,2048]{1,0:T(8,128)(2,1)}, bf16[640,2048]{1,0:T(8,128)(2,1)}) custom-call(s32[3,8]{1,0:T(4,128)} %add_add_fusion.ranks_ref, bf16[640,512]{1,0:T(8,128)(2,1)} %bitcast.147, bf16[640,512]{1,0:T(8,128)(2,1)} %bitcast.155, bf16[2,64,2048]{2,1,0:T(8,128)(2,1)} %copy-done.29, ...), custom_call_target="tpu_custom_call" | custom-call | flops 4026531840 | bytes 12000000 | tf_op jit(solution)/shard_map/expert_backward/pallas_call | solution.py:677
  273.4 8.5 %expert_grads.2 = (bf16[2,64,2048]{2,1,0:T(8,128)(2,1)}, bf16[2,64,2048]{2,1,0:T(8,128)(2,1)}, bf16[2,64,2048]{2,1,0:T(8,128)(2,1)}, bf16[2,64,2048]{2,1,0:T(8,1...) custom-call(s32[3,8]{1,0:T(4,128)} %add_add_fusion.ranks_ref, ...), custom_call_target="tpu_custom_call" | custom-call | flops 2684354560 | bytes 10000000 | tf_op jit(solution)/shard_map/expert_grads/pallas_call | solution.py:677
  283.7 29.8 %middle_backward.1 = (f32[512,512]{1,0:T(8,128)}, bf16[512,128]{1,0:T(8,128)(2,1)}, bf16[640,512]{1,0:T(8,128)(2,1)}, f32[24,512]{1,0:T(8,128)}, f32[128,512]{1,...) custom-call(s32[3,8]{1,0:T(4,128)} %add_add_fusion.ranks_ref, s32[1,4]{1,0:T(1,128)} %lengths_ref.5, ...), custom_call_target="tpu_custom_call" | custom-call | flops 24999999488 | bytes 20000000 | tf_op jit(solution)/shard_map/middle_backward/pallas_call | solution.py:677
  318.0 10.6 %collective-permute-done.45 = bf16[2,64,2048]{2,1,0:T(8,128)(2,1)S(1)} collective-permute-done((bf16[2,64,2048]{2,1,0:T(8,128)(2,1)}, bf16[2,64,2048]{2,1,0:T(8,128)(2,1)S(1)}, u32[]{:S(2)}, u32[]{:S(2)}) %collective-permute-start.45) | collective-permute-done | bytes 524320 | tf_op jit(solution)/shard_map/ppermute | solution.py:720
  333.4 8.8 %expert_backward.3 = (bf16[640,512]{1,0:T(8,128)(2,1)}, bf16[640,2048]{1,0:T(8,128)(2,1)}, bf16[640,2048]{1,0:T(8,128)(2,1)}) custom-call(s32[3,8]{1,0:T(4,128)} %add_add_fusion.ranks_ref, bf16[640,512]{1,0:T(8,128)(2,1)} %bitcast.142, bf16[640,512]{1,0:T(8,128)(2,1)} %bitcast.150, bf16[2,64,2048]{2,1,0:T(8,128)(2,1)} %copy-done.28, ...), custom_call_target="tpu_custom_call" | custom-call | flops 4026531840 | bytes 12000000 | tf_op jit(solution)/shard_map/expert_backward/pallas_call | solution.py:677
  344.9 8.5 %expert_grads.3 = (bf16[2,64,2048]{2,1,0:T(8,128)(2,1)}, bf16[2,64,2048]{2,1,0:T(8,128)(2,1)}, bf16[2,64,2048]{2,1,0:T(8,128)(2,1)}, bf16[2,64,2048]{2,1,0:T(8,1...) custom-call(s32[3,8]{1,0:T(4,128)} %add_add_fusion.ranks_ref, ...), custom_call_target="tpu_custom_call" | custom-call | flops 2684354560 | bytes 10000000 | tf_op jit(solution)/shard_map/expert_grads/pallas_call | solution.py:677
  361.6 10.0 %collective-permute-done.38 = bf16[2,64,2048]{2,1,0:T(8,128)(2,1)S(1)} collective-permute-done((bf16[2,64,2048]{2,1,0:T(8,128)(2,1)}, bf16[2,64,2048]{2,1,0:T(8,128)(2,1)S(1)}, u32[]{:S(2)}, u32[]{:S(2)}) %collective-permute-start.38) | collective-permute-done | bytes 524320 | tf_op jit(solution)/shard_map/ppermute | solution.py:720
  478.9 6.5 %all-to-all-start.10 = ((f32[32,2,128]{2,1,0:T(2,128)}), f32[32,2,128]{2,1,0:T(2,128)S(1)}, u32[]{:S(2)}, u32[]{:S(2)}) async-start(f32[32,2,128]{2,1,0:T(2,128)} %broadcast_in_dim.47), calls=%async_computation.11 | async-start | bytes 65536 | tf_op jit(solution)/shard_map/all_to_all | solution.py:1118
  485.4 7.1 %all-to-all-done.10 = f32[32,2,128]{2,1,0:T(2,128)S(1)} async-done(((f32[32,2,128]{2,1,0:T(2,128)}), f32[32,2,128]{2,1,0:T(2,128)S(1)}, u32[]{:S(2)}, u32[]{:S(2)}) %all-to-all-start.10) | async-done | bytes 32800 | tf_op jit(solution)/shard_map/all_to_all | solution.py:1118
  (300 shorter events, 222.7 us)
Async XLA Ops:
  9.5 21.3 %collective-permute-start.2 = (bf16[2,64,2048]{2,1,0:T(8,128)(2,1)S(1)}, bf16[2,64,2048]{2,1,0:T(8,128)(2,1)S(1)}, u32[]{:S(2)}, u32[]{:S(2)}) collective-permute-start(bf16[2,64,2048]{2,1,0:T(8,128)(2,1)S(1)} %pad_maximum_fusion.refs_0_), channel_id=1, source_target_pairs={{0,8},{1,5},{2,10},{3,7},{8,16},{9,1},{10,18},{11,3},{16,24},{17,9... | collective-permute-start | bytes 1572872 | tf_op jit(solution)/shard_map/ppermute | solution.py:720
  12.7 18.2 %collective-permute-start.17 = (bf16[2,64,2048]{2,1,0:T(8,128)(2,1)S(1)}, bf16[2,64,2048]{2,1,0:T(8,128)(2,1)}, u32[]{:S(2)}, u32[]{:S(2)}) collective-permute-start(bf16[2,64,2048]{2,1,0:T(8,128)(2,1)S(1)} %pad_maximum_fusion.1.refs_0_), channel_id=1, source_target_pairs={{0,8},{1,5},{2,10},{3,7},{8,16},{9,1},{10,18},{11,3},{16,24},{17,9... | collective-permute-start | bytes 1572872 | tf_op jit(solution)/shard_map/ppermute | solution.py:720
  52.0 18.6 %collective-permute-start.5 = (bf16[2,64,2048]{2,1,0:T(8,128)(2,1)}, bf16[2,64,2048]{2,1,0:T(8,128)(2,1)}, u32[]{:S(2)}, u32[]{:S(2)}) collective-permute-start(bf16[2,64,2048]{2,1,0:T(8,128)(2,1)} %collective-permute-done.4.refs_3_), channel_id=1, source_target_pairs={{0,8},{1,5},{2,10},{3,7},{8,16},{9,1},{10,18},{11,3},{16,24},{17,9... | collective-permute-start | bytes 1572872 | tf_op jit(solution)/shard_map/ppermute | solution.py:720
  70.6 19.7 %collective-permute-start.6 = (bf16[2,64,2048]{2,1,0:T(8,128)(2,1)}, bf16[2,64,2048]{2,1,0:T(8,128)(2,1)}, u32[]{:S(2)}, u32[]{:S(2)}) collective-permute-start(bf16[2,64,2048]{2,1,0:T(8,128)(2,1)} %collective-permute-done.5.refs_4_), channel_id=1, source_target_pairs={{0,8},{1,5},{2,10},{3,7},{8,16},{9,1},{10,18},{11,3},{16,24},{17,9... | collective-permute-start | bytes 1572872 | tf_op jit(solution)/shard_map/ppermute | solution.py:720
  72.0 18.3 %collective-permute-start.21 = (bf16[2,64,2048]{2,1,0:T(8,128)(2,1)}, bf16[2,64,2048]{2,1,0:T(8,128)(2,1)}, u32[]{:S(2)}, u32[]{:S(2)}) collective-permute-start(bf16[2,64,2048]{2,1,0:T(8,128)(2,1)} %collective-permute-done.20.refs_4_), channel_id=1, source_target_pairs={{0,8},{1,5},{2,10},{3,7},{8,16},{9,1},{10,18},{11,3},{16,24},{17,9... | collective-permute-start | bytes 1572872 | tf_op jit(solution)/shard_map/ppermute | solution.py:720
  73.3 17.0 %all-to-all-start.1 = ((bf16[4,160,512]{2,1,0:T(8,128)(2,1)}), bf16[4,160,512]{2,1,0:T(8,128)(2,1)S(1)}, u32[]{:S(2)}, u32[]{:S(2)}) async-start(bf16[4,160,512]{2,1,0:T(8,128)(2,1)} %bitcast.149), calls=%async_computation.1 | async-start | bytes 1310720 | tf_op jit(solution)/shard_map/all_to_all | solution.py:747
  76.8 125.4 %all-gather.2.cloned.1.call-start = ((), (), s32[]{:S(2)}) async-start(), calls=%async_computation.12 | async-start | bytes 4718592 | tf_op jit(solution)/shard_map/all_gather | solution.py:896
  90.3 19.7 %collective-permute-start.22 = (bf16[2,64,2048]{2,1,0:T(8,128)(2,1)}, bf16[2,64,2048]{2,1,0:T(8,128)(2,1)}, u32[]{:S(2)}, u32[]{:S(2)}) collective-permute-start(bf16[2,64,2048]{2,1,0:T(8,128)(2,1)} %collective-permute-done.21.refs_5_), channel_id=1, source_target_pairs={{0,8},{1,5},{2,10},{3,7},{8,16},{9,1},{10,18},{11,3},{16,24},{17,9... | collective-permute-start | bytes 1572872 | tf_op jit(solution)/shard_map/ppermute | solution.py:720
  91.8 19.6 %collective-permute-start.7 = (bf16[2,64,2048]{2,1,0:T(8,128)(2,1)}, bf16[2,64,2048]{2,1,0:T(8,128)(2,1)}, u32[]{:S(2)}, u32[]{:S(2)}) collective-permute-start(bf16[2,64,2048]{2,1,0:T(8,128)(2,1)} %collective-permute-done.6.refs_5_), channel_id=1, source_target_pairs={{0,8},{1,5},{2,10},{3,7},{8,16},{9,1},{10,18},{11,3},{16,24},{17,9... | collective-permute-start | bytes 1572872 | tf_op jit(solution)/shard_map/ppermute | solution.py:720
  110.0 19.7 %collective-permute-start.23 = (bf16[2,64,2048]{2,1,0:T(8,128)(2,1)}, bf16[2,64,2048]{2,1,0:T(8,128)(2,1)}, u32[]{:S(2)}, u32[]{:S(2)}) collective-permute-start(bf16[2,64,2048]{2,1,0:T(8,128)(2,1)} %collective-permute-done.22.refs_6_), channel_id=1, source_target_pairs={{0,8},{1,5},{2,10},{3,7},{8,16},{9,1},{10,18},{11,3},{16,24},{17,9... | collective-permute-start | bytes 1572872 | tf_op jit(solution)/shard_map/ppermute | solution.py:720
  111.4 18.3 %collective-permute-start.8 = (bf16[2,64,2048]{2,1,0:T(8,128)(2,1)}, bf16[2,64,2048]{2,1,0:T(8,128)(2,1)}, u32[]{:S(2)}, u32[]{:S(2)}) collective-permute-start(bf16[2,64,2048]{2,1,0:T(8,128)(2,1)} %collective-permute-done.7.refs_6_), channel_id=1, source_target_pairs={{0,8},{1,5},{2,10},{3,7},{8,16},{9,1},{10,18},{11,3},{16,24},{17,9... | collective-permute-start | bytes 1572872 | tf_op jit(solution)/shard_map/ppermute | solution.py:720
  272.6 186.5 %reduce-scatter.2.cloned.1.call-start = ((), (), s32[]{:S(2)}) async-start(), calls=%async_computation.13 | async-start | bytes 4718592 | tf_op jit(solution)/shard_map/reduce_scatter | solution.py:1009
  313.5 17.4 %collective-permute-start.26 = (bf16[8,64,1792]{2,1,0:T(8,128)(2,1)}, bf16[8,64,1792]{2,1,0:T(8,128)(2,1)}, u32[]{:S(2)}, u32[]{:S(2)}) collective-permute-start(bf16[8,64,1792]{2,1,0:T(8,128)(2,1)} %get-tuple-element.125), channel_id=1, source_target_pairs={{0,1},{1,0},{2,3},{3,2},{4,5},{5,4},{6,7},{7,6},{8,9},{9,8},{10,11... | collective-permute-start | bytes 5505032 | tf_op jit(solution)/shard_map/ppermute | solution.py:731
  314.5 18.0 %all-to-all-start.7 = ((bf16[4,160,512]{2,1,0:T(8,128)(2,1)}), bf16[4,160,512]{2,1,0:T(8,128)(2,1)S(1)}, u32[]{:S(2)}, u32[]{:S(2)}) async-start(bf16[4,160,512]{2,1,0:T(8,128)(2,1)} %bitcast.154), calls=%async_computation.8 | async-start | bytes 1310720 | tf_op jit(solution)/shard_map/all_to_all | solution.py:747
  330.8 27.2 %collective-permute-start.46 = (bf16[2,64,2048]{2,1,0:T(8,128)(2,1)S(1)}, bf16[2,64,2048]{2,1,0:T(8,128)(2,1)}, u32[]{:S(2)}, u32[]{:S(2)}) collective-permute-start(bf16[2,64,2048]{2,1,0:T(8,128)(2,1)S(1)} %add.335), channel_id=1, source_target_pairs={{0,8},{1,5},{2,10},{3,7},{8,16},{9,1},{10,18},{11,3},{16,24},{17,9... | collective-permute-start | bytes 1572872 | tf_op jit(solution)/shard_map/ppermute | solution.py:720
  353.4 18.2 %collective-permute-start.38 = (bf16[2,64,2048]{2,1,0:T(8,128)(2,1)}, bf16[2,64,2048]{2,1,0:T(8,128)(2,1)S(1)}, u32[]{:S(2)}, u32[]{:S(2)}) collective-permute-start(bf16[2,64,2048]{2,1,0:T(8,128)(2,1)} %get-tuple-element.131), channel_id=1, source_target_pairs={{0,8},{1,5},{2,10},{3,7},{8,16},{9,1},{10,18},{11,3},{16,24},{17,9... | collective-permute-start | bytes 1572872 | tf_op jit(solution)/shard_map/ppermute | solution.py:720
  356.5 17.7 %collective-permute-start.29 = (bf16[64,1792]{1,0:T(8,128)(2,1)S(1)}, bf16[64,1792]{1,0:T(8,128)(2,1)S(1)}, u32[]{:S(2)}, u32[]{:S(2)}) collective-permute-start(bf16[64,1792]{1,0:T(8,128)(2,1)S(1)} %fusion.26), channel_id=1, source_target_pairs={{0,8},{1,5},{2,10},{3,7},{8,16},{9,1},{10,18},{11,3},{16,24},{17,9... | collective-permute-start | bytes 688136 | tf_op jit(solution)/shard_map/ppermute | solution.py:720
  359.2 20.4 %collective-permute-start.47 = (bf16[2,64,2048]{2,1,0:T(8,128)(2,1)S(1)}, bf16[2,64,2048]{2,1,0:T(8,128)(2,1)S(1)}, u32[]{:S(2)}, u32[]{:S(2)}) collective-permute-start(bf16[2,64,2048]{2,1,0:T(8,128)(2,1)S(1)} %add.336), channel_id=1, source_target_pairs={{0,8},{1,5},{2,10},{3,7},{8,16},{9,1},{10,18},{11,3},{16,24},{17,9... | collective-permute-start | bytes 1572872 | tf_op jit(solution)/shard_map/ppermute | solution.py:720
  396.6 21.9 %collective-permute-start.49 = (bf16[2,64,2048]{2,1,0:T(8,128)(2,1)}, bf16[2,64,2048]{2,1,0:T(8,128)(2,1)}, u32[]{:S(2)}, u32[]{:S(2)}) collective-permute-start(bf16[2,64,2048]{2,1,0:T(8,128)(2,1)} %add.338), channel_id=1, source_target_pairs={{0,8},{1,5},{2,10},{3,7},{8,16},{9,1},{10,18},{11,3},{16,24},{17,9... | collective-permute-start | bytes 1572872 | tf_op jit(solution)/shard_map/ppermute | solution.py:720
  401.1 21.5 %collective-permute-start.41 = (bf16[2,64,2048]{2,1,0:T(8,128)(2,1)}, bf16[2,64,2048]{2,1,0:T(8,128)(2,1)}, u32[]{:S(2)}, u32[]{:S(2)}) collective-permute-start(bf16[2,64,2048]{2,1,0:T(8,128)(2,1)} %add.330), channel_id=1, source_target_pairs={{0,8},{1,5},{2,10},{3,7},{8,16},{9,1},{10,18},{11,3},{16,24},{17,9... | collective-permute-start | bytes 1572872 | tf_op jit(solution)/shard_map/ppermute | solution.py:720
  405.3 20.8 %collective-permute-start.32 = (bf16[64,1792]{1,0:T(8,128)(2,1)}, bf16[64,1792]{1,0:T(8,128)(2,1)}, u32[]{:S(2)}, u32[]{:S(2)}) collective-permute-start(bf16[64,1792]{1,0:T(8,128)(2,1)} %fusion.20), channel_id=1, source_target_pairs={{0,8},{1,5},{2,10},{3,7},{8,16},{9,1},{10,18},{11,3},{16,24},{17,9... | collective-permute-start | bytes 688136 | tf_op jit(solution)/shard_map/ppermute | solution.py:720
  413.7 34.6 %all-to-all-start.9 = ((bf16[32,64,128]{2,1,0:T(8,128)(2,1)}), bf16[32,64,128]{2,1,0:T(8,128)(2,1)S(1)}, u32[]{:S(2)}, u32[]{:S(2)}) async-start(bf16[32,64,128]{2,1,0:T(8,128)(2,1)} %bitcast.52), calls=%async_computation.10 | async-start | bytes 1048576 | tf_op jit(solution)/shard_map/all_to_all | solution.py:1102
  424.7 15.8 %collective-permute-start.42 = (bf16[2,64,2048]{2,1,0:T(8,128)(2,1)}, bf16[2,64,2048]{2,1,0:T(8,128)(2,1)}, u32[]{:S(2)}, u32[]{:S(2)}) collective-permute-start(bf16[2,64,2048]{2,1,0:T(8,128)(2,1)} %add.331), channel_id=1, source_target_pairs={{0,8},{1,5},{2,10},{3,7},{8,16},{9,1},{10,18},{11,3},{16,24},{17,9... | collective-permute-start | bytes 1572872 | tf_op jit(solution)/shard_map/ppermute | solution.py:720
  427.9 17.5 %collective-permute-start.33 = (bf16[64,1792]{1,0:T(8,128)(2,1)}, bf16[64,1792]{1,0:T(8,128)(2,1)}, u32[]{:S(2)}, u32[]{:S(2)}) collective-permute-start(bf16[64,1792]{1,0:T(8,128)(2,1)} %fusion.18), channel_id=1, source_target_pairs={{0,8},{1,5},{2,10},{3,7},{8,16},{9,1},{10,18},{11,3},{16,24},{17,9... | collective-permute-start | bytes 688136 | tf_op jit(solution)/shard_map/ppermute | solution.py:720
  (91 other events, 1191.8 us)
Sparse Core Ops, SparseCore 0:
  129.9 72.2 all-gather.1
  277.1 95.6 reduce-scatter.1
